TPU v7x, 128 devices: a whole 4x4x4 slice. The times are simulated.
128 devices in a mesh: band: 8 (over z, core), patch: 16 (over y, x).
Axes of the slice: x: 4, y: 4, z: 4, core: 2. Of those that a mesh axis runs over, the one named last changes fastest.
Arguments:
- grid_feats: bfloat16 [262144, 227], P(('band', 'patch')), may hold values from -6 to 6
- mesh_feats: bfloat16 [32768, 512], P(('band', 'patch')), may hold values from -6 to 6
- cotangent: bfloat16 [32768, 512], P(('band', 'patch')), may hold values from -6 to 6
- w_embed: bfloat16 [227, 512], replicated, may hold values from -0.375 to 0.375
- w_send: bfloat16 [512, 512], replicated, may hold values from -0.25 to 0.25
- w_recv: bfloat16 [512, 512], replicated, may hold values from -0.25 to 0.25
- w_out: bfloat16 [512, 512], replicated, may hold values from -0.0625 to 0.0625
- u_src: bfloat16 [256, 512], replicated, may hold values from -0.375 to 0.375
- u_dst: bfloat16 [256, 512], replicated, may hold values from -0.375 to 0.375
- u_out: bfloat16 [512, 256], replicated, may hold values from -0.09375 to 0.09375
- v_in: bfloat16 [256, 512], replicated, may hold values from -0.375 to 0.375
- v_out: bfloat16 [512, 256], replicated, may hold values from -0.25 to 0.25
- send_rows: int32 [128, 2048], P(('band', 'patch')), may hold values from 0 to 2047, as said below
- enc_src: int32 [128, 4096], P(('band', 'patch')), may hold values from 0 to 2047, as said below
- enc_dst: int32 [128, 4096], P(('band', 'patch')), may hold values from -1 to 255, as said below
- halo_send: int32 [128, 2, 2, 32], P(('band', 'patch')), may hold values from 0 to 255, as said below
- mesh_src: int32 [128, 2048], P(('band', 'patch')), may hold values from 0 to 383, as said below
- mesh_dst: int32 [128, 2048], P(('band', 'patch')), may hold values from -1 to 255, as said below
Outputs:
- grid_grad: bfloat16 [262144, 227], P(('band', 'patch'))
- mesh_grad: float32 [32768, 512], P(('band', 'patch'))
- grad_w_embed: float32 [227, 512], replicated
- grad_w_send: float32 [512, 512], replicated
- grad_w_recv: float32 [512, 512], replicated
- grad_w_out: float32 [512, 512], replicated
- grad_u_src: float32 [256, 512], replicated
- grad_u_dst: float32 [256, 512], replicated
- grad_u_out: float32 [512, 256], replicated
- grad_v_in: float32 [256, 512], replicated
- grad_v_out: float32 [512, 256], replicated
Inputs may be any that keep to these rules, and one draw needn't show every extreme that they name: Each send_rows[d] names each of the device's 2048 local grid rows exactly once. `enc_src`: index into the device's received grid rows; the first 2048 slots name each received row once and are live. `enc_dst`: local mesh node of a live slot, -1 for an empty slot; empty slots follow all live ones of a device; some device has all 4096 slots live. halo_send[d, 0, 0] and [d, 0, 1] go to the band neighbour below and above, [d, 1, 0] and [d, 1, 1] to the patch neighbours below and above. `mesh_src`: row of the halo table: own 256 nodes, then the blocks from band - 1, band + 1, patch - 1, patch + 1; the first 128 slots name each received row once and are live. `mesh_dst`: local receiver of a live slot, -1 for an empty slot; empty slots follow all live ones of a device; some device has all 2048 slots live.
All inputs are finite; a program needn't handle non-finite values.
Results may differ from a plain program's by a relative error of at most 0.025.
Values may be sent and summed in bfloat16 or wider, within the bound.
No kernel may reach another device: no remote copies, remote signals or barrier semaphores. Data moves between devices by JAX's collectives and lax.ppermute only.
A program may use at most 128 MiB of HBM per device.

v0:
```python
import jax
import jax.numpy as jnp
from jax import lax
from jax.sharding import PartitionSpec as P


def padded(block, sides, width, periodic):
    for axis, dim in sides:
        count = lax.axis_size(axis)
        forward = [(i, i + 1) for i in range(count - 1)]
        if periodic:
            forward.append((count - 1, 0))
        backward = [(target, source) for source, target in forward]
        low = lax.ppermute(
            lax.slice_in_dim(block, block.shape[dim] - width, None, axis=dim), axis, forward
        )
        high = lax.ppermute(lax.slice_in_dim(block, 0, width, axis=dim), axis, backward)
        block = jnp.concatenate([low, block, high], axis=dim)
    return block


def silu_grad(value):
    sigma = jax.nn.sigmoid(value)
    return sigma * (1.0 + value * (1.0 - sigma))


def node_table(index, count):
    return (jnp.arange(count, dtype=jnp.int32)[:, None] == index[None, :]).astype(jnp.bfloat16)


def matmul(left, right):
    return jnp.dot(left, right, preferred_element_type=jnp.float32)


def inner_left(left, right):
    return lax.dot_general(
        left, right, (((0,), (0,)), ((), ())), preferred_element_type=jnp.float32
    )


def outer_right(left, right):
    return lax.dot_general(
        left, right, (((1,), (1,)), ((), ())), preferred_element_type=jnp.float32
    )


def embed_rows(grid_rows, w_embed):
    embed_pre = matmul(grid_rows, w_embed)
    return (embed_pre, jax.nn.silu(embed_pre).astype(jnp.bfloat16))


def embed_back(grid_rows, embed_pre, embedded_grad, w_embed):
    embed_grad = (embedded_grad.astype(jnp.float32) * silu_grad(embed_pre)).astype(jnp.bfloat16)
    return (
        inner_left(grid_rows, embed_grad),
        outer_right(embed_grad, w_embed).astype(jnp.bfloat16),
    )


def encoder_edges(embedded, mesh_rows, w_send, w_recv, w_out, sources, targets):
    sender_part = matmul(embedded, w_send)
    node_part = matmul(mesh_rows, w_recv)
    active = targets >= 0
    clipped = jnp.maximum(targets, 0)
    edge_pre = jnp.take(sender_part, sources, axis=0) + jnp.take(node_part, clipped, axis=0)
    message = jnp.where(active[:, None], jax.nn.silu(edge_pre), 0.0).astype(jnp.bfloat16)
    incidence = node_table(targets, mesh_rows.shape[0])
    gathered = matmul(incidence, message).astype(jnp.bfloat16)
    latent = (mesh_rows.astype(jnp.float32) + matmul(gathered, w_out)).astype(jnp.bfloat16)
    return (edge_pre, gathered, latent, incidence, active)


def encoder_back(
    embedded,
    mesh_rows,
    w_send,
    w_recv,
    w_out,
    sources,
    targets,
    edge_pre,
    gathered,
    incidence,
    active,
    latent_grad,
):
    grad_out = inner_left(gathered, latent_grad)
    gathered_grad = outer_right(latent_grad, w_out)
    clipped = jnp.maximum(targets, 0)
    enc_edge_grad = jnp.where(
        active[:, None], jnp.take(gathered_grad, clipped, axis=0) * silu_grad(edge_pre), 0.0
    ).astype(jnp.bfloat16)
    node_grad = matmul(incidence, enc_edge_grad).astype(jnp.bfloat16)
    sender_grad = (
        jnp.zeros((embedded.shape[0], embedded.shape[1]), jnp.float32)
        .at[sources]
        .add(enc_edge_grad.astype(jnp.float32))
        .astype(jnp.bfloat16)
    )
    grad_recv = inner_left(mesh_rows, node_grad)
    grad_send = inner_left(embedded, sender_grad)
    mesh_grad = latent_grad.astype(jnp.float32) + outer_right(node_grad, w_recv)
    embedded_grad = outer_right(sender_grad, w_send).astype(jnp.bfloat16)
    return (mesh_grad, embedded_grad, (grad_send, grad_recv, grad_out))


def mesh_pass(halo_table, latent, cot_rows, u_src, u_dst, u_out, v_in, v_out, sources, targets):
    half = latent.shape[1] // 2
    nodes = latent.shape[0]
    upper = latent[:, :half]
    lower = latent[:, half:]
    source_part = matmul(halo_table, u_src)
    target_part = matmul(lower, u_dst)
    active = targets >= 0
    clipped = jnp.maximum(targets, 0)
    mesh_pre = jnp.take(source_part, sources, axis=0) + jnp.take(target_part, clipped, axis=0)
    mesh_msg = jnp.where(active[:, None], jax.nn.silu(mesh_pre), 0.0).astype(jnp.bfloat16)
    incidence = node_table(targets, nodes)
    summed = matmul(incidence, mesh_msg).astype(jnp.bfloat16)
    coupled = (upper.astype(jnp.float32) + matmul(summed, u_out)).astype(jnp.bfloat16)
    hidden_pre = matmul(coupled, v_in)
    hidden_act = jax.nn.silu(hidden_pre).astype(jnp.bfloat16)
    upper_cot = cot_rows[:, :half]
    lower_cot = cot_rows[:, half:]
    hidden_grad = (outer_right(lower_cot, v_out) * silu_grad(hidden_pre)).astype(jnp.bfloat16)
    grad_v_out = inner_left(hidden_act, lower_cot)
    grad_v_in = inner_left(coupled, hidden_grad)
    coupled_grad = (upper_cot.astype(jnp.float32) + outer_right(hidden_grad, v_in)).astype(
        jnp.bfloat16
    )
    grad_u_out = inner_left(summed, coupled_grad)
    summed_grad = outer_right(coupled_grad, u_out)
    mesh_edge_grad = jnp.where(
        active[:, None], jnp.take(summed_grad, clipped, axis=0) * silu_grad(mesh_pre), 0.0
    ).astype(jnp.bfloat16)
    target_grad = matmul(incidence, mesh_edge_grad).astype(jnp.bfloat16)
    source_grad = (
        jnp.zeros((halo_table.shape[0], source_part.shape[1]), jnp.float32)
        .at[sources]
        .add(mesh_edge_grad.astype(jnp.float32))
        .astype(jnp.bfloat16)
    )
    grad_u_dst = inner_left(lower, target_grad)
    grad_u_src = inner_left(halo_table, source_grad)
    table_grad = outer_right(source_grad, u_src)
    lower_grad = (
        lower_cot.astype(jnp.float32) + outer_right(target_grad, u_dst) + table_grad[:nodes]
    )
    halo_grad = table_grad[nodes:].astype(jnp.bfloat16)
    return (
        coupled_grad,
        lower_grad,
        halo_grad,
        (grad_u_src, grad_u_dst, grad_u_out, grad_v_in, grad_v_out),
    )


def trade_blocks(blocks):
    band_in = padded(blocks[0:2], (("band", 0),), 1, False)
    cycle_in = padded(blocks[2:4], (("patch", 0),), 1, True)
    return (band_in[0], band_in[3], cycle_in[0], cycle_in[3])


def spread_rows(local, order):
    band_pos = lax.axis_index("band")
    band_count = lax.axis_size("band")
    rim_rows = order.shape[0] // 16
    keep_rows = order.shape[0] - 4 * rim_rows
    picked = jnp.take(local, order, axis=0)
    blocks = picked[keep_rows:].reshape(4, rim_rows, local.shape[1])
    below_in, above_in, west_in, east_in = trade_blocks(blocks)
    from_below = jnp.where(band_pos > 0, below_in, blocks[0])
    from_above = jnp.where(band_pos < band_count - 1, above_in, blocks[1])
    return jnp.concatenate([picked[:keep_rows], from_below, from_above, west_in, east_in], axis=0)


def return_rows(grads, order):
    band_pos = lax.axis_index("band")
    band_count = lax.axis_size("band")
    rim_rows = order.shape[0] // 16
    keep_rows = order.shape[0] - 4 * rim_rows
    blocks = grads[keep_rows:].reshape(4, rim_rows, grads.shape[1])
    below_back, above_back, west_back, east_back = trade_blocks(blocks)
    first_block = jnp.where(band_pos > 0, below_back, blocks[0])
    second_block = jnp.where(band_pos < band_count - 1, above_back, blocks[1])
    local = jnp.concatenate(
        [grads[:keep_rows], first_block, second_block, west_back, east_back], axis=0
    )
    return jnp.zeros(grads.shape, grads.dtype).at[order].set(local)


def band_rim(pieces):
    return padded(pieces, (("band", 0),), 1, False)


def cycle_rim(pieces):
    return padded(pieces, (("patch", 0),), 1, True)


def body(
    grid_feats,
    mesh_feats,
    cotangent,
    w_embed,
    w_send,
    w_recv,
    w_out,
    u_src,
    u_dst,
    u_out,
    v_in,
    v_out,
    send_rows,
    enc_src,
    enc_dst,
    halo_send,
    mesh_src,
    mesh_dst,
):
    row_order = send_rows[0]
    own_pre, own_embedded = embed_rows(grid_feats, w_embed)
    embedded = spread_rows(own_embedded, row_order)
    sources = enc_src[0]
    targets = enc_dst[0]
    edge_pre, gathered, latent, incidence, active = encoder_edges(
        embedded, mesh_feats, w_send, w_recv, w_out, sources, targets
    )
    half = latent.shape[1] // 2
    lower = latent[:, half:]
    band_in = band_rim(jnp.take(lower, halo_send[0, 0], axis=0))
    cycle_in = cycle_rim(jnp.take(lower, halo_send[0, 1], axis=0))
    halo_table = jnp.concatenate([lower, band_in[0], band_in[3], cycle_in[0], cycle_in[3]], axis=0)
    coupled_grad, lower_grad, halo_grad, mesh_grads = mesh_pass(
        halo_table, latent, cotangent, u_src, u_dst, u_out, v_in, v_out, mesh_src[0], mesh_dst[0]
    )
    rim_count = halo_send.shape[3]
    returned = halo_grad.reshape(4, rim_count, half)
    band_back = band_rim(returned[0:2])
    cycle_back = cycle_rim(returned[2:4])
    lower_grad = lower_grad.at[halo_send[0, 0, 0]].add(band_back[0].astype(jnp.float32))
    lower_grad = lower_grad.at[halo_send[0, 0, 1]].add(band_back[3].astype(jnp.float32))
    lower_grad = lower_grad.at[halo_send[0, 1, 0]].add(cycle_back[0].astype(jnp.float32))
    lower_grad = lower_grad.at[halo_send[0, 1, 1]].add(cycle_back[3].astype(jnp.float32))
    latent_grad = jnp.concatenate([coupled_grad.astype(jnp.float32), lower_grad], axis=1).astype(
        jnp.bfloat16
    )
    mesh_grad, embedded_grad, enc_grads = encoder_back(
        embedded,
        mesh_feats,
        w_send,
        w_recv,
        w_out,
        sources,
        targets,
        edge_pre,
        gathered,
        incidence,
        active,
        latent_grad,
    )
    own_grad = return_rows(embedded_grad, row_order)
    grad_embed, grid_grad = embed_back(grid_feats, own_pre, own_grad, w_embed)
    totals = lax.psum(
        (
            grad_embed,
            enc_grads[0],
            enc_grads[1],
            enc_grads[2],
            mesh_grads[0],
            mesh_grads[1],
            mesh_grads[2],
            mesh_grads[3],
            mesh_grads[4],
        ),
        ("band", "patch"),
    )
    return (
        grid_grad,
        mesh_grad,
        totals[0],
        totals[1],
        totals[2],
        totals[3],
        totals[4],
        totals[5],
        totals[6],
        totals[7],
        totals[8],
    )


def solution(mesh):
    in_specs = (
        P(("band", "patch"), None),
        P(("band", "patch"), None),
        P(("band", "patch"), None),
        P(),
        P(),
        P(),
        P(),
        P(),
        P(),
        P(),
        P(),
        P(),
        P(("band", "patch"), None),
        P(("band", "patch"), None),
        P(("band", "patch"), None),
        P(("band", "patch"), None, None, None),
        P(("band", "patch"), None),
        P(("band", "patch"), None),
    )
    out_specs = (
        P(("band", "patch"), None),
        P(("band", "patch"), None),
        P(),
        P(),
        P(),
        P(),
        P(),
        P(),
        P(),
        P(),
        P(),
    )
    return jax.shard_map(body, mesh=mesh, in_specs=in_specs, out_specs=out_specs, check_vma=False)
```

profile of v0, /device:TPU:1, one launch (start us, length us, event | category | flops | bytes accessed | tf_op | source)
XLA Modules:
  0.0 483.3 jit_solution(7409408222091249871)
XLA Ops:
  9.3 4.3 multiply_convert_fusion.1
  13.6 9.2 %gather_fusion = bf16[2048,512]{1,0:T(8,128)(2,1)} fusion(bf16[2048,512]{1,0:T(8,128)(2,1)S(1)} %get-tuple-element.77, s32[2048]{0:T(1024)S(1)} %broadcast_clamp_fusion.2), kind=kCustom, calls=%fused_computation.6 | custom fusion | bytes 4202496 | tf_op jit(solution)/shard_map/jit(_take)/gather | solution.py:169
  22.8 1.8 broadcast_select_fusion
  24.7 5.1 %collective-permute-start = (bf16[1,128,512]{2,1,0:T(8,128)(2,1)S(1)}, bf16[1,128,512]{2,1,0:T(8,128)(2,1)S(1)}, u32[]{:S(2)}, u32[]{:S(2)}) collective-permute-start(bf16[1,128,512]{2,1,0:T(8,128)(2,1)S(1)} %slice_bitcast_fusion.7), channel_id=1, source_target_pairs={{0,16},{16,32},{32,48},{48,64},{64,80},{80,96},{96,112},{1,17},{17... | collective-permute-start | bytes 393224 | tf_op jit(solution)/shard_map/ppermute | solution.py:14
  31.7 1.6 slice_bitcast_fusion.6
  33.3 1.9 collective-permute-start.1
  35.7 4.5 collective-permute-done.1
  40.3 1.7 slice_bitcast_fusion.2
  43.5 16.9 %gather_fusion.3 = f32[4096,512]{1,0:T(8,128)} fusion(f32[256,512]{1,0:T(8,128)S(1)} %fusion.77, s32[4096]{0:T(1024)S(1)} %get-tuple-element.81), kind=kCustom, calls=%fused_computation.clone | custom fusion | bytes 16793600 | tf_op jit(solution)/shard_map/jit(_take)/gather | solution.py:65
  60.4 3.7 collective-permute-start.3
  66.8 4.8 %fusion.76 = f32[2048,512]{1,0:T(8,128)} fusion(bf16[2048,512]{1,0:T(8,128)(2,1)} %bitcast_dynamic-update-slice_fusion.2, bf16[512,512]{1,0:T(8,128)(2,1)S(1)} %copy-done.10), kind=kOutput, calls=%fused_computation.176 | convolution fusion | flops 1073741824 | bytes 6815744 | tf_op jit(solution)/shard_map/dot_general | solution.py:32
  71.6 20.2 %gather_fusion.1 = f32[4096,512]{1,0:T(8,128)} fusion(f32[2048,512]{1,0:T(8,128)} %fusion.76, s32[4096]{0:T(1024)S(1)} %get-tuple-element.82), kind=kCustom, calls=%fused_computation.7 | custom fusion | bytes 16793600 | tf_op jit(solution)/shard_map/jit(_take)/gather | solution.py:65
  91.9 10.4 %fusion.16 = bf16[256,512]{1,0:T(8,128)(2,1)S(1)} fusion(pred[4096]{0:T(1024)(128)(4,1)S(1)} %get-tuple-element.66, s32[4096]{0:T(1024)S(1)} %bitcast.172, f32[4096,512]{1,0:T(8,128)} %gather_fusion.3, f32[4096,512]{1,0:T(8,128)} %gather_fusion.1, pred[4096]{0:T(1024)(128)(4,1)S(1)} %get-tuple-element.65, pred[4096]{0:T(1024)(128)(4,1)S(1)} %compare_and_fusion), kind=kOutput, calls=%fused_computation.55 | convolution fusion | flops 1093795840 | bytes 17068032 | tf_op jit(solution)/shard_map/dot_general | solution.py:32
  103.7 3.1 collective-permute-start.4
  106.8 1.9 collective-permute-start.5
  109.6 5.8 %collective-permute-start.7 = (bf16[1,32,256]{2,1,0:T(8,128)(2,1)S(1)}, bf16[1,32,256]{2,1,0:T(8,128)(2,1)S(1)}, u32[]{:S(2)}, u32[]{:S(2)}) collective-permute-start(bf16[1,32,256]{2,1,0:T(8,128)(2,1)S(1)} %get-tuple-element.61), channel_id=1, source_target_pairs={{1,0},{2,1},{3,2},{4,3},{5,4},{6,5},{7,6},{8,7},{9,8},{10,9},{11,1... | collective-permute-start | bytes 49160 | tf_op jit(solution)/shard_map/ppermute | solution.py:17
  115.3 8.9 %gather_fusion.6 = f32[2048,512]{1,0:T(8,128)} fusion(f32[256,512]{1,0:T(8,128)S(1)} %fusion.70, s32[2048]{0:T(1024)S(1)} %get-tuple-element.83), kind=kCustom, calls=%fused_computation.2.clone | custom fusion | bytes 8396800 | tf_op jit(solution)/shard_map/jit(_take)/gather | solution.py:116
  124.6 9.0 %gather_fusion.2 = f32[2048,512]{1,0:T(8,128)} fusion(f32[384,512]{1,0:T(8,128)S(1)} %fusion.78, s32[2048]{0:T(1024)S(1)} %get-tuple-element.84), kind=kCustom, calls=%fused_computation.8 | custom fusion | bytes 8396800 | tf_op jit(solution)/shard_map/jit(_take)/gather | solution.py:116
  133.6 5.6 %fusion.15 = bf16[256,512]{1,0:T(8,128)(2,1)S(1)} fusion(pred[2048]{0:T(1024)(128)(4,1)S(1)} %get-tuple-element.68, s32[2048]{0:T(1024)S(1)} %bitcast.182, f32[2048,512]{1,0:T(8,128)} %gather_fusion.6, f32[2048,512]{1,0:T(8,128)} %gather_fusion.2, pred[2048]{0:T(1024)(128)(4,1)S(1)} %get-tuple-element.67, pred[2048]{0:T(1024)(128)(4,1)S(1)} %compare_and_fusion.1), kind=kOutput, calls=%fused_computation.54 | convolution fusion | flops 546963456 | bytes 8665088 | tf_op jit(solution)/shard_map/dot_general | solution.py:32
  141.9 8.9 %gather_fusion.7 = f32[2048,512]{1,0:T(8,128)} fusion(f32[256,512]{1,0:T(8,128)S(1)} %fusion.80, s32[2048]{0:T(1024)S(1)} %get-tuple-element.83), kind=kCustom, calls=%fused_computation.5.clone | custom fusion | bytes 8396800 | tf_op jit(solution)/shard_map/jit(_take)/gather | solution.py:134
  150.8 6.3 %fusion.5 = bf16[2048,512]{1,0:T(8,128)(2,1)S(1)} fusion(f32[2048,512]{1,0:T(8,128)} %gather_fusion.7, pred[2048]{0:T(1024)(128)(4,1)S(1)} %get-tuple-element.67, pred[2048]{0:T(1024)(128)(4,1)S(1)} %get-tuple-element.68, f32[2048,512]{1,0:T(8,128)} %gather_fusion.6, f32[2048,512]{1,0:T(8,128)} %gather_fusion.2, pred[2048]{0:T(1024)(128)(4,1)S(1)} %compare_and_fusion.1), kind=kLoop, calls=%fused_computation.26 | loop fusion | flops 14680064 | bytes 14686208 | tf_op jit(solution)/shard_map/convert_element_type | solution.py:135
  158.5 13.7 %scatter_custom_fusion = f32[384,512]{1,0:T(8,128)} fusion(s32[2048]{0:T(1024)S(1)} %bitcast.185, bf16[2048,512]{1,0:T(8,128)(2,1)S(1)} %fusion.5, f32[]{:T(128)} %constant.59.clone.1), kind=kCustom, calls=%fused_computation.29 | custom fusion | flops 2097152 | bytes 2883588 | tf_op jit(solution)/shard_map/scatter-add | solution.py:140
  172.3 1.6 fusion.75
  173.8 2.4 fusion.33
  176.2 2.1 fusion.81
  178.3 2.2 fusion.32
  181.8 3.9 collective-permute-start.8
  185.8 1.9 collective-permute-start.9
  187.8 4.8 collective-permute-start.11
  198.4 16.9 %gather_fusion.8 = f32[4096,512]{1,0:T(8,128)} fusion(f32[256,512]{1,0:T(8,128)S(1)} %fusion.44, s32[4096]{0:T(1024)S(1)} %get-tuple-element.81), kind=kCustom, calls=%fused_computation.3.clone | custom fusion | bytes 16793600 | tf_op jit(solution)/shard_map/jit(_take)/gather | solution.py:91
  215.3 11.1 %fusion.1 = bf16[4096,512]{1,0:T(8,128)(2,1)} fusion(f32[4096,512]{1,0:T(8,128)} %gather_fusion.8, pred[4096]{0:T(1024)(128)(4,1)S(1)} %get-tuple-element.65, pred[4096]{0:T(1024)(128)(4,1)S(1)} %get-tuple-element.66, f32[4096,512]{1,0:T(8,128)} %gather_fusion.3, f32[4096,512]{1,0:T(8,128)} %gather_fusion.1, pred[4096]{0:T(1024)(128)(4,1)S(1)} %compare_and_fusion), kind=kLoop, calls=%fused_computation.18 | loop fusion | flops 29360128 | bytes 29372416 | tf_op jit(solution)/shard_map/convert_element_type | solution.py:92
  226.5 27.8 %scatter_custom_fusion.5 = f32[2048,512]{1,0:T(8,128)} fusion(s32[4096]{0:T(1024)S(1)} %bitcast.175, bf16[4096,512]{1,0:T(8,128)(2,1)} %fusion.1, f32[]{:T(128)} %constant.59.clone.1), kind=kCustom, calls=%fused_computation.20 | custom fusion | flops 4194304 | bytes 8388612 | tf_op jit(solution)/shard_map/scatter-add | solution.py:97
  254.2 3.6 convolution_convert_fusion
  258.3 2.2 fusion.24
  260.6 4.3 collective-permute-start.12
  266.9 1.9 collective-permute-start.13
  270.1 3.8 collective-permute-done.13
  275.4 4.8 collective-permute-start.15
  282.1 11.2 %scatter_custom_fusion.6 = bf16[2048,512]{1,0:T(8,128)(2,1)} fusion(s32[2048]{0:T(1024)} %bitcast.179, bf16[2048,512]{1,0:T(8,128)(2,1)S(1)} %bitcast_dynamic-update-slice_fusion, bf16[]{:T(256)} %constant.49.clone.1), kind=kCustom, calls=%fused_computation.71 | custom fusion | bytes 2097664 | tf_op jit(solution)/shard_map/scatter | solution.py:189
  293.3 4.5 multiply_convert_fusion
  297.8 1.4 convolution_bitcast_fusion.1
  299.2 2.3 convolution_add_fusion
  301.5 2.0 copy.40
  303.6 1.7 convolution_convert_fusion.1
  305.2 159.3 %all-reduce.3.cloned.1.call-done = (f32[227,512]{1,0:T(8,128)}, f32[512,512]{1,0:T(8,128)}, f32[512,512]{0,1:T(8,128)}, f32[512,512]{1,0:T(8,128)}, f32[256,512]...) async-done(((f32[227,512]{1,0:T(8,128)}, f32[512,512]{1,0:T(8,128)}, f32[512,512]{0,1:T(8,128)}, ...) | async-done | bytes 6232080 | tf_op jit(solution)/shard_map/psum | solution.py:263
  464.5 2.7 copy.41
  467.2 1.9 copy.69
  469.1 2.3 copy.70
  (178 shorter events, 34.3 us)
Async XLA Ops:
  7.2 457.4 %all-reduce.3.cloned.1.call-start = ((), (), s32[]{:S(2)}) async-start(), calls=%async_computation | async-start | bytes 12484608 | tf_op jit(solution)/shard_map/psum | solution.py:263
  22.8 8.3 %copy-start.37 = (s32[1,4096]{1,0:T(1,128)S(1)}, s32[1,4096]{1,0:T(1,128)}, u32[]{:S(2)}) copy-start(s32[1,4096]{1,0:T(1,128)} %param.37) | copy-start | bytes 49156
  22.8 8.3 %copy-start.41 = (s32[1,2048]{1,0:T(1,128)S(1)}, s32[1,2048]{1,0:T(1,128)}, u32[]{:S(2)}) copy-start(s32[1,2048]{1,0:T(1,128)} %param.41) | copy-start | bytes 24580
  22.8 8.3 %copy-start.38 = (s32[1,4096]{1,0:T(1,128)S(1)}, s32[1,4096]{1,0:T(1,128)}, u32[]{:S(2)}) copy-start(s32[1,4096]{1,0:T(1,128)} %param.38) | copy-start | bytes 49156
  22.8 8.4 %copy-start.39 = (s32[1,2048]{1,0:T(1,128)S(1)}, s32[1,2048]{1,0:T(1,128)}, u32[]{:S(2)}) copy-start(s32[1,2048]{1,0:T(1,128)} %param.40) | copy-start | bytes 24580
  22.8 8.4 %copy-start.5 = (bf16[256,512]{1,0:T(8,128)(2,1)S(1)}, bf16[256,512]{1,0:T(8,128)(2,1)}, u32[]{:S(2)}) copy-start(bf16[256,512]{1,0:T(8,128)(2,1)} %param.25) | copy-start | bytes 786436
  22.8 8.4 %copy-start.7 = (bf16[512,512]{1,0:T(8,128)(2,1)S(1)}, bf16[512,512]{1,0:T(8,128)(2,1)}, u32[]{:S(2)}) copy-start(bf16[512,512]{1,0:T(8,128)(2,1)} %param.29) | copy-start | bytes 1572868
  22.8 8.7 %copy-start.42 = (s32[1,2,2,32]{3,2,1,0:T(2,128)S(1)}, s32[1,2,2,32]{3,2,1,0:T(2,128)}, u32[]{:S(2)}) copy-start(s32[1,2,2,32]{3,2,1,0:T(2,128)} %param.39) | copy-start | bytes 1540
  24.7 18.7 %slice-start = ((bf16[256,512]{1,0:T(8,128)(2,1)}), bf16[256,256]{1,0:T(8,128)(2,1)S(1)}, s32[]{:S(2)}) async-start(bf16[256,512]{1,0:T(8,128)(2,1)} %param.26), calls=%async_computation.1 | async-start | bytes 262144 | tf_op jit(solution)/shard_map/slice | solution.py:123
  24.7 7.0 %collective-permute-start = (bf16[1,128,512]{2,1,0:T(8,128)(2,1)S(1)}, bf16[1,128,512]{2,1,0:T(8,128)(2,1)S(1)}, u32[]{:S(2)}, u32[]{:S(2)}) collective-permute-start(bf16[1,128,512]{2,1,0:T(8,128)(2,1)S(1)} %slice_bitcast_fusion.7), channel_id=1, source_target_pairs={{0,16},{16,32},{32,48},{48,64},{64,80},{80,96},{96,112},{1,17},{17... | collective-permute-start | bytes 393224 | tf_op jit(solution)/shard_map/ppermute | solution.py:14
  33.3 7.0 %collective-permute-start.1 = (bf16[1,128,512]{2,1,0:T(8,128)(2,1)S(1)}, bf16[1,128,512]{2,1,0:T(8,128)(2,1)S(1)}, u32[]{:S(2)}, u32[]{:S(2)}) collective-permute-start(bf16[1,128,512]{2,1,0:T(8,128)(2,1)S(1)} %get-tuple-element.53), channel_id=1, source_target_pairs={{16,0},{32,16},{48,32},{64,48},{80,64},{96,80},{112,96},{17,1},{33... | collective-permute-start | bytes 393224 | tf_op jit(solution)/shard_map/ppermute | solution.py:17
  42.0 22.1 %collective-permute-start.2 = (bf16[1,128,512]{2,1,0:T(8,128)(2,1)S(1)}, bf16[1,128,512]{2,1,0:T(8,128)(2,1)S(1)}, u32[]{:S(2)}, u32[]{:S(2)}) collective-permute-start(bf16[1,128,512]{2,1,0:T(8,128)(2,1)S(1)} %get-tuple-element.52), channel_id=1, source_target_pairs={{0,1},{1,2},{2,3},{3,4},{4,5},{5,6},{6,7},{7,8},{8,9},{9,10},{10,1... | collective-permute-start | bytes 393224 | tf_op jit(solution)/shard_map/ppermute | solution.py:14
  43.5 23.3 %copy-start.10 = (bf16[512,512]{1,0:T(8,128)(2,1)S(1)}, bf16[512,512]{1,0:T(8,128)(2,1)}, u32[]{:S(2)}) copy-start(bf16[512,512]{1,0:T(8,128)(2,1)} %param.28) | copy-start | bytes 1572868
  60.4 5.7 %collective-permute-start.3 = (bf16[1,128,512]{2,1,0:T(8,128)(2,1)S(1)}, bf16[1,128,512]{2,1,0:T(8,128)(2,1)S(1)}, u32[]{:S(2)}, u32[]{:S(2)}) collective-permute-start(bf16[1,128,512]{2,1,0:T(8,128)(2,1)S(1)} %get-tuple-element.50), channel_id=1, source_target_pairs={{1,0},{2,1},{3,2},{4,3},{5,4},{6,5},{7,6},{8,7},{9,8},{10,9},{11,1... | collective-permute-start | bytes 393224 | tf_op jit(solution)/shard_map/ppermute | solution.py:17
  91.9 10.4 %copy-start.8 = (bf16[512,512]{1,0:T(8,128)(2,1)S(1)}, bf16[512,512]{1,0:T(8,128)(2,1)}, u32[]{:S(2)}) copy-start(bf16[512,512]{1,0:T(8,128)(2,1)} %param.30) | copy-start | bytes 1572868
  91.9 10.8 %copy-start.22 = (bf16[256,512]{1,0:T(8,128)(2,1)S(1)}, bf16[256,512]{1,0:T(8,128)(2,1)}, u32[]{:S(2)}) copy-start(bf16[256,512]{1,0:T(8,128)(2,1)} %param.32) | copy-start | bytes 786436
  102.3 22.0 %copy-start.24 = (bf16[256,512]{1,0:T(8,128)(2,1)}, bf16[256,512]{1,0:T(8,128)(2,1)S(1)}, u32[]{:S(2)}) copy-start(bf16[256,512]{1,0:T(8,128)(2,1)S(1)} %fusion.16) | copy-start | bytes 786436
  103.7 20.6 %collective-permute-start.4 = (bf16[1,32,256]{2,1,0:T(8,128)(2,1)S(1)}, bf16[1,32,256]{2,1,0:T(8,128)(2,1)S(1)}, u32[]{:S(2)}, u32[]{:S(2)}) collective-permute-start(bf16[1,32,256]{2,1,0:T(8,128)(2,1)S(1)} %get-tuple-element.64), channel_id=1, source_target_pairs={{0,16},{16,32},{32,48},{48,64},{64,80},{80,96},{96,112},{1,17},{17... | collective-permute-start | bytes 49160 | tf_op jit(solution)/shard_map/ppermute | solution.py:14
  106.8 17.5 %collective-permute-start.5 = (bf16[1,32,256]{2,1,0:T(8,128)(2,1)S(1)}, bf16[1,32,256]{2,1,0:T(8,128)(2,1)S(1)}, u32[]{:S(2)}, u32[]{:S(2)}) collective-permute-start(bf16[1,32,256]{2,1,0:T(8,128)(2,1)S(1)} %get-tuple-element.63), channel_id=1, source_target_pairs={{16,0},{32,16},{48,32},{64,48},{80,64},{96,80},{112,96},{17,1},{33... | collective-permute-start | bytes 49160 | tf_op jit(solution)/shard_map/ppermute | solution.py:17
  109.5 14.8 %collective-permute-start.6 = (bf16[1,32,256]{2,1,0:T(8,128)(2,1)S(1)}, bf16[1,32,256]{2,1,0:T(8,128)(2,1)S(1)}, u32[]{:S(2)}, u32[]{:S(2)}) collective-permute-start(bf16[1,32,256]{2,1,0:T(8,128)(2,1)S(1)} %get-tuple-element.62), channel_id=1, source_target_pairs={{0,1},{1,2},{2,3},{3,4},{4,5},{5,6},{6,7},{7,8},{8,9},{9,10},{10,1... | collective-permute-start | bytes 49160 | tf_op jit(solution)/shard_map/ppermute | solution.py:14
  109.6 14.8 %collective-permute-start.7 = (bf16[1,32,256]{2,1,0:T(8,128)(2,1)S(1)}, bf16[1,32,256]{2,1,0:T(8,128)(2,1)S(1)}, u32[]{:S(2)}, u32[]{:S(2)}) collective-permute-start(bf16[1,32,256]{2,1,0:T(8,128)(2,1)S(1)} %get-tuple-element.61), channel_id=1, source_target_pairs={{1,0},{2,1},{3,2},{4,3},{5,4},{6,5},{7,6},{8,7},{9,8},{10,9},{11,1... | collective-permute-start | bytes 49160 | tf_op jit(solution)/shard_map/ppermute | solution.py:17
  115.3 9.0 %copy-start.17 = (bf16[256,512]{1,0:T(8,128)(2,1)S(1)}, bf16[256,512]{1,0:T(8,128)(2,1)}, u32[]{:S(2)}) copy-start(bf16[256,512]{1,0:T(8,128)(2,1)} %param.31) | copy-start | bytes 786436
  124.4 9.2 %copy-start.12 = (bf16[384,256]{1,0:T(8,128)(2,1)}, bf16[384,256]{1,0:T(8,128)(2,1)S(1)}, u32[]{:S(2)}) copy-start(bf16[384,256]{1,0:T(8,128)(2,1)S(1)} %constant_dynamic-update-slice_fusion) | copy-start | bytes 589828
  133.6 7.0 %copy-start.15 = (bf16[256,512]{1,0:T(8,128)(2,1)S(1)}, bf16[256,512]{1,0:T(8,128)(2,1)}, u32[]{:S(2)}) copy-start(bf16[256,512]{1,0:T(8,128)(2,1)} %param.34) | copy-start | bytes 786436
  133.6 7.2 %copy-start.34 = (bf16[256,512]{1,0:T(8,128)(2,1)S(1)}, bf16[256,512]{1,0:T(8,128)(2,1)}, u32[]{:S(2)}) copy-start(bf16[256,512]{1,0:T(8,128)(2,1)} %param.26) | copy-start | bytes 786436
  133.6 7.2 %copy-start.43 = (bf16[512,256]{1,0:T(8,128)(2,1)S(1)}, bf16[512,256]{1,0:T(8,128)(2,1)}, u32[]{:S(2)}) copy-start(bf16[512,256]{1,0:T(8,128)(2,1)} %param.35) | copy-start | bytes 786436
  172.2 8.2 %copy-start.26 = (bf16[256,512]{1,0:T(8,128)(2,1)S(1)}, bf16[256,512]{1,0:T(8,128)(2,1)}, u32[]{:S(2)}) copy-start(bf16[256,512]{1,0:T(8,128)(2,1)} %fusion.17) | copy-start | bytes 786436
  172.2 9.3 %copy-start.23 = (bf16[256,512]{1,0:T(8,128)(2,1)S(1)}, bf16[256,512]{1,0:T(8,128)(2,1)}, u32[]{:S(2)}) copy-start(bf16[256,512]{1,0:T(8,128)(2,1)} %param.32) | copy-start | bytes 786436
  172.2 9.3 %copy-start.35 = (bf16[256,512]{1,0:T(8,128)(2,1)S(1)}, bf16[256,512]{1,0:T(8,128)(2,1)}, u32[]{:S(2)}) copy-start(bf16[256,512]{1,0:T(8,128)(2,1)} %param.26) | copy-start | bytes 786436
  172.2 20.3 %copy-start.14 = (bf16[256,256]{1,0:T(8,128)(2,1)S(1)}, bf16[256,256]{1,0:T(8,128)(2,1)}, u32[]{:S(2)}) copy-start(bf16[256,256]{1,0:T(8,128)(2,1)} %copy-done.13) | copy-start | bytes 393220
  172.2 20.3 %copy-start.19 = (bf16[256,512]{1,0:T(8,128)(2,1)S(1)}, bf16[256,512]{1,0:T(8,128)(2,1)}, u32[]{:S(2)}) copy-start(bf16[256,512]{1,0:T(8,128)(2,1)} %copy-done.18) | copy-start | bytes 786436
  176.2 21.9 %copy-start.9 = (bf16[512,512]{1,0:T(8,128)(2,1)S(1)}, bf16[512,512]{1,0:T(8,128)(2,1)}, u32[]{:S(2)}) copy-start(bf16[512,512]{1,0:T(8,128)(2,1)} %param.30) | copy-start | bytes 1572868
  181.8 11.8 %collective-permute-start.8 = (bf16[1,32,256]{2,1,0:T(8,128)(2,1)S(1)}, bf16[1,32,256]{2,1,0:T(8,128)(2,1)S(1)}, u32[]{:S(2)}, u32[]{:S(2)}) collective-permute-start(bf16[1,32,256]{2,1,0:T(8,128)(2,1)S(1)} %get-tuple-element.60), channel_id=1, source_target_pairs={{0,16},{16,32},{32,48},{48,64},{64,80},{80,96},{96,112},{1,17},{17... | collective-permute-start | bytes 49160 | tf_op jit(solution)/shard_map/ppermute | solution.py:14
  185.8 8.9 %collective-permute-start.9 = (bf16[1,32,256]{2,1,0:T(8,128)(2,1)S(1)}, bf16[1,32,256]{2,1,0:T(8,128)(2,1)S(1)}, u32[]{:S(2)}, u32[]{:S(2)}) collective-permute-start(bf16[1,32,256]{2,1,0:T(8,128)(2,1)S(1)} %get-tuple-element.59), channel_id=1, source_target_pairs={{16,0},{32,16},{48,32},{64,48},{80,64},{96,80},{112,96},{17,1},{33... | collective-permute-start | bytes 49160 | tf_op jit(solution)/shard_map/ppermute | solution.py:17
  187.7 8.0 %collective-permute-start.10 = (bf16[1,32,256]{2,1,0:T(8,128)(2,1)S(1)}, bf16[1,32,256]{2,1,0:T(8,128)(2,1)S(1)}, u32[]{:S(2)}, u32[]{:S(2)}) collective-permute-start(bf16[1,32,256]{2,1,0:T(8,128)(2,1)S(1)} %get-tuple-element.58), channel_id=1, source_target_pairs={{0,1},{1,2},{2,3},{3,4},{4,5},{5,6},{6,7},{7,8},{8,9},{9,10},{10,1... | collective-permute-start | bytes 49160 | tf_op jit(solution)/shard_map/ppermute | solution.py:14
  187.8 8.9 %collective-permute-start.11 = (bf16[1,32,256]{2,1,0:T(8,128)(2,1)S(1)}, bf16[1,32,256]{2,1,0:T(8,128)(2,1)S(1)}, u32[]{:S(2)}, u32[]{:S(2)}) collective-permute-start(bf16[1,32,256]{2,1,0:T(8,128)(2,1)S(1)} %get-tuple-element.57), channel_id=1, source_target_pairs={{1,0},{2,1},{3,2},{4,3},{5,4},{6,5},{7,6},{8,7},{9,8},{10,9},{11,1... | collective-permute-start | bytes 49160 | tf_op jit(solution)/shard_map/ppermute | solution.py:17
  226.4 27.8 %copy-start.11 = (bf16[512,512]{1,0:T(8,128)(2,1)S(1)}, bf16[512,512]{1,0:T(8,128)(2,1)}, u32[]{:S(2)}) copy-start(bf16[512,512]{1,0:T(8,128)(2,1)} %param.28) | copy-start | bytes 1572868
  258.0 7.0 %copy-start.3 = (bf16[4096,512]{1,0:T(8,128)(2,1)S(1)}, bf16[4096,512]{1,0:T(8,128)(2,1)}, u32[]{:S(2)}) copy-start(bf16[4096,512]{1,0:T(8,128)(2,1)} %fusion.1) | copy-start | bytes 12582916
  260.6 8.2 %copy-start.6 = (bf16[256,512]{1,0:T(8,128)(2,1)S(1)}, bf16[256,512]{1,0:T(8,128)(2,1)}, u32[]{:S(2)}) copy-start(bf16[256,512]{1,0:T(8,128)(2,1)} %param.25) | copy-start | bytes 786436
  260.6 13.4 %copy-start.25 = (bf16[256,512]{1,0:T(8,128)(2,1)S(1)}, bf16[256,512]{1,0:T(8,128)(2,1)}, u32[]{:S(2)}) copy-start(bf16[256,512]{1,0:T(8,128)(2,1)} %copy-done.24) | copy-start | bytes 786436
  260.6 6.3 %collective-permute-start.12 = (bf16[1,128,512]{2,1,0:T(8,128)(2,1)S(1)}, bf16[1,128,512]{2,1,0:T(8,128)(2,1)S(1)}, u32[]{:S(2)}, u32[]{:S(2)}) collective-permute-start(bf16[1,128,512]{2,1,0:T(8,128)(2,1)S(1)} %slice_bitcast_fusion.5), channel_id=1, source_target_pairs={{0,16},{16,32},{32,48},{48,64},{64,80},{80,96},{96,112},{1,17},{17... | collective-permute-start | bytes 393224 | tf_op jit(solution)/shard_map/ppermute | solution.py:14
  266.2 15.0 %copy-start.27 = (bf16[256,512]{1,0:T(8,128)(2,1)}, bf16[256,512]{1,0:T(8,128)(2,1)S(1)}, u32[]{:S(2)}) copy-start(bf16[256,512]{1,0:T(8,128)(2,1)S(1)} %fusion.19) | copy-start | bytes 786436
  266.9 7.0 %collective-permute-start.13 = (bf16[1,128,512]{2,1,0:T(8,128)(2,1)S(1)}, bf16[1,128,512]{2,1,0:T(8,128)(2,1)S(1)}, u32[]{:S(2)}, u32[]{:S(2)}) collective-permute-start(bf16[1,128,512]{2,1,0:T(8,128)(2,1)S(1)} %get-tuple-element.48), channel_id=1, source_target_pairs={{16,0},{32,16},{48,32},{64,48},{80,64},{96,80},{112,96},{17,1},{33... | collective-permute-start | bytes 393224 | tf_op jit(solution)/shard_map/ppermute | solution.py:17
  273.9 7.2 %collective-permute-start.14 = (bf16[1,128,512]{2,1,0:T(8,128)(2,1)S(1)}, bf16[1,128,512]{2,1,0:T(8,128)(2,1)S(1)}, u32[]{:S(2)}, u32[]{:S(2)}) collective-permute-start(bf16[1,128,512]{2,1,0:T(8,128)(2,1)S(1)} %get-tuple-element.47), channel_id=1, source_target_pairs={{0,1},{1,2},{2,3},{3,4},{4,5},{5,6},{6,7},{7,8},{8,9},{9,10},{10,1... | collective-permute-start | bytes 393224 | tf_op jit(solution)/shard_map/ppermute | solution.py:14
  275.4 6.7 %collective-permute-start.15 = (bf16[1,128,512]{2,1,0:T(8,128)(2,1)S(1)}, bf16[1,128,512]{2,1,0:T(8,128)(2,1)S(1)}, u32[]{:S(2)}, u32[]{:S(2)}) collective-permute-start(bf16[1,128,512]{2,1,0:T(8,128)(2,1)S(1)} %get-tuple-element.45), channel_id=1, source_target_pairs={{1,0},{2,1},{3,2},{4,3},{5,4},{6,5},{7,6},{8,7},{9,8},{10,9},{11,1... | collective-permute-start | bytes 393224 | tf_op jit(solution)/shard_map/ppermute | solution.py:17
  464.5 8.7 %copy-start.32 = (f32[256,512]{1,0:T(8,128)S(1)}, f32[256,512]{1,0:T(8,128)}, u32[]{:S(2)}) copy-start(f32[256,512]{1,0:T(8,128)} %get-tuple-element.94) | copy-start | bytes 1572868
  464.5 9.5 %copy-start.31 = (f32[512,256]{1,0:T(8,128)S(1)}, f32[512,256]{1,0:T(8,128)}, u32[]{:S(2)}) copy-start(f32[512,256]{1,0:T(8,128)} %get-tuple-element.95) | copy-start | bytes 1572868
  467.2 7.6 %copy-start.30 = (f32[256,512]{1,0:T(8,128)S(1)}, f32[256,512]{1,0:T(8,128)}, u32[]{:S(2)}) copy-start(f32[256,512]{1,0:T(8,128)} %get-tuple-element.96) | copy-start | bytes 1572868
  (14 other events, 47.3 us)
Sparse Core Ops, SparseCore 0:
  299.3 165.1 all-reduce.2
where the time goes:
time: 484 us; the launch traced here: 483 us
  waiting for transfers between devices  172 us (36%)
  local copies, waits for them, and re-layouts  122 us (25%)
  other arithmetic  75.2 us (16%)
  matrix products  54.9 us (11%)
  starting transfers between devices  44.6 us (9%)
  between operations  14.9 us (3%)
    psum x1, waiting for transfers between devices, body(): lax.psum((grad_embed, enc_grads[0], enc_grads[1], enc_grads[2], mesh_grad...  159 us
    dot_general x12, matrix products, matmul(): return jnp.dot(left, right, preferred_element_type=jnp.float32)  29.3 us
    scatter-add x1, other arithmetic, encoder_back(): sender_grad = jnp.zeros((embedded.shape[0], embedded.shape[1]), jnp.float...  27.8 us
    ppermute x8, starting transfers between devices, padded(): lax.ppermute(lax.slice_in_dim(block, 0, width, axis=dim), axis, backward)  26.7 us
    gather x1, local copies, waits for them, and re-layouts, encoder_edges(): jnp.take(sender_part, sources, axis=0)  20.2 us
    unnamed x106, local copies, waits for them, and re-layouts  18.4 us
    ppermute x8, starting transfers between devices, padded(): lax.ppermute(lax.slice_in_dim(block, block.shape[dim] - width, None, axis...  17.8 us
    gather x1, local copies, waits for them, and re-layouts, encoder_edges(): jnp.take(node_part, clipped, axis=0)  16.9 us
  transfers between devices with their start and end apart: 17, of which 8 were waited for; matrix products, arithmetic and copies ran while one was open for 9% of the time, Pallas kernels for 0%

commit v1 on v0

v1 whole, which is shorter than its diff:
```python
import jax
import jax.numpy as jnp
from jax import lax
from jax.experimental import pallas as pl
from jax.experimental.pallas import tpu as pltpu
from jax.sharding import PartitionSpec as P

BF16 = jnp.bfloat16
F32 = jnp.float32
LANES = 128
EDGE_TILE = 512
ROW_TILE = 512
VMEM_LIMIT = 56 * 1024 * 1024


def mm(left, right):
    return lax.dot_general(left, right, (((1,), (0,)), ((), ())), preferred_element_type=F32)


def mm_left(left, right):
    return lax.dot_general(left, right, (((0,), (0,)), ((), ())), preferred_element_type=F32)


def mm_right(left, right):
    return lax.dot_general(left, right, (((1,), (1,)), ((), ())), preferred_element_type=F32)


def table_by_row(index, count):
    n = index.shape[1]
    rows = lax.broadcasted_iota(jnp.int32, (count, n), 0)
    return jnp.where(rows == index, 1.0, 0.0).astype(BF16)


def table_by_column(index, count):
    n = index.shape[1]
    parts = []
    for start in range(0, n, LANES):
        width = min(LANES, n - start)
        piece = jnp.broadcast_to(index[:, start : start + width], (LANES, width))
        column = jnp.transpose(piece)
        wide = jnp.concatenate([column] * (count // LANES), axis=1)
        columns = lax.broadcasted_iota(jnp.int32, (width, count), 1)
        parts.append(jnp.where(wide == columns, 1.0, 0.0).astype(BF16))
    return parts[0] if len(parts) == 1 else jnp.concatenate(parts, axis=0)


def silu_both(value):
    sigma = 0.5 * jnp.tanh(0.5 * value) + 0.5
    act = value * sigma
    return act, sigma + act * (1.0 - sigma)


def call(kernel, out_shape, **more):
    return pl.pallas_call(
        kernel,
        out_shape=out_shape,
        compiler_params=pltpu.CompilerParams(vmem_limit_bytes=VMEM_LIMIT),
        **more,
    )


def shape(dims, kind):
    return jax.ShapeDtypeStruct(tuple(dims), kind)


def pick_rim_kernel(order_ref, grid_ref, *out_refs):
    rim = out_refs[0].shape[1]
    keep = order_ref.shape[1] - 4 * rim
    table = table_by_row(order_ref[:, keep:], grid_ref.shape[1])
    picked = mm(grid_ref[...], table).astype(BF16)
    for k in range(4):
        out_refs[k][...] = picked[:, k * rim : (k + 1) * rim]


def keep_kernel(order_ref, grid_ref, mesh_ref, embed_ref, send_ref, recv_ref, rows_ref, sender_ref, node_ref):
    keep = rows_ref.shape[1]
    node_ref[...] = mm(mesh_ref[...], recv_ref[...]).astype(BF16)

    def step(i, carry):
        start = pl.multiple_of(i * ROW_TILE, ROW_TILE)
        table = table_by_row(order_ref[:, pl.ds(start, ROW_TILE)], grid_ref.shape[1])
        rows = mm(grid_ref[...], table).astype(BF16)
        rows_ref[:, pl.ds(start, ROW_TILE)] = rows
        embedded = silu_both(mm_left(rows, embed_ref[...]))[0].astype(BF16)
        sender_ref[pl.ds(start, ROW_TILE), :] = mm(embedded, send_ref[...]).astype(BF16)
        return carry

    lax.fori_loop(0, keep // ROW_TILE, step, 0)


def encode_kernel(
    flag_ref, src_ref, dst_ref, halo_ref, sender_ref, node_ref, mesh_ref, embed_ref, send_ref, out_w_ref,
    in0, in1, in2, in3, own0, own1,
    rim_ref, slope_ref, gathered_ref, latent_ref, h00, h01, h10, h11,
    table, total,
):
    step = pl.program_id(0)
    keep = sender_ref.shape[0]
    rim = in0.shape[1]
    rows = keep + 4 * rim
    nodes = node_ref.shape[0]

    @pl.when(step == 0)
    def _():
        table[0:keep, :] = sender_ref[...]
        table[rows : rows + nodes, :] = node_ref[...]
        rim_ref[:, 0:rim] = jnp.where(flag_ref[0] > 0, in0[...], own0[...])
        rim_ref[:, rim : 2 * rim] = jnp.where(flag_ref[1] > 0, in1[...], own1[...])
        rim_ref[:, 2 * rim : 3 * rim] = in2[...]
        rim_ref[:, 3 * rim : 4 * rim] = in3[...]
        embedded = silu_both(mm_left(rim_ref[...], embed_ref[...]))[0].astype(BF16)
        table[keep:rows, :] = mm(embedded, send_ref[...]).astype(BF16)
        total[...] = jnp.zeros_like(total)

    both = jnp.concatenate([table_by_column(src_ref[...], rows), table_by_column(dst_ref[...], nodes)], axis=1)
    act, slope = silu_both(mm(both, table[...]))
    slope_ref[...] = slope.astype(BF16)
    total[...] += mm(table_by_row(dst_ref[...], nodes), act.astype(BF16))

    @pl.when(step == pl.num_programs(0) - 1)
    def _():
        gathered = total[...].astype(BF16)
        gathered_ref[...] = gathered
        latent = (mesh_ref[...].astype(F32) + mm(gathered, out_w_ref[...])).astype(BF16)
        latent_ref[...] = latent
        lower = latent[:, latent.shape[1] // 2 :]
        for a, b, ref in ((0, 0, h00), (0, 1, h01), (1, 0, h10), (1, 1, h11)):
            pick = table_by_row(halo_ref[0, a, b : b + 1, :], nodes)
            ref[...] = mm_left(pick, lower).astype(BF16)


def mesh_kernel(
    src_ref, dst_ref, latent_ref, cot_ref, b0, b1, b2, b3, u_src_ref, u_dst_ref, u_out_ref, v_in_ref, v_out_ref,
    g0, g1, g2, g3, coupled_grad_ref, lower_grad_ref, halo_table_ref, ends_ref, summed_ref, coupled_ref, hidden_ref, hidden_grad_ref,
    table, slope_s, total, ends,
):
    nodes = latent_ref.shape[0]
    half = latent_ref.shape[1] // 2
    width = b0.shape[0]
    rows = nodes + 4 * width
    upper = latent_ref[:, :half]
    lower = latent_ref[:, half:]
    halo_table_ref[0:nodes, :] = lower
    for k, ref in enumerate((b0, b1, b2, b3)):
        halo_table_ref[nodes + k * width : nodes + (k + 1) * width, :] = ref[...]
    table[0:rows, :] = mm(halo_table_ref[...], u_src_ref[...]).astype(BF16)
    table[rows : rows + nodes, :] = mm(lower, u_dst_ref[...]).astype(BF16)
    total[...] = jnp.zeros_like(total)
    ends[...] = jnp.zeros_like(ends)
    steps = src_ref.shape[1] // EDGE_TILE

    def forward(i, carry):
        start = pl.multiple_of(i * EDGE_TILE, EDGE_TILE)
        src = src_ref[:, pl.ds(start, EDGE_TILE)]
        dst = dst_ref[:, pl.ds(start, EDGE_TILE)]
        both = jnp.concatenate([table_by_column(src, rows), table_by_column(dst, nodes)], axis=1)
        act, slope = silu_both(mm(both, table[...]))
        slope_s[pl.ds(start, EDGE_TILE), :] = slope.astype(BF16)
        total[...] += mm(table_by_row(dst, nodes), act.astype(BF16))
        return carry

    lax.fori_loop(0, steps, forward, 0)
    summed = total[...].astype(BF16)
    summed_ref[...] = summed
    coupled = (upper.astype(F32) + mm(summed, u_out_ref[...])).astype(BF16)
    coupled_ref[...] = coupled
    act, slope = silu_both(mm(coupled, v_in_ref[...]))
    hidden_ref[...] = act.astype(BF16)
    upper_cot = cot_ref[:, :half]
    lower_cot = cot_ref[:, half:]
    hidden_grad = (mm_right(lower_cot, v_out_ref[...]) * slope).astype(BF16)
    hidden_grad_ref[...] = hidden_grad
    coupled_grad = (upper_cot.astype(F32) + mm_right(hidden_grad, v_in_ref[...])).astype(BF16)
    coupled_grad_ref[...] = coupled_grad
    summed_grad = mm_right(coupled_grad, u_out_ref[...]).astype(BF16)

    def backward(i, carry):
        start = pl.multiple_of(i * EDGE_TILE, EDGE_TILE)
        src = src_ref[:, pl.ds(start, EDGE_TILE)]
        dst = dst_ref[:, pl.ds(start, EDGE_TILE)]
        grad = mm(table_by_column(dst, nodes), summed_grad) * slope_s[pl.ds(start, EDGE_TILE), :].astype(F32)
        both = jnp.concatenate([table_by_row(src, rows), table_by_row(dst, nodes)], axis=0)
        ends[...] += mm(both, grad.astype(BF16))
        return carry

    lax.fori_loop(0, steps, backward, 0)
    ends_ref[...] = ends[...].astype(BF16)
    source_grad = ends_ref[0:rows, :]
    target_grad = ends_ref[rows : rows + nodes, :]
    table_grad = mm_right(source_grad, u_src_ref[...])
    lower_grad_ref[...] = lower_cot.astype(F32) + mm_right(target_grad, u_dst_ref[...]) + table_grad[0:nodes, :]
    for k, ref in enumerate((g0, g1, g2, g3)):
        ref[...] = table_grad[nodes + k * width : nodes + (k + 1) * width, :].astype(BF16)


def mesh_weight_kernel(
    halo_table_ref, ends_ref, summed_ref, coupled_ref, hidden_ref, hidden_grad_ref, coupled_grad_ref, cot_ref,
    u_src_ref, u_dst_ref, u_out_ref, v_in_ref, v_out_ref,
):
    rows = halo_table_ref.shape[0]
    nodes, half = coupled_ref.shape
    u_src_ref[...] = mm_left(halo_table_ref[...], ends_ref[0:rows, :])
    u_dst_ref[...] = mm_left(halo_table_ref[0:nodes, :], ends_ref[rows : rows + nodes, :])
    u_out_ref[...] = mm_left(summed_ref[...], coupled_grad_ref[...])
    v_in_ref[...] = mm_left(coupled_ref[...], hidden_grad_ref[...])
    v_out_ref[...] = mm_left(hidden_ref[...], cot_ref[:, half:])


def encoder_back_kernel(
    src_ref, dst_ref, halo_ref, slope_ref, keep_rows_ref, rim_rows_ref, gathered_ref, mesh_ref,
    coupled_grad_ref, lower_grad_ref, r0, r1, r2, r3, embed_ref, send_ref, recv_ref, out_w_ref,
    keep_grad_ref, g0, g1, g2, g3, mesh_grad_ref, grad_embed_ref, grad_send_ref, grad_recv_ref, grad_out_ref,
    edge_s, latent_s, nodes_s,
):
    nodes = mesh_ref.shape[0]
    keep = keep_rows_ref.shape[1]
    rim = g0.shape[1]
    lower_grad = lower_grad_ref[...]
    for a, b, ref in ((0, 0, r0), (0, 1, r1), (1, 0, r2), (1, 1, r3)):
        lower_grad += mm(table_by_row(halo_ref[0, a, b : b + 1, :], nodes), ref[...])
    half = lower_grad.shape[1]
    latent_s[:, :half] = coupled_grad_ref[...]
    latent_s[:, half:] = lower_grad.astype(BF16)
    latent_grad = latent_s[...]
    grad_out_ref[...] = mm_left(gathered_ref[...], latent_grad)
    gathered_grad = mm_right(latent_grad, out_w_ref[...]).astype(BF16)
    nodes_s[...] = jnp.zeros_like(nodes_s)

    def edges(i, carry):
        start = pl.multiple_of(i * EDGE_TILE, EDGE_TILE)
        dst = dst_ref[:, pl.ds(start, EDGE_TILE)]
        grad = mm(table_by_column(dst, nodes), gathered_grad) * slope_ref[pl.ds(start, EDGE_TILE), :].astype(F32)
        grad = grad.astype(BF16)
        edge_s[pl.ds(start, EDGE_TILE), :] = grad
        nodes_s[...] += mm(table_by_row(dst, nodes), grad)
        return carry

    lax.fori_loop(0, src_ref.shape[1] // EDGE_TILE, edges, 0)
    node_grad = nodes_s[...].astype(BF16)
    grad_recv_ref[...] = mm_left(mesh_ref[...], node_grad)
    mesh_grad_ref[...] = latent_grad.astype(F32) + mm_right(node_grad, recv_ref[...])
    grad_embed_ref[...] = jnp.zeros_like(grad_embed_ref)
    grad_send_ref[...] = jnp.zeros_like(grad_send_ref)

    def back(rows, start, count):
        ids = lax.broadcasted_iota(jnp.int32, (count, src_ref.shape[1]), 0) + start
        table = jnp.where(ids == src_ref[...], 1.0, 0.0).astype(BF16)
        sender_grad = mm(table, edge_s[...]).astype(BF16)
        act, slope = silu_both(mm_left(rows, embed_ref[...]))
        grad_send_ref[...] += mm_left(act.astype(BF16), sender_grad)
        embedded_grad = mm_right(sender_grad, send_ref[...]).astype(BF16)
        embed_grad = (embedded_grad.astype(F32) * slope).astype(BF16)
        grad_embed_ref[...] += mm(rows, embed_grad)
        return mm_right(embed_ref[...], embed_grad).astype(BF16)

    rim_grad = back(rim_rows_ref[...], keep, 4 * rim)
    for k, ref in enumerate((g0, g1, g2, g3)):
        ref[...] = rim_grad[:, k * rim : (k + 1) * rim]

    def kept(i, carry):
        start = pl.multiple_of(i * ROW_TILE, ROW_TILE)
        keep_grad_ref[:, pl.ds(start, ROW_TILE)] = back(keep_rows_ref[:, pl.ds(start, ROW_TILE)], start, ROW_TILE)
        return carry

    lax.fori_loop(0, keep // ROW_TILE, kept, 0)


def place_kernel(flag_ref, order_ref, keep_ref, in0, in1, in2, in3, own0, own1, grid_grad_ref, all_s):
    keep = keep_ref.shape[1]
    rim = in0.shape[1]
    all_s[:, 0:keep] = keep_ref[...]
    all_s[:, keep : keep + rim] = jnp.where(flag_ref[0] > 0, in0[...], own0[...])
    all_s[:, keep + rim : keep + 2 * rim] = jnp.where(flag_ref[1] > 0, in1[...], own1[...])
    all_s[:, keep + 2 * rim : keep + 3 * rim] = in2[...]
    all_s[:, keep + 3 * rim : keep + 4 * rim] = in3[...]

    def place(i, carry):
        start = pl.multiple_of(i * ROW_TILE, ROW_TILE)
        ids = lax.broadcasted_iota(jnp.int32, (ROW_TILE, order_ref.shape[1]), 0) + start
        table = jnp.where(ids == order_ref[...], 1.0, 0.0).astype(BF16)
        grid_grad_ref[:, pl.ds(start, ROW_TILE)] = mm_right(all_s[...], table).astype(BF16)
        return carry

    lax.fori_loop(0, grid_grad_ref.shape[1] // ROW_TILE, place, 0)


def trade(below, above, west, east):
    bands = lax.axis_size("band")
    patches = lax.axis_size("patch")
    up = [(i, i + 1) for i in range(bands - 1)]
    down = [(i + 1, i) for i in range(bands - 1)]
    right = [(i, (i + 1) % patches) for i in range(patches)]
    left = [((i + 1) % patches, i) for i in range(patches)]
    return (
        lax.ppermute(above, "band", up),
        lax.ppermute(below, "band", down),
        lax.ppermute(east, "patch", right),
        lax.ppermute(west, "patch", left),
    )


def body(
    grid_feats, mesh_feats, cotangent, w_embed, w_send, w_recv, w_out, u_src, u_dst, u_out, v_in, v_out,
    send_rows, enc_src, enc_dst, halo_send, mesh_src, mesh_dst,
):
    chans = grid_feats.shape[1]
    grid_rows = grid_feats.shape[0]
    nodes, dim = mesh_feats.shape
    half = dim // 2
    rim = grid_rows // 16
    keep = grid_rows - 4 * rim
    edges = enc_src.shape[1]
    width = halo_send.shape[3]
    table_rows = nodes + 4 * width
    band = lax.axis_index("band")
    flags = jnp.stack([band, lax.axis_size("band") - 1 - band]).astype(jnp.int32)
    smem = pl.BlockSpec(memory_space=pltpu.SMEM)
    vmem = pl.BlockSpec(memory_space=pltpu.VMEM)

    grid_cols = grid_feats.T
    own = call(pick_rim_kernel, [shape((chans, rim), BF16)] * 4)(send_rows, grid_cols)
    arrived = trade(*own)
    keep_rows, keep_sender, node_part = call(
        keep_kernel,
        [shape((chans, keep), BF16), shape((keep, dim), BF16), shape((nodes, dim), BF16)],
    )(send_rows, grid_cols, mesh_feats, w_embed, w_send, w_recv)

    def whole(array):
        dims = array.shape
        return pl.BlockSpec(dims, lambda i: (0,) * len(dims))

    tile = pl.BlockSpec((1, EDGE_TILE), lambda i: (0, i))
    outs = [
        shape((chans, 4 * rim), BF16), shape((edges, dim), BF16), shape((nodes, dim), BF16), shape((nodes, dim), BF16),
    ] + [shape((width, half), BF16)] * 4
    ins = (halo_send, keep_sender, node_part, mesh_feats, w_embed, w_send, w_out, *arrived, own[0], own[1])
    rim_rows, slope, gathered, latent, h00, h01, h10, h11 = call(
        encode_kernel,
        outs,
        grid=(edges // EDGE_TILE,),
        in_specs=[smem, tile, tile] + [whole(x) for x in ins],
        out_specs=[
            whole(outs[0]), pl.BlockSpec((EDGE_TILE, dim), lambda i: (i, 0)),
        ] + [whole(x) for x in outs[2:]],
        scratch_shapes=[pltpu.VMEM((grid_rows + nodes, dim), BF16), pltpu.VMEM((nodes, dim), F32)],
    )(flags, enc_src, enc_dst, *ins)

    halos = trade(h00, h01, h10, h11)
    outs = [shape((width, half), BF16)] * 4 + [
        shape((nodes, half), BF16), shape((nodes, half), F32), shape((table_rows, half), BF16),
        shape((table_rows + nodes, dim), BF16), shape((nodes, dim), BF16), shape((nodes, half), BF16),
        shape((nodes, dim), BF16), shape((nodes, dim), BF16),
    ]
    (g0, g1, g2, g3, coupled_grad, lower_grad, halo_table, ends, summed, coupled, hidden, hidden_grad) = call(
        mesh_kernel,
        outs,
        scratch_shapes=[
            pltpu.VMEM((table_rows + nodes, dim), BF16), pltpu.VMEM((mesh_src.shape[1], dim), BF16),
            pltpu.VMEM((nodes, dim), F32), pltpu.VMEM((table_rows + nodes, dim), F32),
        ],
    )(mesh_src, mesh_dst, latent, cotangent, *halos, u_src, u_dst, u_out, v_in, v_out)
    returned = trade(g0, g1, g2, g3)
    mesh_grads = call(
        mesh_weight_kernel,
        [shape((half, dim), F32), shape((half, dim), F32), shape((dim, half), F32), shape((half, dim), F32), shape((dim, half), F32)],
    )(halo_table, ends, summed, coupled, hidden, hidden_grad, coupled_grad, cotangent)
    mesh_totals = lax.psum(mesh_grads, ("band", "patch"))

    keep_grad, q0, q1, q2, q3, mesh_grad, grad_embed, grad_send, grad_recv, grad_out = call(
        encoder_back_kernel,
        [shape((chans, keep), BF16)] + [shape((chans, rim), BF16)] * 4 + [
            shape((nodes, dim), F32), shape((chans, dim), F32), shape((dim, dim), F32), shape((dim, dim), F32), shape((dim, dim), F32),
        ],
        scratch_shapes=[pltpu.VMEM((edges, dim), BF16), pltpu.VMEM((nodes, dim), BF16), pltpu.VMEM((nodes, dim), F32)],
    )(
        enc_src, enc_dst, halo_send, slope, keep_rows, rim_rows, gathered, mesh_feats, coupled_grad, lower_grad,
        *returned, w_embed, w_send, w_recv, w_out,
    )
    enc_totals = lax.psum((grad_embed, grad_send, grad_recv, grad_out), ("band", "patch"))
    back = trade(q0, q1, q2, q3)
    grid_grad = call(
        place_kernel,
        shape((chans, grid_rows), BF16),
        in_specs=[smem] + [vmem] * 8,
        scratch_shapes=[pltpu.VMEM((chans, grid_rows), BF16)],
    )(flags, send_rows, keep_grad, *back, q0, q1)
    return (grid_grad.T, mesh_grad, *enc_totals, *mesh_totals)


def solution(mesh):
    rows = P(("band", "patch"), None)
    in_specs = (rows,) * 3 + (P(),) * 9 + (rows,) * 3 + (P(("band", "patch"), None, None, None),) + (rows,) * 2
    out_specs = (rows,) * 2 + (P(),) * 9
    return jax.shard_map(body, mesh=mesh, in_specs=in_specs, out_specs=out_specs, check_vma=False)
```

time: 484 us -> 296 us (0.61)
  local copies, waits for them, and re-layouts: 122 us -> 14.9 us
  other arithmetic: 75.2 us -> 0.59 us
  Pallas kernels: 0 us -> 73.9 us
  matrix products: 54.9 us -> 0 us
  waiting for transfers between devices: 172 us -> 146 us
    gather x9 -> x0, local copies, waits for them, and re-layouts: 91.4 us -> none  [the longest x1 20.2 us: encoder_edges(): jnp.take(sender_part, sources, axis=0)]
    pallas_call x0 -> x7, Pallas kernels: none -> 73.9 us  [the longest x1 24 us: body(): call(encoder_back_kernel, [shape((chans, keep), BF16)] + [shape((chans, r...]
    dot_general x30 -> x0, matrix products: 54.9 us -> none  [the longest x12 29.3 us: matmul(): return jnp.dot(left, right, preferred_element_type=jnp.float32)]
    scatter-add x6 -> x0, other arithmetic: 45.8 us -> none  [the longest x1 27.8 us: encoder_back(): sender_grad = jnp.zeros((embedded.shape[0], embedded.shape[1]), jnp.float...]
    convert_element_type x3 -> x0, other arithmetic: 21.9 us -> none  [the longest x1 11.1 us: encoder_back(): enc_edge_grad = jnp.where(active[:, None], jnp.take(gathered_grad, clippe...]
    psum x1, waiting for transfers between devices: 159 us -> 141 us  [body(): lax.psum((grad_embed, grad_send, grad_recv, grad_out), ('band', 'patch'))]
    scatter x1 -> x0, local copies, waits for them, and re-layouts: 11.2 us -> none  [return_rows(): return jnp.zeros(grads.shape, grads.dtype).at[order].set(local)]
    ppermute x16, waiting for transfers between devices: 12.3 us -> 5.28 us  [the longest x4 3.94 us: trade(): lax.ppermute(below, 'band', down)]
  transfers between devices with their start and end apart: 17 -> 17, of which waited for: 8 -> 3; matrix products, arithmetic and copies ran while one was open for 9% -> 0% of each run, Pallas kernels for 0% -> 5%
where the time goes in v1:
time: 296 us
  waiting for transfers between devices  146 us (49%)
  Pallas kernels  73.9 us (25%)
  starting transfers between devices  45.9 us (16%)
  local copies, waits for them, and re-layouts  14.9 us (5%)
  between operations  14.4 us (5%)
    psum x1, waiting for transfers between devices, body(): lax.psum((grad_embed, grad_send, grad_recv, grad_out), ('band', 'patch'))  141 us
    pallas_call x1, Pallas kernels, body(): call(encoder_back_kernel, [shape((chans, keep), BF16)] + [shape((chans, r...  24 us
    pallas_call x1, Pallas kernels, body(): call(encode_kernel, outs, grid=(edges // EDGE_TILE,), in_specs=[smem, til...  19.8 us
    ppermute x4, starting transfers between devices, trade(): lax.ppermute(west, 'patch', left)  18.6 us
    ppermute x4, starting transfers between devices, trade(): lax.ppermute(above, 'band', up)  17.4 us
    unnamed x61, local copies, waits for them, and re-layouts  14.9 us
    pallas_call x1, Pallas kernels, body(): call(mesh_kernel, outs, scratch_shapes=[pltpu.VMEM((table_rows + nodes, d...  11.8 us
    ppermute x4, starting transfers between devices, trade(): lax.ppermute(below, 'band', down)  7.68 us
  transfers between devices with their start and end apart: 17, of which 3 were waited for; matrix products, arithmetic and copies ran while one was open for 0% of the time, Pallas kernels for 5%

profile of v1, /device:TPU:1, one launch (start us, length us, event | category | flops | bytes accessed | tf_op | source)
XLA Modules:
  0.0 295.9 jit_solution(3591751709816439978)
XLA Ops:
  7.2 0.0 all-reduce.3.cloned.1.call-start
  7.2 2.6 shard_map.258
  9.8 2.0 collective-permute-start.2
  11.8 3.7 %collective-permute-start.3 = (bf16[227,128]{1,0:T(8,128)(2,1)}, bf16[227,128]{1,0:T(8,128)(2,1)S(1)}, u32[]{:S(2)}, u32[]{:S(2)}) collective-permute-start(bf16[227,128]{1,0:T(8,128)(2,1)} %get-tuple-element.58), channel_id=1, source_target_pairs={{1,0},{2,1},{3,2},{4,3},{5,4},{6,5},{7,6},{8,7},{9,8},{10,9},{11,1... | collective-permute-start | bytes 174344 | tf_op jit(solution)/shard_map/ppermute | solution.py:298
  15.6 4.5 %collective-permute-start = (bf16[227,128]{1,0:T(8,128)(2,1)}, bf16[227,128]{1,0:T(8,128)(2,1)S(1)}, u32[]{:S(2)}, u32[]{:S(2)}) collective-permute-start(bf16[227,128]{1,0:T(8,128)(2,1)} %get-tuple-element.55.own1), channel_id=1, source_target_pairs={{0,16},{16,32},{32,48},{48,64},{64,80},{80,96},{96,112},{1,17},{17... | collective-permute-start | bytes 174344 | tf_op jit(solution)/shard_map/ppermute | solution.py:295
  20.1 1.9 collective-permute-start.1
  22.0 7.2 %shard_map.257 = (bf16[227,1536]{1,0:T(8,128)(2,1)}, bf16[1536,512]{1,0:T(8,128)(2,1)}, bf16[256,512]{1,0:T(8,128)(2,1)}) custom-call(s32[1,2048]{1,0:T(1,128)} %order_ref.5, bf16[227,2048]{1,0:T(8,128)(2,1)} %bitcast.5, bf16[256,512]{1,0:T(8,128)(2,1)} %mesh_ref.5, bf16[227,512]{1,0:T(8,128)(2,1)} %embed_ref.5, bf16[512,512]{1,0:T(8,128)(2,1)} %send_ref.5, ...), custom_call_target="tpu_custom_call" | custom-call | tf_op jit(solution)/shard_map/pallas_call | solution.py:323
  29.2 0.6 pad_add_fusion.flag_ref
  29.8 0.6 copy-done.12
  30.4 0.0 copy-done.13
  30.4 0.0 copy-done.14
  30.4 0.0 copy-done.15
  30.5 19.8 %shard_map.259 = (bf16[227,512]{1,0:T(8,128)(2,1)}, bf16[4096,512]{1,0:T(8,128)(2,1)}, bf16[256,512]{1,0:T(8,128)(2,1)}, bf16[256,512]{1,0:T(8,128)(2,1)}, bf16[...) custom-call(s32[2]{0:T(128)} %pad_add_fusion.flag_ref, ...), custom_call_target="tpu_custom_call" | custom-call | tf_op jit(solution)/shard_map/pallas_call | solution.py:337
  50.3 3.6 %collective-permute-start.4 = (bf16[32,256]{1,0:T(8,128)(2,1)}, bf16[32,256]{1,0:T(8,128)(2,1)S(1)}, u32[]{:S(2)}, u32[]{:S(2)}) collective-permute-start(bf16[32,256]{1,0:T(8,128)(2,1)} %get-tuple-element.64), channel_id=1, source_target_pairs={{0,16},{16,32},{32,48},{48,64},{64,80},{80,96},{96,112},{1,17},{17... | collective-permute-start | bytes 49160 | tf_op jit(solution)/shard_map/ppermute | solution.py:295
  54.0 1.9 collective-permute-start.5
  55.9 0.1 collective-permute-start.6
  56.0 4.8 %collective-permute-start.7 = (bf16[32,256]{1,0:T(8,128)(2,1)}, bf16[32,256]{1,0:T(8,128)(2,1)S(1)}, u32[]{:S(2)}, u32[]{:S(2)}) collective-permute-start(bf16[32,256]{1,0:T(8,128)(2,1)} %get-tuple-element.67), channel_id=1, source_target_pairs={{1,0},{2,1},{3,2},{4,3},{5,4},{6,5},{7,6},{8,7},{9,8},{10,9},{11,1... | collective-permute-start | bytes 49160 | tf_op jit(solution)/shard_map/ppermute | solution.py:298
  60.8 1.3 collective-permute-done.6.b2
  62.1 0.6 copy-done.22
  62.7 11.8 %shard_map.260 = (bf16[32,256]{1,0:T(8,128)(2,1)}, bf16[32,256]{1,0:T(8,128)(2,1)}, bf16[32,256]{1,0:T(8,128)(2,1)}, bf16[32,256]{1,0:T(8,128)(2,1)}, bf16[256,2...) custom-call(s32[1,2048]{1,0:T(1,128)} %src_ref.4, ...), custom_call_target="tpu_custom_call" | custom-call | tf_op jit(solution)/shard_map/pallas_call | solution.py:354
  74.5 4.8 %collective-permute-start.8 = (bf16[32,256]{1,0:T(8,128)(2,1)}, bf16[32,256]{1,0:T(8,128)(2,1)S(1)}, u32[]{:S(2)}, u32[]{:S(2)}) collective-permute-start(bf16[32,256]{1,0:T(8,128)(2,1)} %get-tuple-element.70), channel_id=1, source_target_pairs={{0,16},{16,32},{32,48},{48,64},{64,80},{80,96},{96,112},{1,17},{17... | collective-permute-start | bytes 49160 | tf_op jit(solution)/shard_map/ppermute | solution.py:295
  79.2 1.9 collective-permute-start.9
  81.2 0.1 collective-permute-start.10
  81.3 5.3 %collective-permute-start.11 = (bf16[32,256]{1,0:T(8,128)(2,1)}, bf16[32,256]{1,0:T(8,128)(2,1)S(1)}, u32[]{:S(2)}, u32[]{:S(2)}) collective-permute-start(bf16[32,256]{1,0:T(8,128)(2,1)} %get-tuple-element.73), channel_id=1, source_target_pairs={{1,0},{2,1},{3,2},{4,3},{5,4},{6,5},{7,6},{8,7},{9,8},{10,9},{11,1... | collective-permute-start | bytes 49160 | tf_op jit(solution)/shard_map/ppermute | solution.py:298
  86.6 3.4 %shard_map.263 = (f32[256,512]{1,0:T(8,128)}, f32[256,512]{1,0:T(8,128)}, f32[512,256]{1,0:T(8,128)}, f32[256,512]{1,0:T(8,128)}, f32[512,256]{1,0:T(8,128)}) custom-call(bf16[384,256]{1,0:T(8,128)(2,1)} %get-tuple-element.84.halo_table_ref, bf16[640,512]{1,0:T(8,128)(2,1)} %get-tuple-element.85.ends_ref, bf16[256,512]{1,0:T(8,128)(2,1)} %get-tuple-element.86.summed_ref, ...), custom_call_target="tpu_custom_call" | custom-call | tf_op jit(solution)/shard_map/pallas_call | solution.py:363
  90.0 0.5 copy-done.16
  90.6 0.0 copy-done.18
  90.6 0.0 copy-done.19
  90.6 24.0 %shard_map.261 = (bf16[227,1536]{1,0:T(8,128)(2,1)}, bf16[227,128]{1,0:T(8,128)(2,1)}, bf16[227,128]{1,0:T(8,128)(2,1)}, bf16[227,128]{1,0:T(8,128)(2,1)}, bf16[...) custom-call(s32[1,4096]{1,0:T(1,128)} %src_ref.5, ...), custom_call_target="tpu_custom_call" | custom-call | tf_op jit(solution)/shard_map/pallas_call | solution.py:369
  114.6 0.0 all-reduce.3.cloned.1.call-update
  114.7 0.8 copy-done.25
  115.4 0.0 copy-done.24
  115.5 4.8 %collective-permute-start.15 = (bf16[227,128]{1,0:T(8,128)(2,1)S(1)}, bf16[227,128]{1,0:T(8,128)(2,1)S(1)}, u32[]{:S(2)}, u32[]{:S(2)}) collective-permute-start(bf16[227,128]{1,0:T(8,128)(2,1)S(1)} %copy-done.24), channel_id=1, source_target_pairs={{1,0},{2,1},{3,2},{4,3},{5,4},{6,5},{7,6},{8,7},{9,8},{10,9},{11,1... | collective-permute-start | bytes 174344 | tf_op jit(solution)/shard_map/ppermute | solution.py:298
  120.2 4.5 %collective-permute-start.12 = (bf16[227,128]{1,0:T(8,128)(2,1)S(1)}, bf16[227,128]{1,0:T(8,128)(2,1)S(1)}, u32[]{:S(2)}, u32[]{:S(2)}) collective-permute-start(bf16[227,128]{1,0:T(8,128)(2,1)S(1)} %copy-done.7), channel_id=1, source_target_pairs={{0,16},{16,32},{32,48},{48,64},{64,80},{80,96},{96,112},{1,17},{17... | collective-permute-start | bytes 174344 | tf_op jit(solution)/shard_map/ppermute | solution.py:295
  124.7 1.9 collective-permute-start.13
  126.7 3.9 %collective-permute-done.13.in1 = bf16[227,128]{1,0:T(8,128)(2,1)S(1)} collective-permute-done((bf16[227,128]{1,0:T(8,128)(2,1)S(1)}, bf16[227,128]{1,0:T(8,128)(2,1)S(1)}, u32[]{:S(2)}, u32[]{:S(2)}) %collective-permute-start.13) | collective-permute-done | bytes 58144 | tf_op jit(solution)/shard_map/ppermute | solution.py:296
  130.6 0.6 copy-done.11
  131.2 5.2 %shard_map.262 = bf16[227,2048]{1,0:T(8,128)(2,1)} custom-call(s32[2]{0:T(128)} %pad_add_fusion.flag_ref, s32[1,2048]{1,0:T(1,128)} %order_ref.5, bf16[227,1536]{1,0:T(8,128)(2,1)} %get-tuple-element.74.keep_ref, bf16[227,128]{1,0:T(8,128)(2,1)} %copy-done.10, bf16[227,128]{1,0:T(8,128)(2,1)} %copy-done.11, bf16[227,128]{1,0:T(8,128)(2,1)} %copy-done.8, ...), custom_call_target="tpu_custom_call" | custom-call | tf_op jit(solution)/shard_map/pallas_call | solution.py:381
  136.4 141.0 %all-reduce.3.cloned.1.call-done = (f32[227,512]{1,0:T(8,128)}, f32[512,512]{1,0:T(8,128)}, f32[512,512]{1,0:T(8,128)}, f32[512,512]{1,0:T(8,128)}, f32[256,512]...) async-done(((f32[227,512]{1,0:T(8,128)}, f32[512,512]{1,0:T(8,128)}, f32[512,512]{1,0:T(8,128)}, ...) | async-done | bytes 6232080 | tf_op jit(solution)/shard_map/psum | solution.py:379
  277.4 2.0 copy.38
  279.4 2.3 copy.39
  281.7 2.4 copy.40
  284.1 1.0 copy.41
  285.0 0.8 copy.42
  285.8 0.8 copy.43
  286.6 0.8 copy.44
  287.4 0.8 copy.45
  288.2 0.8 copy.46
  (56 shorter events, 0.1 us)
Async XLA Ops:
  7.2 270.2 %all-reduce.3.cloned.1.call-start = ((), (), s32[]{:S(2)}) async-start(), calls=%async_computation | async-start | bytes 12484608 | tf_op jit(solution)/shard_map/psum | solution.py:379
  9.8 20.0 %collective-permute-start.2 = (bf16[227,128]{1,0:T(8,128)(2,1)}, bf16[227,128]{1,0:T(8,128)(2,1)S(1)}, u32[]{:S(2)}, u32[]{:S(2)}) collective-permute-start(bf16[227,128]{1,0:T(8,128)(2,1)} %get-tuple-element.57), channel_id=1, source_target_pairs={{0,1},{1,2},{2,3},{3,4},{4,5},{5,6},{6,7},{7,8},{8,9},{9,10},{10,1... | collective-permute-start | bytes 174344 | tf_op jit(solution)/shard_map/ppermute | solution.py:297
  11.8 17.9 %collective-permute-start.3 = (bf16[227,128]{1,0:T(8,128)(2,1)}, bf16[227,128]{1,0:T(8,128)(2,1)S(1)}, u32[]{:S(2)}, u32[]{:S(2)}) collective-permute-start(bf16[227,128]{1,0:T(8,128)(2,1)} %get-tuple-element.58), channel_id=1, source_target_pairs={{1,0},{2,1},{3,2},{4,3},{5,4},{6,5},{7,6},{8,7},{9,8},{10,9},{11,1... | collective-permute-start | bytes 174344 | tf_op jit(solution)/shard_map/ppermute | solution.py:298
  15.6 14.2 %collective-permute-start = (bf16[227,128]{1,0:T(8,128)(2,1)}, bf16[227,128]{1,0:T(8,128)(2,1)S(1)}, u32[]{:S(2)}, u32[]{:S(2)}) collective-permute-start(bf16[227,128]{1,0:T(8,128)(2,1)} %get-tuple-element.55.own1), channel_id=1, source_target_pairs={{0,16},{16,32},{32,48},{48,64},{64,80},{80,96},{96,112},{1,17},{17... | collective-permute-start | bytes 174344 | tf_op jit(solution)/shard_map/ppermute | solution.py:295
  20.1 9.7 %collective-permute-start.1 = (bf16[227,128]{1,0:T(8,128)(2,1)}, bf16[227,128]{1,0:T(8,128)(2,1)S(1)}, u32[]{:S(2)}, u32[]{:S(2)}) collective-permute-start(bf16[227,128]{1,0:T(8,128)(2,1)} %get-tuple-element.56.own0), channel_id=1, source_target_pairs={{16,0},{32,16},{48,32},{64,48},{80,64},{96,80},{112,96},{17,1},{33... | collective-permute-start | bytes 174344 | tf_op jit(solution)/shard_map/ppermute | solution.py:296
  29.8 0.6 copy-start.12
  29.8 0.6 copy-start.13
  29.8 0.6 copy-start.14
  29.8 0.6 copy-start.15
  50.3 10.4 %collective-permute-start.4 = (bf16[32,256]{1,0:T(8,128)(2,1)}, bf16[32,256]{1,0:T(8,128)(2,1)S(1)}, u32[]{:S(2)}, u32[]{:S(2)}) collective-permute-start(bf16[32,256]{1,0:T(8,128)(2,1)} %get-tuple-element.64), channel_id=1, source_target_pairs={{0,16},{16,32},{32,48},{48,64},{64,80},{80,96},{96,112},{1,17},{17... | collective-permute-start | bytes 49160 | tf_op jit(solution)/shard_map/ppermute | solution.py:295
  54.0 6.8 %collective-permute-start.5 = (bf16[32,256]{1,0:T(8,128)(2,1)}, bf16[32,256]{1,0:T(8,128)(2,1)S(1)}, u32[]{:S(2)}, u32[]{:S(2)}) collective-permute-start(bf16[32,256]{1,0:T(8,128)(2,1)} %get-tuple-element.65), channel_id=1, source_target_pairs={{16,0},{32,16},{48,32},{64,48},{80,64},{96,80},{112,96},{17,1},{33... | collective-permute-start | bytes 49160 | tf_op jit(solution)/shard_map/ppermute | solution.py:296
  55.9 6.2 %collective-permute-start.6 = (bf16[32,256]{1,0:T(8,128)(2,1)}, bf16[32,256]{1,0:T(8,128)(2,1)S(1)}, u32[]{:S(2)}, u32[]{:S(2)}) collective-permute-start(bf16[32,256]{1,0:T(8,128)(2,1)} %get-tuple-element.66), channel_id=1, source_target_pairs={{0,1},{1,2},{2,3},{3,4},{4,5},{5,6},{6,7},{7,8},{8,9},{9,10},{10,1... | collective-permute-start | bytes 49160 | tf_op jit(solution)/shard_map/ppermute | solution.py:297
  56.0 6.1 %collective-permute-start.7 = (bf16[32,256]{1,0:T(8,128)(2,1)}, bf16[32,256]{1,0:T(8,128)(2,1)S(1)}, u32[]{:S(2)}, u32[]{:S(2)}) collective-permute-start(bf16[32,256]{1,0:T(8,128)(2,1)} %get-tuple-element.67), channel_id=1, source_target_pairs={{1,0},{2,1},{3,2},{4,3},{5,4},{6,5},{7,6},{8,7},{9,8},{10,9},{11,1... | collective-permute-start | bytes 49160 | tf_op jit(solution)/shard_map/ppermute | solution.py:298
  60.8 1.3 copy-start.20
  60.8 1.3 copy-start.21
  62.1 0.6 copy-start.22
  62.1 0.6 copy-start.23
  74.5 15.5 %collective-permute-start.8 = (bf16[32,256]{1,0:T(8,128)(2,1)}, bf16[32,256]{1,0:T(8,128)(2,1)S(1)}, u32[]{:S(2)}, u32[]{:S(2)}) collective-permute-start(bf16[32,256]{1,0:T(8,128)(2,1)} %get-tuple-element.70), channel_id=1, source_target_pairs={{0,16},{16,32},{32,48},{48,64},{64,80},{80,96},{96,112},{1,17},{17... | collective-permute-start | bytes 49160 | tf_op jit(solution)/shard_map/ppermute | solution.py:295
  79.2 10.7 %collective-permute-start.9 = (bf16[32,256]{1,0:T(8,128)(2,1)}, bf16[32,256]{1,0:T(8,128)(2,1)S(1)}, u32[]{:S(2)}, u32[]{:S(2)}) collective-permute-start(bf16[32,256]{1,0:T(8,128)(2,1)} %get-tuple-element.71), channel_id=1, source_target_pairs={{16,0},{32,16},{48,32},{64,48},{80,64},{96,80},{112,96},{17,1},{33... | collective-permute-start | bytes 49160 | tf_op jit(solution)/shard_map/ppermute | solution.py:296
  81.2 8.8 %collective-permute-start.10 = (bf16[32,256]{1,0:T(8,128)(2,1)}, bf16[32,256]{1,0:T(8,128)(2,1)S(1)}, u32[]{:S(2)}, u32[]{:S(2)}) collective-permute-start(bf16[32,256]{1,0:T(8,128)(2,1)} %get-tuple-element.72), channel_id=1, source_target_pairs={{0,1},{1,2},{2,3},{3,4},{4,5},{5,6},{6,7},{7,8},{8,9},{9,10},{10,1... | collective-permute-start | bytes 49160 | tf_op jit(solution)/shard_map/ppermute | solution.py:297
  81.3 8.8 %collective-permute-start.11 = (bf16[32,256]{1,0:T(8,128)(2,1)}, bf16[32,256]{1,0:T(8,128)(2,1)S(1)}, u32[]{:S(2)}, u32[]{:S(2)}) collective-permute-start(bf16[32,256]{1,0:T(8,128)(2,1)} %get-tuple-element.73), channel_id=1, source_target_pairs={{1,0},{2,1},{3,2},{4,3},{5,4},{6,5},{7,6},{8,7},{9,8},{10,9},{11,1... | collective-permute-start | bytes 49160 | tf_op jit(solution)/shard_map/ppermute | solution.py:298
  90.0 0.6 copy-start.16
  90.0 0.6 copy-start.17
  90.0 0.6 copy-start.18
  90.0 0.6 copy-start.19
  114.6 0.8 copy-start.25
  114.6 0.8 copy-start.24
  114.6 5.6 %copy-start.7 = (bf16[227,128]{1,0:T(8,128)(2,1)S(1)}, bf16[227,128]{1,0:T(8,128)(2,1)}, u32[]{:S(2)}) copy-start(bf16[227,128]{1,0:T(8,128)(2,1)} %get-tuple-element.75.own1) | copy-start | bytes 174340
  114.6 10.1 %copy-start.6 = (bf16[227,128]{1,0:T(8,128)(2,1)S(1)}, bf16[227,128]{1,0:T(8,128)(2,1)}, u32[]{:S(2)}) copy-start(bf16[227,128]{1,0:T(8,128)(2,1)} %get-tuple-element.76.own0) | copy-start | bytes 174340
  115.4 11.2 %collective-permute-start.14 = (bf16[227,128]{1,0:T(8,128)(2,1)S(1)}, bf16[227,128]{1,0:T(8,128)(2,1)S(1)}, u32[]{:S(2)}, u32[]{:S(2)}) collective-permute-start(bf16[227,128]{1,0:T(8,128)(2,1)S(1)} %copy-done.25), channel_id=1, source_target_pairs={{0,1},{1,2},{2,3},{3,4},{4,5},{5,6},{6,7},{7,8},{8,9},{9,10},{10,1... | collective-permute-start | bytes 174344 | tf_op jit(solution)/shard_map/ppermute | solution.py:297
  115.5 11.2 %collective-permute-start.15 = (bf16[227,128]{1,0:T(8,128)(2,1)S(1)}, bf16[227,128]{1,0:T(8,128)(2,1)S(1)}, u32[]{:S(2)}, u32[]{:S(2)}) collective-permute-start(bf16[227,128]{1,0:T(8,128)(2,1)S(1)} %copy-done.24), channel_id=1, source_target_pairs={{1,0},{2,1},{3,2},{4,3},{5,4},{6,5},{7,6},{8,7},{9,8},{10,9},{11,1... | collective-permute-start | bytes 174344 | tf_op jit(solution)/shard_map/ppermute | solution.py:298
  120.2 6.4 %collective-permute-start.12 = (bf16[227,128]{1,0:T(8,128)(2,1)S(1)}, bf16[227,128]{1,0:T(8,128)(2,1)S(1)}, u32[]{:S(2)}, u32[]{:S(2)}) collective-permute-start(bf16[227,128]{1,0:T(8,128)(2,1)S(1)} %copy-done.7), channel_id=1, source_target_pairs={{0,16},{16,32},{32,48},{48,64},{64,80},{80,96},{96,112},{1,17},{17... | collective-permute-start | bytes 174344 | tf_op jit(solution)/shard_map/ppermute | solution.py:295
  124.7 5.9 %collective-permute-start.13 = (bf16[227,128]{1,0:T(8,128)(2,1)S(1)}, bf16[227,128]{1,0:T(8,128)(2,1)S(1)}, u32[]{:S(2)}, u32[]{:S(2)}) collective-permute-start(bf16[227,128]{1,0:T(8,128)(2,1)S(1)} %copy-done.6), channel_id=1, source_target_pairs={{16,0},{32,16},{48,32},{64,48},{80,64},{96,80},{112,96},{17,1},{33... | collective-permute-start | bytes 174344 | tf_op jit(solution)/shard_map/ppermute | solution.py:296
  126.6 4.0 %copy-start.8 = (bf16[227,128]{1,0:T(8,128)(2,1)}, bf16[227,128]{1,0:T(8,128)(2,1)S(1)}, u32[]{:S(2)}) copy-start(bf16[227,128]{1,0:T(8,128)(2,1)S(1)} %collective-permute-done.14.in2) | copy-start | bytes 174340
  126.7 4.0 %copy-start.9 = (bf16[227,128]{1,0:T(8,128)(2,1)}, bf16[227,128]{1,0:T(8,128)(2,1)S(1)}, u32[]{:S(2)}) copy-start(bf16[227,128]{1,0:T(8,128)(2,1)S(1)} %collective-permute-done.15.in3) | copy-start | bytes 174340
  126.7 3.9 %copy-start.10 = (bf16[227,128]{1,0:T(8,128)(2,1)}, bf16[227,128]{1,0:T(8,128)(2,1)S(1)}, u32[]{:S(2)}) copy-start(bf16[227,128]{1,0:T(8,128)(2,1)S(1)} %collective-permute-done.12.in0) | copy-start | bytes 174340
  130.6 0.6 copy-start.11
  277.4 6.7 %copy-start = (f32[512,512]{1,0:T(8,128)S(1)}, f32[512,512]{1,0:T(8,128)}, u32[]{:S(2)}) copy-start(f32[512,512]{1,0:T(8,128)} %get-tuple-element.109) | copy-start | bytes 3145732
  277.4 7.6 %copy-start.5 = (f32[256,512]{1,0:T(8,128)S(1)}, f32[256,512]{1,0:T(8,128)}, u32[]{:S(2)}) copy-start(f32[256,512]{1,0:T(8,128)} %get-tuple-element.110) | copy-start | bytes 1572868
  277.4 8.4 %copy-start.4 = (f32[256,512]{1,0:T(8,128)S(1)}, f32[256,512]{1,0:T(8,128)}, u32[]{:S(2)}) copy-start(f32[256,512]{1,0:T(8,128)} %get-tuple-element.111) | copy-start | bytes 1572868
  279.4 7.2 %copy-start.3 = (f32[512,256]{1,0:T(8,128)S(1)}, f32[512,256]{1,0:T(8,128)}, u32[]{:S(2)}) copy-start(f32[512,256]{1,0:T(8,128)} %get-tuple-element.112) | copy-start | bytes 1572868
  281.7 5.7 %copy-start.2 = (f32[256,512]{1,0:T(8,128)S(1)}, f32[256,512]{1,0:T(8,128)}, u32[]{:S(2)}) copy-start(f32[256,512]{1,0:T(8,128)} %get-tuple-element.113) | copy-start | bytes 1572868
  281.7 6.5 %copy-start.1 = (f32[512,256]{1,0:T(8,128)S(1)}, f32[512,256]{1,0:T(8,128)}, u32[]{:S(2)}) copy-start(f32[512,256]{1,0:T(8,128)} %get-tuple-element.114) | copy-start | bytes 1572868
Sparse Core Ops, SparseCore 0:
  114.8 162.5 all-reduce.2

commit v2 on v1

--- a/solution.py
+++ b/solution.py
@@ -1,8 +1,11 @@
+import functools
+
 import jax
 import jax.numpy as jnp
 from jax import lax
 from jax.experimental import pallas as pl
 from jax.experimental.pallas import tpu as pltpu
+from jax.sharding import Mesh
 from jax.sharding import PartitionSpec as P
 
 BF16 = jnp.bfloat16
@@ -11,6 +14,9 @@
 EDGE_TILE = 512
 ROW_TILE = 512
 VMEM_LIMIT = 56 * 1024 * 1024
+BAND = ("z", "core")
+PATCH = ("y", "x")
+CHIPS = ("z", "y", "x")
 
 
 def mm(left, right):
@@ -193,24 +199,56 @@
         ref[...] = table_grad[nodes + k * width : nodes + (k + 1) * width, :].astype(BF16)
 
 
+def store_halves(core_ref, mine_ref, other_ref, start, value):
+    half = mine_ref.shape[0]
+    value = value.astype(BF16)
+    done = 0
+    while done < value.shape[0]:
+        row = start + done
+        count = min(value.shape[0] - done, half - row % half)
+        piece = value[done : done + count, :]
+        here = row % half
+
+        @pl.when(core_ref[0] == row // half)
+        def _(piece=piece, here=here, count=count):
+            mine_ref[here : here + count, :] = piece
+
+        @pl.when(core_ref[0] != row // half)
+        def _(piece=piece, here=here, count=count):
+            other_ref[here : here + count, :] = piece
+
+        done += count
+
+
+def side_by_side(value):
+    rows = value.shape[0] // 2
+    return jnp.concatenate([value[:rows, :], value[rows:, :]], axis=1)
+
+
 def mesh_weight_kernel(
-    halo_table_ref, ends_ref, summed_ref, coupled_ref, hidden_ref, hidden_grad_ref, coupled_grad_ref, cot_ref,
-    u_src_ref, u_dst_ref, u_out_ref, v_in_ref, v_out_ref,
+    core_ref, halo_table_ref, ends_ref, summed_ref, coupled_ref, hidden_ref, hidden_grad_ref, coupled_grad_ref, cot_ref,
+    mine_ref, other_ref,
 ):
     rows = halo_table_ref.shape[0]
     nodes, half = coupled_ref.shape
-    u_src_ref[...] = mm_left(halo_table_ref[...], ends_ref[0:rows, :])
-    u_dst_ref[...] = mm_left(halo_table_ref[0:nodes, :], ends_ref[rows : rows + nodes, :])
-    u_out_ref[...] = mm_left(summed_ref[...], coupled_grad_ref[...])
-    v_in_ref[...] = mm_left(coupled_ref[...], hidden_grad_ref[...])
-    v_out_ref[...] = mm_left(hidden_ref[...], cot_ref[:, half:])
+    parts = (
+        mm_left(halo_table_ref[...], ends_ref[0:rows, :]),
+        mm_left(halo_table_ref[0:nodes, :], ends_ref[rows : rows + nodes, :]),
+        side_by_side(mm_left(summed_ref[...], coupled_grad_ref[...])),
+        mm_left(coupled_ref[...], hidden_grad_ref[...]),
+        side_by_side(mm_left(hidden_ref[...], cot_ref[:, half:])),
+    )
+    start = 0
+    for part in parts:
+        store_halves(core_ref, mine_ref, other_ref, start, part)
+        start += part.shape[0]
 
 
 def encoder_back_kernel(
-    src_ref, dst_ref, halo_ref, slope_ref, keep_rows_ref, rim_rows_ref, gathered_ref, mesh_ref,
+    core_ref, src_ref, dst_ref, halo_ref, slope_ref, keep_rows_ref, rim_rows_ref, gathered_ref, mesh_ref,
     coupled_grad_ref, lower_grad_ref, r0, r1, r2, r3, embed_ref, send_ref, recv_ref, out_w_ref,
-    keep_grad_ref, g0, g1, g2, g3, mesh_grad_ref, grad_embed_ref, grad_send_ref, grad_recv_ref, grad_out_ref,
-    edge_s, latent_s, nodes_s,
+    keep_grad_ref, g0, g1, g2, g3, mesh_grad_ref, mine_ref, other_ref,
+    grad_embed_ref, grad_send_ref, edge_s, latent_s, nodes_s,
 ):
     nodes = mesh_ref.shape[0]
     keep = keep_rows_ref.shape[1]
@@ -222,7 +260,8 @@
     latent_s[:, :half] = coupled_grad_ref[...]
     latent_s[:, half:] = lower_grad.astype(BF16)
     latent_grad = latent_s[...]
-    grad_out_ref[...] = mm_left(gathered_ref[...], latent_grad)
+    dim = latent_grad.shape[1]
+    store_halves(core_ref, mine_ref, other_ref, 0, mm_left(gathered_ref[...], latent_grad))
     gathered_grad = mm_right(latent_grad, out_w_ref[...]).astype(BF16)
     nodes_s[...] = jnp.zeros_like(nodes_s)
 
@@ -237,7 +276,7 @@
 
     lax.fori_loop(0, src_ref.shape[1] // EDGE_TILE, edges, 0)
     node_grad = nodes_s[...].astype(BF16)
-    grad_recv_ref[...] = mm_left(mesh_ref[...], node_grad)
+    store_halves(core_ref, mine_ref, other_ref, dim, mm_left(mesh_ref[...], node_grad))
     mesh_grad_ref[...] = latent_grad.astype(F32) + mm_right(node_grad, recv_ref[...])
     grad_embed_ref[...] = jnp.zeros_like(grad_embed_ref)
     grad_send_ref[...] = jnp.zeros_like(grad_send_ref)
@@ -250,7 +289,7 @@
         grad_send_ref[...] += mm_left(act.astype(BF16), sender_grad)
         embedded_grad = mm_right(sender_grad, send_ref[...]).astype(BF16)
         embed_grad = (embedded_grad.astype(F32) * slope).astype(BF16)
-        grad_embed_ref[...] += mm(rows, embed_grad)
+        grad_embed_ref[0 : rows.shape[0], :] += mm(rows, embed_grad)
         return mm_right(embed_ref[...], embed_grad).astype(BF16)
 
     rim_grad = back(rim_rows_ref[...], keep, 4 * rim)
@@ -263,6 +302,8 @@
         return carry
 
     lax.fori_loop(0, keep // ROW_TILE, kept, 0)
+    store_halves(core_ref, mine_ref, other_ref, 2 * dim, grad_send_ref[...])
+    store_halves(core_ref, mine_ref, other_ref, 3 * dim, grad_embed_ref[...])
 
 
 def place_kernel(flag_ref, order_ref, keep_ref, in0, in1, in2, in3, own0, own1, grid_grad_ref, all_s):
@@ -284,19 +325,69 @@
     lax.fori_loop(0, grid_grad_ref.shape[1] // ROW_TILE, place, 0)
 
 
+def add_kernel(a_mine, a_in, b_mine, b_in, sum_ref):
+    count = a_mine.shape[0]
+    sum_ref[0:count, :] = (a_mine[...].astype(F32) + a_in[...].astype(F32)).astype(BF16)
+    sum_ref[count:, :] = (b_mine[...].astype(F32) + b_in[...].astype(F32)).astype(BF16)
+
+
+def total_kernel(parts_ref, out_ref):
+    total = parts_ref[0].astype(F32)
+    for k in range(1, parts_ref.shape[0]):
+        total += parts_ref[k].astype(F32)
+    total = total.astype(BF16)
+    for k in range(parts_ref.shape[0]):
+        out_ref[k] = total
+
+
+def unpack_kernel(a_rows, core_ref, mine_ref, other_ref, embed_ref, send_ref, recv_ref, out_ref, u_src_ref, u_dst_ref, u_out_ref, v_in_ref, v_out_ref):
+    first = core_ref[0] == 0
+
+    def read(base, half, start, count):
+        pieces = []
+        while count > 0:
+            here = start % half
+            some = min(count, half - here)
+            mine = mine_ref[base + here : base + here + some, :]
+            other = other_ref[base + here : base + here + some, :]
+            pieces.append(jnp.where(first == (start < half), mine, other))
+            start += some
+            count -= some
+        value = pieces[0] if len(pieces) == 1 else jnp.concatenate(pieces, axis=0)
+        return value.astype(F32)
+
+    dim, half = v_out_ref.shape
+    a_half = a_rows // 2
+    b_half = mine_ref.shape[0] - a_half
+    for start, ref in ((0, u_src_ref), (half, u_dst_ref), (3 * half, v_in_ref)):
+        ref[...] = read(0, a_half, start, half)
+    for start, ref in ((2 * half, u_out_ref), (4 * half, v_out_ref)):
+        value = read(0, a_half, start, half)
+        ref[0:half, :] = value[:, :half]
+        ref[half:, :] = value[:, half:]
+    for start, ref in ((0, out_ref), (dim, recv_ref), (2 * dim, send_ref)):
+        ref[...] = read(a_half, b_half, start, dim)
+    ref = embed_ref
+    ref[...] = read(a_half, b_half, 3 * dim, half)[0 : ref.shape[0], :]
+
+
 def trade(below, above, west, east):
-    bands = lax.axis_size("band")
-    patches = lax.axis_size("patch")
+    bands = lax.axis_size(BAND)
+    patches = lax.axis_size(PATCH)
     up = [(i, i + 1) for i in range(bands - 1)]
     down = [(i + 1, i) for i in range(bands - 1)]
     right = [(i, (i + 1) % patches) for i in range(patches)]
     left = [((i + 1) % patches, i) for i in range(patches)]
     return (
-        lax.ppermute(above, "band", up),
-        lax.ppermute(below, "band", down),
-        lax.ppermute(east, "patch", right),
-        lax.ppermute(west, "patch", left),
+        lax.ppermute(above, BAND, up),
+        lax.ppermute(below, BAND, down),
+        lax.ppermute(east, PATCH, right),
+        lax.ppermute(west, PATCH, left),
     )
+
+
+def swap_cores(value):
+    return lax.ppermute(value, "core", [(0, 1), (1, 0)])
 
 
 def body(
@@ -312,8 +403,9 @@
     edges = enc_src.shape[1]
     width = halo_send.shape[3]
     table_rows = nodes + 4 * width
-    band = lax.axis_index("band")
-    flags = jnp.stack([band, lax.axis_size("band") - 1 - band]).astype(jnp.int32)
+    band = lax.axis_index(BAND)
+    flags = jnp.stack([band, lax.axis_size(BAND) - 1 - band]).astype(jnp.int32)
+    core = lax.axis_index("core").astype(jnp.int32).reshape(1)
     smem = pl.BlockSpec(memory_space=pltpu.SMEM)
     vmem = pl.BlockSpec(memory_space=pltpu.VMEM)
 
@@ -360,23 +452,27 @@
         ],
     )(mesh_src, mesh_dst, latent, cotangent, *halos, u_src, u_dst, u_out, v_in, v_out)
     returned = trade(g0, g1, g2, g3)
-    mesh_grads = call(
-        mesh_weight_kernel,
-        [shape((half, dim), F32), shape((half, dim), F32), shape((dim, half), F32), shape((half, dim), F32), shape((dim, half), F32)],
-    )(halo_table, ends, summed, coupled, hidden, hidden_grad, coupled_grad, cotangent)
-    mesh_totals = lax.psum(mesh_grads, ("band", "patch"))
-
-    keep_grad, q0, q1, q2, q3, mesh_grad, grad_embed, grad_send, grad_recv, grad_out = call(
+    a_rows = 5 * half
+    a_mine, a_other = call(
+        mesh_weight_kernel, [shape((a_rows // 2, dim), BF16)] * 2, in_specs=[smem] + [vmem] * 8,
+    )(core, halo_table, ends, summed, coupled, hidden, hidden_grad, coupled_grad, cotangent)
+    a_in = swap_cores(a_other)
+
+    b_rows = 3 * dim + half
+    keep_grad, q0, q1, q2, q3, mesh_grad, b_mine, b_other = call(
         encoder_back_kernel,
-        [shape((chans, keep), BF16)] + [shape((chans, rim), BF16)] * 4 + [
-            shape((nodes, dim), F32), shape((chans, dim), F32), shape((dim, dim), F32), shape((dim, dim), F32), shape((dim, dim), F32),
+        [shape((chans, keep), BF16)] + [shape((chans, rim), BF16)] * 4 + [shape((nodes, dim), F32)]
+        + [shape((b_rows // 2, dim), BF16)] * 2,
+        in_specs=[smem] + [vmem] * 18,
+        scratch_shapes=[
+            pltpu.VMEM((half, dim), F32), pltpu.VMEM((dim, dim), F32),
+            pltpu.VMEM((edges, dim), BF16), pltpu.VMEM((nodes, dim), BF16), pltpu.VMEM((nodes, dim), F32),
         ],
-        scratch_shapes=[pltpu.VMEM((edges, dim), BF16), pltpu.VMEM((nodes, dim), BF16), pltpu.VMEM((nodes, dim), F32)],
     )(
-        enc_src, enc_dst, halo_send, slope, keep_rows, rim_rows, gathered, mesh_feats, coupled_grad, lower_grad,
+        core, enc_src, enc_dst, halo_send, slope, keep_rows, rim_rows, gathered, mesh_feats, coupled_grad, lower_grad,
         *returned, w_embed, w_send, w_recv, w_out,
     )
-    enc_totals = lax.psum((grad_embed, grad_send, grad_recv, grad_out), ("band", "patch"))
+    b_in = swap_cores(b_other)
     back = trade(q0, q1, q2, q3)
     grid_grad = call(
         place_kernel,
@@ -384,11 +480,26 @@
         in_specs=[smem] + [vmem] * 8,
         scratch_shapes=[pltpu.VMEM((chans, grid_rows), BF16)],
     )(flags, send_rows, keep_grad, *back, q0, q1)
-    return (grid_grad.T, mesh_grad, *enc_totals, *mesh_totals)
+    chips = lax.axis_size(CHIPS)
+    packed = (a_rows + b_rows) // 2
+    pair = call(add_kernel, shape((packed, dim), BF16))(a_mine, a_in, b_mine, b_in)
+    parts = lax.all_to_all(pair.reshape(chips, packed // chips, dim), CHIPS, 0, 0)
+    parts = call(total_kernel, shape(parts.shape, BF16))(parts)
+    mine = lax.all_to_all(parts, CHIPS, 0, 0).reshape(packed, dim)
+    other = swap_cores(mine)
+    totals = call(
+        functools.partial(unpack_kernel, a_rows),
+        [shape((chans, dim), F32)] + [shape((dim, dim), F32)] * 3 + [shape((half, dim), F32)] * 2
+        + [shape((dim, half), F32), shape((half, dim), F32), shape((dim, half), F32)],
+        in_specs=[smem] + [vmem] * 2,
+    )(core, mine, other)
+    return (grid_grad.T, mesh_grad, *totals)
 
 
 def solution(mesh):
-    rows = P(("band", "patch"), None)
-    in_specs = (rows,) * 3 + (P(),) * 9 + (rows,) * 3 + (P(("band", "patch"), None, None, None),) + (rows,) * 2
+    chips = Mesh(mesh.devices.reshape(mesh.shape["band"] // 2, 2, 4, mesh.shape["patch"] // 4), ("z", "core", "y", "x"))
+    everywhere = BAND + PATCH
+    rows = P(everywhere, None)
+    in_specs = (rows,) * 3 + (P(),) * 9 + (rows,) * 3 + (P(everywhere, None, None, None),) + (rows,) * 2
     out_specs = (rows,) * 2 + (P(),) * 9
-    return jax.shard_map(body, mesh=mesh, in_specs=in_specs, out_specs=out_specs, check_vma=False)
+    return jax.shard_map(body, mesh=chips, in_specs=in_specs, out_specs=out_specs, check_vma=False)

time: 296 us -> 209 us (0.71)
  waiting for transfers between devices: 146 us -> 8.74 us
  blocking collectives: 0 us -> 59.7 us
  between operations: 14.4 us -> 0.94 us
  Pallas kernels: 73.9 us -> 86.2 us
  local copies, waits for them, and re-layouts: 14.9 us -> 4.76 us
    psum x1 -> x0, waiting for transfers between devices: 141 us -> none  [body(): lax.psum((grad_embed, grad_send, grad_recv, grad_out), ('band', 'patch'))]
    all_to_all x0 -> x2, blocking collectives: none -> 59.7 us  [the longest x1 30.6 us: body(): lax.all_to_all(pair.reshape(chips, packed // chips, dim), CHIPS, 0, 0)]
    pallas_call x1 -> x4, Pallas kernels: 3.39 us -> 14.2 us  [the longest x1 4.58 us: body(): call(functools.partial(unpack_kernel, a_rows), [shape((chans, dim), F32)]...]
    unnamed x61 -> x48, local copies, waits for them, and re-layouts: 14.9 us -> 4.76 us
    ppermute x16 -> x19, waiting for transfers between devices: 5.28 us -> 8.74 us  [the longest x4 3.49 us: trade(): lax.ppermute(east, PATCH, right)]
    ppermute x16 -> x19, starting transfers between devices: 45.8 us -> 47 us  [the longest x4 17.9 us: trade(): lax.ppermute(west, PATCH, left)]
  transfers between devices with their start and end apart: 17 -> 19, of which waited for: 3 -> 4; matrix products, arithmetic and copies ran while one was open for 0% -> 0% of each run, Pallas kernels for 5% -> 8%
where the time goes in v2:
time: 209 us; the launch traced here: 208 us
  Pallas kernels  86.2 us (41%)
  blocking collectives  59.7 us (29%)
  starting transfers between devices  47 us (22%)
  waiting for transfers between devices  8.74 us (4%)
  local copies, waits for them, and re-layouts  4.76 us (2%)
    all_to_all x1, blocking collectives, body(): lax.all_to_all(pair.reshape(chips, packed // chips, dim), CHIPS, 0, 0)  30.6 us
    all_to_all x1, blocking collectives, body(): mine = lax.all_to_all(parts, CHIPS, 0, 0).reshape(packed, dim)  29.1 us
    pallas_call x1, Pallas kernels, body(): call(encoder_back_kernel, [shape((chans, keep), BF16)] + [shape((chans, r...  25.4 us
    pallas_call x1, Pallas kernels, body(): call(encode_kernel, outs, grid=(edges // EDGE_TILE,), in_specs=[smem, til...  19.9 us
    ppermute x4, starting transfers between devices, trade(): lax.ppermute(west, PATCH, left)  17.9 us
    ppermute x4, starting transfers between devices, trade(): lax.ppermute(above, BAND, up)  16.2 us
    pallas_call x1, Pallas kernels, body(): call(mesh_kernel, outs, scratch_shapes=[pltpu.VMEM((table_rows + nodes, d...  11.8 us
    ppermute x4, starting transfers between devices, trade(): lax.ppermute(below, BAND, down)  8.17 us
  transfers between devices with their start and end apart: 19, of which 4 were waited for; matrix products, arithmetic and copies ran while one was open for 0% of the time, Pallas kernels for 8%

profile of v2, /device:TPU:1, one launch (start us, length us, event | category | flops | bytes accessed | tf_op | source)
XLA Modules:
  0.0 208.0 jit_solution(9566207761137208511)
XLA Ops:
  0.6 2.6 %shard_map.258 = (bf16[227,128]{1,0:T(8,128)(2,1)}, bf16[227,128]{1,0:T(8,128)(2,1)}, bf16[227,128]{1,0:T(8,128)(2,1)}, bf16[227,128]{1,0:T(8,128)(2,1)}) custom-call(s32[1,2048]{1,0:T(1,128)} %order_ref.5, bf16[227,2048]{1,0:T(8,128)(2,1)} %bitcast.10), custom_call_target="tpu_custom_call" | custom-call | tf_op jit(solution)/shard_map/pallas_call | solution.py:413
  3.2 4.9 %collective-permute-start = (bf16[227,128]{1,0:T(8,128)(2,1)}, bf16[227,128]{1,0:T(8,128)(2,1)S(1)}, u32[]{:S(2)}, u32[]{:S(2)}) collective-permute-start(bf16[227,128]{1,0:T(8,128)(2,1)} %get-tuple-element.59.own1), channel_id=1, source_target_pairs={{0,16},{16,32},{32,48},{48,64},{64,80},{80,96},{96,112},{1,17},{17... | collective-permute-start | bytes 174344 | tf_op jit(solution)/shard_map/ppermute | solution.py:382
  8.2 1.9 collective-permute-start.1
  10.1 1.3 collective-permute-start.2
  11.4 3.8 %collective-permute-start.3 = (bf16[227,128]{1,0:T(8,128)(2,1)}, bf16[227,128]{1,0:T(8,128)(2,1)S(1)}, u32[]{:S(2)}, u32[]{:S(2)}) collective-permute-start(bf16[227,128]{1,0:T(8,128)(2,1)} %get-tuple-element.62), channel_id=1, source_target_pairs={{1,0},{2,1},{3,2},{4,3},{5,4},{6,5},{7,6},{8,7},{9,8},{10,9},{11,1... | collective-permute-start | bytes 174344 | tf_op jit(solution)/shard_map/ppermute | solution.py:385
  15.2 7.1 %shard_map.257 = (bf16[227,1536]{1,0:T(8,128)(2,1)}, bf16[1536,512]{1,0:T(8,128)(2,1)}, bf16[256,512]{1,0:T(8,128)(2,1)}) custom-call(s32[1,2048]{1,0:T(1,128)} %order_ref.5, bf16[227,2048]{1,0:T(8,128)(2,1)} %bitcast.11, bf16[256,512]{1,0:T(8,128)(2,1)} %mesh_ref.5, bf16[227,512]{1,0:T(8,128)(2,1)} %embed_ref.5, bf16[512,512]{1,0:T(8,128)(2,1)} %send_ref.5, ...), custom_call_target="tpu_custom_call" | custom-call | tf_op jit(solution)/shard_map/pallas_call | solution.py:415
  22.3 0.6 pad_add_fusion.flag_ref
  22.9 0.0 copy-start.11
  23.0 0.6 copy-done.10
  23.5 0.0 copy-done.11
  23.6 0.0 copy-done.12
  23.6 0.0 copy-done.13
  23.6 19.9 %shard_map.259 = (bf16[227,512]{1,0:T(8,128)(2,1)}, bf16[4096,512]{1,0:T(8,128)(2,1)}, bf16[256,512]{1,0:T(8,128)(2,1)}, bf16[256,512]{1,0:T(8,128)(2,1)}, bf16[...) custom-call(s32[2]{0:T(128)} %pad_add_fusion.flag_ref, ...), custom_call_target="tpu_custom_call" | custom-call | tf_op jit(solution)/shard_map/pallas_call | solution.py:429
  43.5 4.0 %collective-permute-start.4 = (bf16[32,256]{1,0:T(8,128)(2,1)}, bf16[32,256]{1,0:T(8,128)(2,1)S(1)}, u32[]{:S(2)}, u32[]{:S(2)}) collective-permute-start(bf16[32,256]{1,0:T(8,128)(2,1)} %get-tuple-element.68), channel_id=1, source_target_pairs={{0,16},{16,32},{32,48},{48,64},{64,80},{80,96},{96,112},{1,17},{17... | collective-permute-start | bytes 49160 | tf_op jit(solution)/shard_map/ppermute | solution.py:382
  47.5 1.9 collective-permute-start.5
  49.4 0.1 collective-permute-start.6
  49.5 4.8 %collective-permute-start.7 = (bf16[32,256]{1,0:T(8,128)(2,1)}, bf16[32,256]{1,0:T(8,128)(2,1)S(1)}, u32[]{:S(2)}, u32[]{:S(2)}) collective-permute-start(bf16[32,256]{1,0:T(8,128)(2,1)} %get-tuple-element.71), channel_id=1, source_target_pairs={{1,0},{2,1},{3,2},{4,3},{5,4},{6,5},{7,6},{8,7},{9,8},{10,9},{11,1... | collective-permute-start | bytes 49160 | tf_op jit(solution)/shard_map/ppermute | solution.py:385
  54.3 1.3 collective-permute-done.6.b2
  55.6 0.6 copy-done.19
  56.2 0.0 copy-done.21
  56.2 11.8 %shard_map.260 = (bf16[32,256]{1,0:T(8,128)(2,1)}, bf16[32,256]{1,0:T(8,128)(2,1)}, bf16[32,256]{1,0:T(8,128)(2,1)}, bf16[32,256]{1,0:T(8,128)(2,1)}, bf16[256,2...) custom-call(s32[1,2048]{1,0:T(1,128)} %src_ref.4, ...), custom_call_target="tpu_custom_call" | custom-call | tf_op jit(solution)/shard_map/pallas_call | solution.py:446
  68.0 0.1 collective-permute-start.10
  68.0 4.8 %collective-permute-start.11 = (bf16[32,256]{1,0:T(8,128)(2,1)}, bf16[32,256]{1,0:T(8,128)(2,1)S(1)}, u32[]{:S(2)}, u32[]{:S(2)}) collective-permute-start(bf16[32,256]{1,0:T(8,128)(2,1)} %get-tuple-element.77), channel_id=1, source_target_pairs={{1,0},{2,1},{3,2},{4,3},{5,4},{6,5},{7,6},{8,7},{9,8},{10,9},{11,1... | collective-permute-start | bytes 49160 | tf_op jit(solution)/shard_map/ppermute | solution.py:385
  72.9 5.3 %collective-permute-start.8 = (bf16[32,256]{1,0:T(8,128)(2,1)}, bf16[32,256]{1,0:T(8,128)(2,1)S(1)}, u32[]{:S(2)}, u32[]{:S(2)}) collective-permute-start(bf16[32,256]{1,0:T(8,128)(2,1)} %get-tuple-element.74), channel_id=1, source_target_pairs={{0,16},{16,32},{32,48},{48,64},{64,80},{80,96},{96,112},{1,17},{17... | collective-permute-start | bytes 49160 | tf_op jit(solution)/shard_map/ppermute | solution.py:382
  78.2 1.9 collective-permute-start.9
  80.2 3.3 %collective-permute-done.9.r1 = bf16[32,256]{1,0:T(8,128)(2,1)S(1)} collective-permute-done((bf16[32,256]{1,0:T(8,128)(2,1)}, bf16[32,256]{1,0:T(8,128)(2,1)S(1)}, u32[]{:S(2)}, u32[]{:S(2)}) %collective-permute-start.9) | collective-permute-done | bytes 16416 | tf_op jit(solution)/shard_map/ppermute | solution.py:383
  83.5 0.6 copy-done.20
  84.1 25.4 %shard_map.261 = (bf16[227,1536]{1,0:T(8,128)(2,1)}, bf16[227,128]{1,0:T(8,128)(2,1)}, bf16[227,128]{1,0:T(8,128)(2,1)}, bf16[227,128]{1,0:T(8,128)(2,1)}, bf16[...) custom-call(s32[1]{0:T(128)} %bitcast.2.core_ref, ...), custom_call_target="tpu_custom_call" | custom-call | tf_op jit(solution)/shard_map/pallas_call | solution.py:462
  109.6 3.4 %shard_map.263 = (bf16[640,512]{1,0:T(8,128)(2,1)}, bf16[640,512]{1,0:T(8,128)(2,1)}) custom-call(s32[1]{0:T(128)} %bitcast.2.core_ref, bf16[384,256]{1,0:T(8,128)(2,1)} %get-tuple-element.84.halo_table_ref, bf16[640,512]{1,0:T(8,128)(2,1)} %get-tuple-element.85.ends_ref, bf16[256,512]{1,0:T(8,128)(2,1)} %get-tuple-element.86.summed_ref, ...), custom_call_target="tpu_custom_call" | custom-call | tf_op jit(solution)/shard_map/pallas_call | solution.py:456
  112.9 0.5 collective-permute-start.16
  113.4 1.9 collective-permute-done.16.a_in
  115.4 0.8 copy-done.3
  116.2 0.3 copy-done.2
  116.5 3.4 %shard_map.264 = bf16[1536,512]{1,0:T(8,128)(2,1)} custom-call(bf16[640,512]{1,0:T(8,128)(2,1)} %get-tuple-element.90.a_mine, bf16[640,512]{1,0:T(8,128)(2,1)} %copy-done.3, bf16[896,512]{1,0:T(8,128)(2,1)} %get-tuple-element.92.b_mine, bf16[896,512]{1,0:T(8,128)(2,1)} %copy-done.2), custom_call_target="tpu_custom_call" | custom-call | tf_op jit(solution)/shard_map/pallas_call | solution.py:485
  119.9 30.6 %all_to_all.10.parts_ref = bf16[64,24,512]{2,1,0:T(8,128)(2,1)} all-to-all(bf16[64,24,512]{2,1,0:T(8,128)(2,1)} %bitcast.9), channel_id=1, replica_groups=mesh['z'=4,'core'=2,'y'=4,'x'=4] {'z','y','x'}, dimensions={0} | all-to-all | bytes 3145728 | tf_op jit(solution)/shard_map/all_to_all | solution.py:486
  150.5 2.9 %shard_map.265 = bf16[64,24,512]{2,1,0:T(8,128)(2,1)} custom-call(bf16[64,24,512]{2,1,0:T(8,128)(2,1)} %all_to_all.10.parts_ref), custom_call_target="tpu_custom_call" | custom-call | tf_op jit(solution)/shard_map/pallas_call | solution.py:487
  153.4 29.1 %all_to_all.11 = bf16[64,24,512]{2,1,0:T(8,128)(2,1)S(1)} all-to-all(bf16[64,24,512]{2,1,0:T(8,128)(2,1)} %shard_map.265), channel_id=1, replica_groups=mesh['z'=4,'core'=2,'y'=4,'x'=4] {'z','y','x'}, dimensions={0} | all-to-all | bytes 3145728 | tf_op jit(solution)/shard_map/all_to_all | solution.py:488
  182.5 2.5 %collective-permute-start.18 = (bf16[1536,512]{1,0:T(8,128)(2,1)S(1)}, bf16[1536,512]{1,0:T(8,128)(2,1)S(1)}, u32[]{:S(2)}, u32[]{:S(2)}) collective-permute-start(bf16[1536,512]{1,0:T(8,128)(2,1)S(1)} %bitcast.7), channel_id=1, source_target_pairs={{0,16},{16,0},{1,17},{17,1},{2,18},{18,2},{3,19},{19,3},{4,20},{20... | collective-permute-start | bytes 4718600 | tf_op jit(solution)/shard_map/ppermute | solution.py:390
  185.0 1.9 collective-permute-start.12
  186.9 2.4 %collective-permute-start.13 = (bf16[227,128]{1,0:T(8,128)(2,1)S(1)}, bf16[227,128]{1,0:T(8,128)(2,1)S(1)}, u32[]{:S(2)}, u32[]{:S(2)}) collective-permute-start(bf16[227,128]{1,0:T(8,128)(2,1)S(1)} %copy-done.4), channel_id=1, source_target_pairs={{16,0},{32,16},{48,32},{64,48},{80,64},{96,80},{112,96},{17,1},{33... | collective-permute-start | bytes 174344 | tf_op jit(solution)/shard_map/ppermute | solution.py:383
  189.4 0.4 collective-permute-start.14
  189.7 4.5 %collective-permute-start.15 = (bf16[227,128]{1,0:T(8,128)(2,1)S(1)}, bf16[227,128]{1,0:T(8,128)(2,1)S(1)}, u32[]{:S(2)}, u32[]{:S(2)}) collective-permute-start(bf16[227,128]{1,0:T(8,128)(2,1)S(1)} %copy-done.22), channel_id=1, source_target_pairs={{1,0},{2,1},{3,2},{4,3},{5,4},{6,5},{7,6},{8,7},{9,8},{10,9},{11,1... | collective-permute-start | bytes 174344 | tf_op jit(solution)/shard_map/ppermute | solution.py:385
  194.2 2.2 %collective-permute-done.14.in2 = bf16[227,128]{1,0:T(8,128)(2,1)S(1)} collective-permute-done((bf16[227,128]{1,0:T(8,128)(2,1)S(1)}, bf16[227,128]{1,0:T(8,128)(2,1)S(1)}, u32[]{:S(2)}, u32[]{:S(2)}) %collective-permute-start.14) | collective-permute-done | bytes 58144 | tf_op jit(solution)/shard_map/ppermute | solution.py:384
  196.4 0.6 copy-done.8
  197.0 0.0 copy-done.9
  197.1 5.2 %shard_map.262 = bf16[227,2048]{1,0:T(8,128)(2,1)} custom-call(s32[2]{0:T(128)} %pad_add_fusion.flag_ref, s32[1,2048]{1,0:T(1,128)} %order_ref.5, bf16[227,1536]{1,0:T(8,128)(2,1)} %get-tuple-element.78.keep_ref, bf16[227,128]{1,0:T(8,128)(2,1)} %copy-done.6, bf16[227,128]{1,0:T(8,128)(2,1)} %copy-done.7, bf16[227,128]{1,0:T(8,128)(2,1)} %copy-done.8, ...), custom_call_target="tpu_custom_call" | custom-call | tf_op jit(solution)/shard_map/pallas_call | solution.py:477
  202.3 1.1 copy-done.1
  203.4 4.6 %shard_map.266 = (f32[227,512]{1,0:T(8,128)}, f32[512,512]{1,0:T(8,128)}, f32[512,512]{1,0:T(8,128)}, f32[512,512]{1,0:T(8,128)}, f32[256,512]{1,0:T(8,128)}, /*...) custom-call(s32[1]{0:T(128)} %bitcast.2.core_ref, bf16[1536,512]{1,0:T(8,128)(2,1)} %bitcast.8, ...), custom_call_target="tpu_custom_call" | custom-call | tf_op jit(solution)/shard_map/pallas_call | solution.py:490
  (51 shorter events, 0.1 us)
Async XLA Ops:
  3.2 19.7 %collective-permute-start = (bf16[227,128]{1,0:T(8,128)(2,1)}, bf16[227,128]{1,0:T(8,128)(2,1)S(1)}, u32[]{:S(2)}, u32[]{:S(2)}) collective-permute-start(bf16[227,128]{1,0:T(8,128)(2,1)} %get-tuple-element.59.own1), channel_id=1, source_target_pairs={{0,16},{16,32},{32,48},{48,64},{64,80},{80,96},{96,112},{1,17},{17... | collective-permute-start | bytes 174344 | tf_op jit(solution)/shard_map/ppermute | solution.py:382
  8.2 14.8 %collective-permute-start.1 = (bf16[227,128]{1,0:T(8,128)(2,1)}, bf16[227,128]{1,0:T(8,128)(2,1)S(1)}, u32[]{:S(2)}, u32[]{:S(2)}) collective-permute-start(bf16[227,128]{1,0:T(8,128)(2,1)} %get-tuple-element.60.own0), channel_id=1, source_target_pairs={{16,0},{32,16},{48,32},{64,48},{80,64},{96,80},{112,96},{17,1},{33... | collective-permute-start | bytes 174344 | tf_op jit(solution)/shard_map/ppermute | solution.py:383
  10.1 12.8 %collective-permute-start.2 = (bf16[227,128]{1,0:T(8,128)(2,1)}, bf16[227,128]{1,0:T(8,128)(2,1)S(1)}, u32[]{:S(2)}, u32[]{:S(2)}) collective-permute-start(bf16[227,128]{1,0:T(8,128)(2,1)} %get-tuple-element.61), channel_id=1, source_target_pairs={{0,1},{1,2},{2,3},{3,4},{4,5},{5,6},{6,7},{7,8},{8,9},{9,10},{10,1... | collective-permute-start | bytes 174344 | tf_op jit(solution)/shard_map/ppermute | solution.py:384
  11.4 11.6 %collective-permute-start.3 = (bf16[227,128]{1,0:T(8,128)(2,1)}, bf16[227,128]{1,0:T(8,128)(2,1)S(1)}, u32[]{:S(2)}, u32[]{:S(2)}) collective-permute-start(bf16[227,128]{1,0:T(8,128)(2,1)} %get-tuple-element.62), channel_id=1, source_target_pairs={{1,0},{2,1},{3,2},{4,3},{5,4},{6,5},{7,6},{8,7},{9,8},{10,9},{11,1... | collective-permute-start | bytes 174344 | tf_op jit(solution)/shard_map/ppermute | solution.py:385
  22.9 0.6 copy-start.10
  22.9 0.6 copy-start.11
  22.9 0.6 copy-start.12
  23.0 0.6 copy-start.13
  43.5 10.8 %collective-permute-start.4 = (bf16[32,256]{1,0:T(8,128)(2,1)}, bf16[32,256]{1,0:T(8,128)(2,1)S(1)}, u32[]{:S(2)}, u32[]{:S(2)}) collective-permute-start(bf16[32,256]{1,0:T(8,128)(2,1)} %get-tuple-element.68), channel_id=1, source_target_pairs={{0,16},{16,32},{32,48},{48,64},{64,80},{80,96},{96,112},{1,17},{17... | collective-permute-start | bytes 49160 | tf_op jit(solution)/shard_map/ppermute | solution.py:382
  47.5 6.8 %collective-permute-start.5 = (bf16[32,256]{1,0:T(8,128)(2,1)}, bf16[32,256]{1,0:T(8,128)(2,1)S(1)}, u32[]{:S(2)}, u32[]{:S(2)}) collective-permute-start(bf16[32,256]{1,0:T(8,128)(2,1)} %get-tuple-element.69), channel_id=1, source_target_pairs={{16,0},{32,16},{48,32},{64,48},{80,64},{96,80},{112,96},{17,1},{33... | collective-permute-start | bytes 49160 | tf_op jit(solution)/shard_map/ppermute | solution.py:383
  49.4 6.2 %collective-permute-start.6 = (bf16[32,256]{1,0:T(8,128)(2,1)}, bf16[32,256]{1,0:T(8,128)(2,1)S(1)}, u32[]{:S(2)}, u32[]{:S(2)}) collective-permute-start(bf16[32,256]{1,0:T(8,128)(2,1)} %get-tuple-element.70), channel_id=1, source_target_pairs={{0,1},{1,2},{2,3},{3,4},{4,5},{5,6},{6,7},{7,8},{8,9},{9,10},{10,1... | collective-permute-start | bytes 49160 | tf_op jit(solution)/shard_map/ppermute | solution.py:384
  49.5 6.1 %collective-permute-start.7 = (bf16[32,256]{1,0:T(8,128)(2,1)}, bf16[32,256]{1,0:T(8,128)(2,1)S(1)}, u32[]{:S(2)}, u32[]{:S(2)}) collective-permute-start(bf16[32,256]{1,0:T(8,128)(2,1)} %get-tuple-element.71), channel_id=1, source_target_pairs={{1,0},{2,1},{3,2},{4,3},{5,4},{6,5},{7,6},{8,7},{9,8},{10,9},{11,1... | collective-permute-start | bytes 49160 | tf_op jit(solution)/shard_map/ppermute | solution.py:385
  54.3 1.3 copy-start.15
  54.3 1.3 copy-start.17
  55.6 0.6 copy-start.19
  55.6 0.6 copy-start.21
  68.0 12.2 %collective-permute-start.10 = (bf16[32,256]{1,0:T(8,128)(2,1)}, bf16[32,256]{1,0:T(8,128)(2,1)S(1)}, u32[]{:S(2)}, u32[]{:S(2)}) collective-permute-start(bf16[32,256]{1,0:T(8,128)(2,1)} %get-tuple-element.76), channel_id=1, source_target_pairs={{0,1},{1,2},{2,3},{3,4},{4,5},{5,6},{6,7},{7,8},{8,9},{9,10},{10,1... | collective-permute-start | bytes 49160 | tf_op jit(solution)/shard_map/ppermute | solution.py:384
  68.0 12.1 %collective-permute-start.11 = (bf16[32,256]{1,0:T(8,128)(2,1)}, bf16[32,256]{1,0:T(8,128)(2,1)S(1)}, u32[]{:S(2)}, u32[]{:S(2)}) collective-permute-start(bf16[32,256]{1,0:T(8,128)(2,1)} %get-tuple-element.77), channel_id=1, source_target_pairs={{1,0},{2,1},{3,2},{4,3},{5,4},{6,5},{7,6},{8,7},{9,8},{10,9},{11,1... | collective-permute-start | bytes 49160 | tf_op jit(solution)/shard_map/ppermute | solution.py:385
  72.9 7.3 %collective-permute-start.8 = (bf16[32,256]{1,0:T(8,128)(2,1)}, bf16[32,256]{1,0:T(8,128)(2,1)S(1)}, u32[]{:S(2)}, u32[]{:S(2)}) collective-permute-start(bf16[32,256]{1,0:T(8,128)(2,1)} %get-tuple-element.74), channel_id=1, source_target_pairs={{0,16},{16,32},{32,48},{48,64},{64,80},{80,96},{96,112},{1,17},{17... | collective-permute-start | bytes 49160 | tf_op jit(solution)/shard_map/ppermute | solution.py:382
  78.2 5.3 %collective-permute-start.9 = (bf16[32,256]{1,0:T(8,128)(2,1)}, bf16[32,256]{1,0:T(8,128)(2,1)S(1)}, u32[]{:S(2)}, u32[]{:S(2)}) collective-permute-start(bf16[32,256]{1,0:T(8,128)(2,1)} %get-tuple-element.75), channel_id=1, source_target_pairs={{16,0},{32,16},{48,32},{64,48},{80,64},{96,80},{112,96},{17,1},{33... | collective-permute-start | bytes 49160 | tf_op jit(solution)/shard_map/ppermute | solution.py:383
  80.2 3.3 %copy-start.14 = (bf16[32,256]{1,0:T(8,128)(2,1)}, bf16[32,256]{1,0:T(8,128)(2,1)S(1)}, u32[]{:S(2)}) copy-start(bf16[32,256]{1,0:T(8,128)(2,1)S(1)} %collective-permute-done.10.r2) | copy-start | bytes 49156
  80.2 3.3 %copy-start.16 = (bf16[32,256]{1,0:T(8,128)(2,1)}, bf16[32,256]{1,0:T(8,128)(2,1)S(1)}, u32[]{:S(2)}) copy-start(bf16[32,256]{1,0:T(8,128)(2,1)S(1)} %collective-permute-done.11.r3) | copy-start | bytes 49156
  80.2 3.3 %copy-start.18 = (bf16[32,256]{1,0:T(8,128)(2,1)}, bf16[32,256]{1,0:T(8,128)(2,1)S(1)}, u32[]{:S(2)}) copy-start(bf16[32,256]{1,0:T(8,128)(2,1)S(1)} %collective-permute-done.8.r0) | copy-start | bytes 49156
  83.5 0.6 copy-start.20
  109.5 5.8 %collective-permute-start.17 = (bf16[896,512]{1,0:T(8,128)(2,1)}, bf16[896,512]{1,0:T(8,128)(2,1)S(1)}, u32[]{:S(2)}, u32[]{:S(2)}) collective-permute-start(bf16[896,512]{1,0:T(8,128)(2,1)} %get-tuple-element.93), channel_id=1, source_target_pairs={{0,16},{16,0},{1,17},{17,1},{2,18},{18,2},{3,19},{19,3},{4,20},{20... | collective-permute-start | bytes 2752520 | tf_op jit(solution)/shard_map/ppermute | solution.py:390
  112.9 2.4 %collective-permute-start.16 = (bf16[640,512]{1,0:T(8,128)(2,1)}, bf16[640,512]{1,0:T(8,128)(2,1)S(1)}, u32[]{:S(2)}, u32[]{:S(2)}) collective-permute-start(bf16[640,512]{1,0:T(8,128)(2,1)} %get-tuple-element.91), channel_id=1, source_target_pairs={{0,16},{16,0},{1,17},{17,1},{2,18},{18,2},{3,19},{19,3},{4,20},{20... | collective-permute-start | bytes 1966088 | tf_op jit(solution)/shard_map/ppermute | solution.py:390
  115.4 0.8 copy-start.3
  115.4 1.1 copy-start.2
  153.4 31.6 %copy-start.5 = (bf16[227,128]{1,0:T(8,128)(2,1)S(1)}, bf16[227,128]{1,0:T(8,128)(2,1)}, u32[]{:S(2)}) copy-start(bf16[227,128]{1,0:T(8,128)(2,1)} %get-tuple-element.79.own1) | copy-start | bytes 174340
  153.4 33.5 %copy-start.4 = (bf16[227,128]{1,0:T(8,128)(2,1)S(1)}, bf16[227,128]{1,0:T(8,128)(2,1)}, u32[]{:S(2)}) copy-start(bf16[227,128]{1,0:T(8,128)(2,1)} %get-tuple-element.80.own0) | copy-start | bytes 174340
  153.4 35.9 %copy-start.23 = (bf16[227,128]{1,0:T(8,128)(2,1)S(1)}, bf16[227,128]{1,0:T(8,128)(2,1)}, u32[]{:S(2)}) copy-start(bf16[227,128]{1,0:T(8,128)(2,1)} %get-tuple-element.81) | copy-start | bytes 174340
  153.4 36.3 %copy-start.22 = (bf16[227,128]{1,0:T(8,128)(2,1)S(1)}, bf16[227,128]{1,0:T(8,128)(2,1)}, u32[]{:S(2)}) copy-start(bf16[227,128]{1,0:T(8,128)(2,1)} %get-tuple-element.82) | copy-start | bytes 174340
  182.5 19.8 %copy-start = (bf16[64,24,512]{2,1,0:T(8,128)(2,1)}, bf16[64,24,512]{2,1,0:T(8,128)(2,1)S(1)}, u32[]{:S(2)}) copy-start(bf16[64,24,512]{2,1,0:T(8,128)(2,1)S(1)} %all_to_all.11) | copy-start | bytes 4718596
  182.5 19.7 %collective-permute-start.18 = (bf16[1536,512]{1,0:T(8,128)(2,1)S(1)}, bf16[1536,512]{1,0:T(8,128)(2,1)S(1)}, u32[]{:S(2)}, u32[]{:S(2)}) collective-permute-start(bf16[1536,512]{1,0:T(8,128)(2,1)S(1)} %bitcast.7), channel_id=1, source_target_pairs={{0,16},{16,0},{1,17},{17,1},{2,18},{18,2},{3,19},{19,3},{4,20},{20... | collective-permute-start | bytes 4718600 | tf_op jit(solution)/shard_map/ppermute | solution.py:390
  185.0 9.2 %collective-permute-start.12 = (bf16[227,128]{1,0:T(8,128)(2,1)S(1)}, bf16[227,128]{1,0:T(8,128)(2,1)S(1)}, u32[]{:S(2)}, u32[]{:S(2)}) collective-permute-start(bf16[227,128]{1,0:T(8,128)(2,1)S(1)} %copy-done.5), channel_id=1, source_target_pairs={{0,16},{16,32},{32,48},{48,64},{64,80},{80,96},{96,112},{1,17},{17... | collective-permute-start | bytes 174344 | tf_op jit(solution)/shard_map/ppermute | solution.py:382
  186.9 7.3 %collective-permute-start.13 = (bf16[227,128]{1,0:T(8,128)(2,1)S(1)}, bf16[227,128]{1,0:T(8,128)(2,1)S(1)}, u32[]{:S(2)}, u32[]{:S(2)}) collective-permute-start(bf16[227,128]{1,0:T(8,128)(2,1)S(1)} %copy-done.4), channel_id=1, source_target_pairs={{16,0},{32,16},{48,32},{64,48},{80,64},{96,80},{112,96},{17,1},{33... | collective-permute-start | bytes 174344 | tf_op jit(solution)/shard_map/ppermute | solution.py:383
  189.4 7.1 %collective-permute-start.14 = (bf16[227,128]{1,0:T(8,128)(2,1)S(1)}, bf16[227,128]{1,0:T(8,128)(2,1)S(1)}, u32[]{:S(2)}, u32[]{:S(2)}) collective-permute-start(bf16[227,128]{1,0:T(8,128)(2,1)S(1)} %copy-done.23), channel_id=1, source_target_pairs={{0,1},{1,2},{2,3},{3,4},{4,5},{5,6},{6,7},{7,8},{8,9},{9,10},{10,1... | collective-permute-start | bytes 174344 | tf_op jit(solution)/shard_map/ppermute | solution.py:384
  189.7 6.7 %collective-permute-start.15 = (bf16[227,128]{1,0:T(8,128)(2,1)S(1)}, bf16[227,128]{1,0:T(8,128)(2,1)S(1)}, u32[]{:S(2)}, u32[]{:S(2)}) collective-permute-start(bf16[227,128]{1,0:T(8,128)(2,1)S(1)} %copy-done.22), channel_id=1, source_target_pairs={{1,0},{2,1},{3,2},{4,3},{5,4},{6,5},{7,6},{8,7},{9,8},{10,9},{11,1... | collective-permute-start | bytes 174344 | tf_op jit(solution)/shard_map/ppermute | solution.py:385
  194.2 2.2 %copy-start.6 = (bf16[227,128]{1,0:T(8,128)(2,1)}, bf16[227,128]{1,0:T(8,128)(2,1)S(1)}, u32[]{:S(2)}) copy-start(bf16[227,128]{1,0:T(8,128)(2,1)S(1)} %collective-permute-done.12.in0) | copy-start | bytes 174340
  194.2 2.2 %copy-start.7 = (bf16[227,128]{1,0:T(8,128)(2,1)}, bf16[227,128]{1,0:T(8,128)(2,1)S(1)}, u32[]{:S(2)}) copy-start(bf16[227,128]{1,0:T(8,128)(2,1)S(1)} %collective-permute-done.13.in1) | copy-start | bytes 174340
  196.4 0.6 copy-start.8
  196.4 0.6 copy-start.9
  202.2 1.2 copy-start.1

commit v3 on v2

--- a/solution.py
+++ b/solution.py
@@ -11,7 +11,7 @@
 BF16 = jnp.bfloat16
 F32 = jnp.float32
 LANES = 128
-EDGE_TILE = 512
+EDGE_TILE = 1024
 ROW_TILE = 512
 VMEM_LIMIT = 56 * 1024 * 1024
 BAND = ("z", "core")
@@ -56,10 +56,11 @@
     return act, sigma + act * (1.0 - sigma)
 
 
-def call(kernel, out_shape, **more):
+def call(kernel, out_shape, work, **more):
     return pl.pallas_call(
         kernel,
         out_shape=out_shape,
+        cost_estimate=pl.CostEstimate(flops=int(work * 1e9), bytes_accessed=int(work * 1e6), transcendentals=0),
         compiler_params=pltpu.CompilerParams(vmem_limit_bytes=VMEM_LIMIT),
         **more,
     )
@@ -325,21 +326,6 @@
     lax.fori_loop(0, grid_grad_ref.shape[1] // ROW_TILE, place, 0)
 
 
-def add_kernel(a_mine, a_in, b_mine, b_in, sum_ref):
-    count = a_mine.shape[0]
-    sum_ref[0:count, :] = (a_mine[...].astype(F32) + a_in[...].astype(F32)).astype(BF16)
-    sum_ref[count:, :] = (b_mine[...].astype(F32) + b_in[...].astype(F32)).astype(BF16)
-
-
-def total_kernel(parts_ref, out_ref):
-    total = parts_ref[0].astype(F32)
-    for k in range(1, parts_ref.shape[0]):
-        total += parts_ref[k].astype(F32)
-    total = total.astype(BF16)
-    for k in range(parts_ref.shape[0]):
-        out_ref[k] = total
-
-
 def unpack_kernel(a_rows, core_ref, mine_ref, other_ref, embed_ref, send_ref, recv_ref, out_ref, u_src_ref, u_dst_ref, u_out_ref, v_in_ref, v_out_ref):
     first = core_ref[0] == 0
 
@@ -410,11 +396,12 @@
     vmem = pl.BlockSpec(memory_space=pltpu.VMEM)
 
     grid_cols = grid_feats.T
-    own = call(pick_rim_kernel, [shape((chans, rim), BF16)] * 4)(send_rows, grid_cols)
+    own = call(pick_rim_kernel, [shape((chans, rim), BF16)] * 4, 3)(send_rows, grid_cols)
     arrived = trade(*own)
     keep_rows, keep_sender, node_part = call(
         keep_kernel,
         [shape((chans, keep), BF16), shape((keep, dim), BF16), shape((nodes, dim), BF16)],
+        7,
     )(send_rows, grid_cols, mesh_feats, w_embed, w_send, w_recv)
 
     def whole(array):
@@ -429,6 +416,7 @@
     rim_rows, slope, gathered, latent, h00, h01, h10, h11 = call(
         encode_kernel,
         outs,
+        20,
         grid=(edges // EDGE_TILE,),
         in_specs=[smem, tile, tile] + [whole(x) for x in ins],
         out_specs=[
@@ -446,6 +434,7 @@
     (g0, g1, g2, g3, coupled_grad, lower_grad, halo_table, ends, summed, coupled, hidden, hidden_grad) = call(
         mesh_kernel,
         outs,
+        12,
         scratch_shapes=[
             pltpu.VMEM((table_rows + nodes, dim), BF16), pltpu.VMEM((mesh_src.shape[1], dim), BF16),
             pltpu.VMEM((nodes, dim), F32), pltpu.VMEM((table_rows + nodes, dim), F32),
@@ -454,15 +443,17 @@
     returned = trade(g0, g1, g2, g3)
     a_rows = 5 * half
     a_mine, a_other = call(
-        mesh_weight_kernel, [shape((a_rows // 2, dim), BF16)] * 2, in_specs=[smem] + [vmem] * 8,
+        mesh_weight_kernel, [shape((a_rows // 2, dim), BF16)] * 2, 4, in_specs=[smem] + [vmem] * 8,
     )(core, halo_table, ends, summed, coupled, hidden, hidden_grad, coupled_grad, cotangent)
     a_in = swap_cores(a_other)
+    lower_grad, a_mine = lax.optimization_barrier((lower_grad, a_mine))
 
     b_rows = 3 * dim + half
     keep_grad, q0, q1, q2, q3, mesh_grad, b_mine, b_other = call(
         encoder_back_kernel,
         [shape((chans, keep), BF16)] + [shape((chans, rim), BF16)] * 4 + [shape((nodes, dim), F32)]
         + [shape((b_rows // 2, dim), BF16)] * 2,
+        25,
         in_specs=[smem] + [vmem] * 18,
         scratch_shapes=[
             pltpu.VMEM((half, dim), F32), pltpu.VMEM((dim, dim), F32),
@@ -477,20 +468,24 @@
     grid_grad = call(
         place_kernel,
         shape((chans, grid_rows), BF16),
+        5,
         in_specs=[smem] + [vmem] * 8,
         scratch_shapes=[pltpu.VMEM((chans, grid_rows), BF16)],
     )(flags, send_rows, keep_grad, *back, q0, q1)
     chips = lax.axis_size(CHIPS)
     packed = (a_rows + b_rows) // 2
-    pair = call(add_kernel, shape((packed, dim), BF16))(a_mine, a_in, b_mine, b_in)
-    parts = lax.all_to_all(pair.reshape(chips, packed // chips, dim), CHIPS, 0, 0)
-    parts = call(total_kernel, shape(parts.shape, BF16))(parts)
+    pair = jnp.concatenate([a_mine.astype(F32) + a_in.astype(F32), b_mine.astype(F32) + b_in.astype(F32)], axis=0)
+    pair = pair.astype(BF16).reshape(chips, packed // chips, dim)
+    parts = lax.all_to_all(pair, CHIPS, 0, 0)
+    total = jnp.sum(parts.astype(F32), axis=0).astype(BF16)
+    parts = jnp.broadcast_to(total[None], parts.shape)
     mine = lax.all_to_all(parts, CHIPS, 0, 0).reshape(packed, dim)
     other = swap_cores(mine)
     totals = call(
         functools.partial(unpack_kernel, a_rows),
         [shape((chans, dim), F32)] + [shape((dim, dim), F32)] * 3 + [shape((half, dim), F32)] * 2
         + [shape((dim, half), F32), shape((half, dim), F32), shape((dim, half), F32)],
+        5,
         in_specs=[smem] + [vmem] * 2,
     )(core, mine, other)
     return (grid_grad.T, mesh_grad, *totals)

time: 209 us -> 198 us (0.947)
  Pallas kernels: 86.2 us -> 75.6 us
    pallas_call x7 -> x5, Pallas kernels: 49.1 us -> 40 us  [the longest x1 18.5 us: body(): call(encode_kernel, outs, 20, grid=(edges // EDGE_TILE,), in_specs=[smem,...]
    ppermute x4, waiting for transfers between devices: 3.49 us -> 1.32 us  [trade(): lax.ppermute(east, PATCH, right)]
  transfers between devices with their start and end apart: 19 -> 19, of which waited for: 4 -> 3; matrix products, arithmetic and copies ran while one was open for 0% -> 0% of each run, Pallas kernels for 8% -> 20%
where the time goes in v3:
time: 198 us; the launch traced here: 197 us
  Pallas kernels  75.6 us (38%)
  blocking collectives  61.5 us (31%)
  starting transfers between devices  47 us (24%)
  waiting for transfers between devices  7 us (4%)
  local copies, waits for them, and re-layouts  3.76 us (2%)
    all_to_all x1, blocking collectives, body(): parts = lax.all_to_all(pair, CHIPS, 0, 0)  32.6 us
    all_to_all x1, blocking collectives, body(): mine = lax.all_to_all(parts, CHIPS, 0, 0).reshape(packed, dim)  28.9 us
    pallas_call x1, Pallas kernels, body(): call(encoder_back_kernel, [shape((chans, keep), BF16)] + [shape((chans, r...  23.9 us
    pallas_call x1, Pallas kernels, body(): call(encode_kernel, outs, 20, grid=(edges // EDGE_TILE,), in_specs=[smem,...  18.5 us
    ppermute x4, starting transfers between devices, trade(): lax.ppermute(west, PATCH, left)  18.3 us
    ppermute x4, starting transfers between devices, trade(): lax.ppermute(above, BAND, up)  15.4 us
    pallas_call x1, Pallas kernels, body(): call(mesh_kernel, outs, 12, scratch_shapes=[pltpu.VMEM((table_rows + node...  10.3 us
    ppermute x4, starting transfers between devices, trade(): lax.ppermute(below, BAND, down)  7.68 us
  transfers between devices with their start and end apart: 19, of which 3 were waited for; matrix products, arithmetic and copies ran while one was open for 0% of the time, Pallas kernels for 20%

profile of v3, /device:TPU:1, one launch (start us, length us, event | category | flops | bytes accessed | tf_op | source)
XLA Modules:
  0.0 197.2 jit_solution(7370979417912679354)
XLA Ops:
  0.6 2.6 %shard_map.258 = (bf16[227,128]{1,0:T(8,128)(2,1)}, bf16[227,128]{1,0:T(8,128)(2,1)}, bf16[227,128]{1,0:T(8,128)(2,1)}, bf16[227,128]{1,0:T(8,128)(2,1)}) custom-call(s32[1,2048]{1,0:T(1,128)} %order_ref.5, bf16[227,2048]{1,0:T(8,128)(2,1)} %bitcast.10), custom_call_target="tpu_custom_call" | custom-call | flops 3000000000 | bytes 3000000 | tf_op jit(solution)/shard_map/pallas_call | solution.py:399
  3.2 2.0 %collective-permute-start.2 = (bf16[227,128]{1,0:T(8,128)(2,1)}, bf16[227,128]{1,0:T(8,128)(2,1)S(1)}, u32[]{:S(2)}, u32[]{:S(2)}) collective-permute-start(bf16[227,128]{1,0:T(8,128)(2,1)} %get-tuple-element.63), channel_id=1, source_target_pairs={{0,1},{1,2},{2,3},{3,4},{4,5},{5,6},{6,7},{7,8},{8,9},{9,10},{10,1... | collective-permute-start | bytes 174344 | tf_op jit(solution)/shard_map/ppermute | solution.py:370
  5.3 3.7 %collective-permute-start.3 = (bf16[227,128]{1,0:T(8,128)(2,1)}, bf16[227,128]{1,0:T(8,128)(2,1)S(1)}, u32[]{:S(2)}, u32[]{:S(2)}) collective-permute-start(bf16[227,128]{1,0:T(8,128)(2,1)} %get-tuple-element.64), channel_id=1, source_target_pairs={{1,0},{2,1},{3,2},{4,3},{5,4},{6,5},{7,6},{8,7},{9,8},{10,9},{11,1... | collective-permute-start | bytes 174344 | tf_op jit(solution)/shard_map/ppermute | solution.py:371
  9.0 4.5 %collective-permute-start = (bf16[227,128]{1,0:T(8,128)(2,1)}, bf16[227,128]{1,0:T(8,128)(2,1)S(1)}, u32[]{:S(2)}, u32[]{:S(2)}) collective-permute-start(bf16[227,128]{1,0:T(8,128)(2,1)} %get-tuple-element.61.own1), channel_id=1, source_target_pairs={{0,16},{16,32},{32,48},{48,64},{64,80},{80,96},{96,112},{1,17},{17... | collective-permute-start | bytes 174344 | tf_op jit(solution)/shard_map/ppermute | solution.py:368
  13.5 1.9 collective-permute-start.1
  15.4 7.2 %shard_map.257 = (bf16[227,1536]{1,0:T(8,128)(2,1)}, bf16[1536,512]{1,0:T(8,128)(2,1)}, bf16[256,512]{1,0:T(8,128)(2,1)}) custom-call(s32[1,2048]{1,0:T(1,128)} %order_ref.5, bf16[227,2048]{1,0:T(8,128)(2,1)} %bitcast.11, bf16[256,512]{1,0:T(8,128)(2,1)} %mesh_ref.5, bf16[227,512]{1,0:T(8,128)(2,1)} %embed_ref.5, bf16[512,512]{1,0:T(8,128)(2,1)} %send_ref.5, ...), custom_call_target="tpu_custom_call" | custom-call | flops 7000000000 | bytes 7000000 | tf_op jit(solution)/shard_map/pallas_call | solution.py:401
  22.6 0.6 pad_add_fusion.flag_ref
  23.3 0.6 copy-done.7
  23.8 0.0 copy-done.9
  23.8 0.0 copy-done.10
  23.9 0.0 copy-done.11
  23.9 18.5 %shard_map.259 = (bf16[227,512]{1,0:T(8,128)(2,1)}, bf16[4096,512]{1,0:T(8,128)(2,1)}, bf16[256,512]{1,0:T(8,128)(2,1)}, bf16[256,512]{1,0:T(8,128)(2,1)}, bf16[...) custom-call(s32[2]{0:T(128)} %pad_add_fusion.flag_ref, ...), custom_call_target="tpu_custom_call" | custom-call | flops 20000000000 | bytes 20000000 | tf_op jit(solution)/shard_map/pallas_call | solution.py:416
  42.4 3.7 %collective-permute-start.4 = (bf16[32,256]{1,0:T(8,128)(2,1)}, bf16[32,256]{1,0:T(8,128)(2,1)S(1)}, u32[]{:S(2)}, u32[]{:S(2)}) collective-permute-start(bf16[32,256]{1,0:T(8,128)(2,1)} %get-tuple-element.70), channel_id=1, source_target_pairs={{0,16},{16,32},{32,48},{48,64},{64,80},{80,96},{96,112},{1,17},{17... | collective-permute-start | bytes 49160 | tf_op jit(solution)/shard_map/ppermute | solution.py:368
  46.1 1.9 collective-permute-start.5
  48.0 0.1 collective-permute-start.6
  48.1 4.8 %collective-permute-start.7 = (bf16[32,256]{1,0:T(8,128)(2,1)}, bf16[32,256]{1,0:T(8,128)(2,1)S(1)}, u32[]{:S(2)}, u32[]{:S(2)}) collective-permute-start(bf16[32,256]{1,0:T(8,128)(2,1)} %get-tuple-element.73), channel_id=1, source_target_pairs={{1,0},{2,1},{3,2},{4,3},{5,4},{6,5},{7,6},{8,7},{9,8},{10,9},{11,1... | collective-permute-start | bytes 49160 | tf_op jit(solution)/shard_map/ppermute | solution.py:371
  52.9 1.3 collective-permute-done.6.b2
  54.2 0.6 copy-done.22
  54.8 10.3 %shard_map.260 = (bf16[32,256]{1,0:T(8,128)(2,1)}, bf16[32,256]{1,0:T(8,128)(2,1)}, bf16[32,256]{1,0:T(8,128)(2,1)}, bf16[32,256]{1,0:T(8,128)(2,1)}, bf16[256,2...) custom-call(s32[1,2048]{1,0:T(1,128)} %src_ref.4, ...), custom_call_target="tpu_custom_call" | custom-call | flops 12000000000 | bytes 12000000 | tf_op jit(solution)/shard_map/pallas_call | solution.py:434
  65.1 4.8 %collective-permute-start.8 = (bf16[32,256]{1,0:T(8,128)(2,1)}, bf16[32,256]{1,0:T(8,128)(2,1)S(1)}, u32[]{:S(2)}, u32[]{:S(2)}) collective-permute-start(bf16[32,256]{1,0:T(8,128)(2,1)} %get-tuple-element.84), channel_id=1, source_target_pairs={{0,16},{16,32},{32,48},{48,64},{64,80},{80,96},{96,112},{1,17},{17... | collective-permute-start | bytes 49160 | tf_op jit(solution)/shard_map/ppermute | solution.py:368
  69.9 1.9 collective-permute-start.9
  71.8 0.1 collective-permute-start.10
  71.9 5.3 %collective-permute-start.11 = (bf16[32,256]{1,0:T(8,128)(2,1)}, bf16[32,256]{1,0:T(8,128)(2,1)S(1)}, u32[]{:S(2)}, u32[]{:S(2)}) collective-permute-start(bf16[32,256]{1,0:T(8,128)(2,1)} %get-tuple-element.87), channel_id=1, source_target_pairs={{1,0},{2,1},{3,2},{4,3},{5,4},{6,5},{7,6},{8,7},{9,8},{10,9},{11,1... | collective-permute-start | bytes 49160 | tf_op jit(solution)/shard_map/ppermute | solution.py:371
  77.2 3.4 %shard_map.261 = (bf16[640,512]{1,0:T(8,128)(2,1)}, bf16[640,512]{1,0:T(8,128)(2,1)}) custom-call(s32[1]{0:T(128)} %bitcast.2.core_ref, bf16[384,256]{1,0:T(8,128)(2,1)} %get-tuple-element.76.halo_table_ref, bf16[640,512]{1,0:T(8,128)(2,1)} %get-tuple-element.77.ends_ref, bf16[256,512]{1,0:T(8,128)(2,1)} %get-tuple-element.78.summed_ref, ...), custom_call_target="tpu_custom_call" | custom-call | flops 4000000000 | bytes 4000000 | tf_op jit(solution)/shard_map/pallas_call | solution.py:445
  80.7 0.5 copy-done.16
  81.2 0.0 copy-done.17
  81.2 0.0 copy-done.18
  81.2 0.0 copy-done.19
  81.3 23.9 %shard_map.262 = (bf16[227,1536]{1,0:T(8,128)(2,1)}, bf16[227,128]{1,0:T(8,128)(2,1)}, bf16[227,128]{1,0:T(8,128)(2,1)}, bf16[227,128]{1,0:T(8,128)(2,1)}, bf16[...) custom-call(s32[1]{0:T(128)} %bitcast.2.core_ref, ...), custom_call_target="tpu_custom_call" | custom-call | flops 24999999488 | bytes 25000000 | tf_op jit(solution)/shard_map/pallas_call | solution.py:452
  105.2 0.6 collective-permute-start.17
  105.8 0.2 add_convert_fusion.1
  106.0 2.1 %collective-permute-done.17 = bf16[896,512]{1,0:T(8,128)(2,1)S(1)} collective-permute-done((bf16[896,512]{1,0:T(8,128)(2,1)}, bf16[896,512]{1,0:T(8,128)(2,1)S(1)}, u32[]{:S(2)}, u32[]{:S(2)}) %collective-permute-start.17) | collective-permute-done | bytes 917536 | tf_op jit(solution)/shard_map/ppermute | solution.py:376
  108.1 0.3 add_convert_fusion
  108.4 0.1 pad_maximum_fusion
  108.5 32.6 %all_to_all.10 = bf16[64,24,512]{2,1,0:T(8,128)(2,1)S(1)} all-to-all(bf16[64,24,512]{2,1,0:T(8,128)(2,1)S(1)} %bitcast.7), channel_id=1, replica_groups=mesh['z'=4,'core'=2,'y'=4,'x'=4] {'z','y','x'}, dimensions={0} | all-to-all | bytes 3145728 | tf_op jit(solution)/shard_map/all_to_all | solution.py:479
  141.1 0.2 reduce_sum.12
  141.3 0.1 broadcast_in_dim.2
  141.5 28.9 %all_to_all.11 = bf16[64,24,512]{2,1,0:T(8,128)(2,1)S(1)} all-to-all(bf16[64,24,512]{2,1,0:T(8,128)(2,1)S(1)} %broadcast_in_dim.2), channel_id=1, replica_groups=mesh['z'=4,'core'=2,'y'=4,'x'=4] {'z','y','x'}, dimensions={0} | all-to-all | bytes 3145728 | tf_op jit(solution)/shard_map/all_to_all | solution.py:482
  170.3 2.5 %collective-permute-start.18 = (bf16[1536,512]{1,0:T(8,128)(2,1)S(1)}, bf16[1536,512]{1,0:T(8,128)(2,1)S(1)}, u32[]{:S(2)}, u32[]{:S(2)}) collective-permute-start(bf16[1536,512]{1,0:T(8,128)(2,1)S(1)} %bitcast.8), channel_id=1, source_target_pairs={{0,16},{16,0},{1,17},{17,1},{2,18},{18,2},{3,19},{19,3},{4,20},{20... | collective-permute-start | bytes 4718600 | tf_op jit(solution)/shard_map/ppermute | solution.py:376
  172.9 0.3 collective-permute-start.14
  173.2 4.5 %collective-permute-start.15 = (bf16[227,128]{1,0:T(8,128)(2,1)S(1)}, bf16[227,128]{1,0:T(8,128)(2,1)S(1)}, u32[]{:S(2)}, u32[]{:S(2)}) collective-permute-start(bf16[227,128]{1,0:T(8,128)(2,1)S(1)} %copy-done.6), channel_id=1, source_target_pairs={{1,0},{2,1},{3,2},{4,3},{5,4},{6,5},{7,6},{8,7},{9,8},{10,9},{11,1... | collective-permute-start | bytes 174344 | tf_op jit(solution)/shard_map/ppermute | solution.py:371
  177.7 2.5 %collective-permute-start.12 = (bf16[227,128]{1,0:T(8,128)(2,1)S(1)}, bf16[227,128]{1,0:T(8,128)(2,1)S(1)}, u32[]{:S(2)}, u32[]{:S(2)}) collective-permute-start(bf16[227,128]{1,0:T(8,128)(2,1)S(1)} %copy-done.5), channel_id=1, source_target_pairs={{0,16},{16,32},{32,48},{48,64},{64,80},{80,96},{96,112},{1,17},{17... | collective-permute-start | bytes 174344 | tf_op jit(solution)/shard_map/ppermute | solution.py:368
  180.1 1.9 collective-permute-start.13
  182.1 3.5 %collective-permute-done.13.in1 = bf16[227,128]{1,0:T(8,128)(2,1)S(1)} collective-permute-done((bf16[227,128]{1,0:T(8,128)(2,1)S(1)}, bf16[227,128]{1,0:T(8,128)(2,1)S(1)}, u32[]{:S(2)}, u32[]{:S(2)}) %collective-permute-start.13) | collective-permute-done | bytes 58144 | tf_op jit(solution)/shard_map/ppermute | solution.py:369
  185.7 0.6 copy-done.15
  186.3 5.2 %shard_map.263 = bf16[227,2048]{1,0:T(8,128)(2,1)} custom-call(s32[2]{0:T(128)} %pad_add_fusion.flag_ref, s32[1,2048]{1,0:T(1,128)} %order_ref.5, bf16[227,1536]{1,0:T(8,128)(2,1)} %get-tuple-element.88.keep_ref, bf16[227,128]{1,0:T(8,128)(2,1)} %copy-done.14, bf16[227,128]{1,0:T(8,128)(2,1)} %copy-done.15, bf16[227,128]{1,0:T(8,128)(2,1)} %copy-done.12, ...), custom_call_target="tpu_custom_call" | custom-call | flops 5000000000 | bytes 5000000 | tf_op jit(solution)/shard_map/pallas_call | solution.py:468
  191.5 1.2 copy-done.3
  192.6 4.6 %shard_map.264 = (f32[227,512]{1,0:T(8,128)}, f32[512,512]{1,0:T(8,128)}, f32[512,512]{1,0:T(8,128)}, f32[512,512]{1,0:T(8,128)}, f32[256,512]{1,0:T(8,128)}, /*...) custom-call(s32[1]{0:T(128)} %bitcast.2.core_ref, bf16[1536,512]{1,0:T(8,128)(2,1)} %bitcast.9, ...), custom_call_target="tpu_custom_call" | custom-call | flops 5000000000 | bytes 5000000 | tf_op jit(solution)/shard_map/pallas_call | solution.py:484
  (54 shorter events, 0.2 us)
Async XLA Ops:
  3.2 20.0 %collective-permute-start.2 = (bf16[227,128]{1,0:T(8,128)(2,1)}, bf16[227,128]{1,0:T(8,128)(2,1)S(1)}, u32[]{:S(2)}, u32[]{:S(2)}) collective-permute-start(bf16[227,128]{1,0:T(8,128)(2,1)} %get-tuple-element.63), channel_id=1, source_target_pairs={{0,1},{1,2},{2,3},{3,4},{4,5},{5,6},{6,7},{7,8},{8,9},{9,10},{10,1... | collective-permute-start | bytes 174344 | tf_op jit(solution)/shard_map/ppermute | solution.py:370
  5.3 17.9 %collective-permute-start.3 = (bf16[227,128]{1,0:T(8,128)(2,1)}, bf16[227,128]{1,0:T(8,128)(2,1)S(1)}, u32[]{:S(2)}, u32[]{:S(2)}) collective-permute-start(bf16[227,128]{1,0:T(8,128)(2,1)} %get-tuple-element.64), channel_id=1, source_target_pairs={{1,0},{2,1},{3,2},{4,3},{5,4},{6,5},{7,6},{8,7},{9,8},{10,9},{11,1... | collective-permute-start | bytes 174344 | tf_op jit(solution)/shard_map/ppermute | solution.py:371
  9.0 14.2 %collective-permute-start = (bf16[227,128]{1,0:T(8,128)(2,1)}, bf16[227,128]{1,0:T(8,128)(2,1)S(1)}, u32[]{:S(2)}, u32[]{:S(2)}) collective-permute-start(bf16[227,128]{1,0:T(8,128)(2,1)} %get-tuple-element.61.own1), channel_id=1, source_target_pairs={{0,16},{16,32},{32,48},{48,64},{64,80},{80,96},{96,112},{1,17},{17... | collective-permute-start | bytes 174344 | tf_op jit(solution)/shard_map/ppermute | solution.py:368
  13.5 9.7 %collective-permute-start.1 = (bf16[227,128]{1,0:T(8,128)(2,1)}, bf16[227,128]{1,0:T(8,128)(2,1)S(1)}, u32[]{:S(2)}, u32[]{:S(2)}) collective-permute-start(bf16[227,128]{1,0:T(8,128)(2,1)} %get-tuple-element.62.own0), channel_id=1, source_target_pairs={{16,0},{32,16},{48,32},{64,48},{80,64},{96,80},{112,96},{17,1},{33... | collective-permute-start | bytes 174344 | tf_op jit(solution)/shard_map/ppermute | solution.py:369
  23.2 0.6 copy-start.7
  23.2 0.6 copy-start.9
  23.2 0.6 copy-start.10
  23.3 0.6 copy-start.11
  42.4 10.4 %collective-permute-start.4 = (bf16[32,256]{1,0:T(8,128)(2,1)}, bf16[32,256]{1,0:T(8,128)(2,1)S(1)}, u32[]{:S(2)}, u32[]{:S(2)}) collective-permute-start(bf16[32,256]{1,0:T(8,128)(2,1)} %get-tuple-element.70), channel_id=1, source_target_pairs={{0,16},{16,32},{32,48},{48,64},{64,80},{80,96},{96,112},{1,17},{17... | collective-permute-start | bytes 49160 | tf_op jit(solution)/shard_map/ppermute | solution.py:368
  46.1 6.8 %collective-permute-start.5 = (bf16[32,256]{1,0:T(8,128)(2,1)}, bf16[32,256]{1,0:T(8,128)(2,1)S(1)}, u32[]{:S(2)}, u32[]{:S(2)}) collective-permute-start(bf16[32,256]{1,0:T(8,128)(2,1)} %get-tuple-element.71), channel_id=1, source_target_pairs={{16,0},{32,16},{48,32},{64,48},{80,64},{96,80},{112,96},{17,1},{33... | collective-permute-start | bytes 49160 | tf_op jit(solution)/shard_map/ppermute | solution.py:369
  48.0 6.2 %collective-permute-start.6 = (bf16[32,256]{1,0:T(8,128)(2,1)}, bf16[32,256]{1,0:T(8,128)(2,1)S(1)}, u32[]{:S(2)}, u32[]{:S(2)}) collective-permute-start(bf16[32,256]{1,0:T(8,128)(2,1)} %get-tuple-element.72), channel_id=1, source_target_pairs={{0,1},{1,2},{2,3},{3,4},{4,5},{5,6},{6,7},{7,8},{8,9},{9,10},{10,1... | collective-permute-start | bytes 49160 | tf_op jit(solution)/shard_map/ppermute | solution.py:370
  48.1 6.1 %collective-permute-start.7 = (bf16[32,256]{1,0:T(8,128)(2,1)}, bf16[32,256]{1,0:T(8,128)(2,1)S(1)}, u32[]{:S(2)}, u32[]{:S(2)}) collective-permute-start(bf16[32,256]{1,0:T(8,128)(2,1)} %get-tuple-element.73), channel_id=1, source_target_pairs={{1,0},{2,1},{3,2},{4,3},{5,4},{6,5},{7,6},{8,7},{9,8},{10,9},{11,1... | collective-permute-start | bytes 49160 | tf_op jit(solution)/shard_map/ppermute | solution.py:371
  52.9 1.3 copy-start.20
  52.9 1.3 copy-start.21
  54.2 0.6 copy-start.22
  54.2 0.6 copy-start.23
  65.1 15.5 %collective-permute-start.8 = (bf16[32,256]{1,0:T(8,128)(2,1)}, bf16[32,256]{1,0:T(8,128)(2,1)S(1)}, u32[]{:S(2)}, u32[]{:S(2)}) collective-permute-start(bf16[32,256]{1,0:T(8,128)(2,1)} %get-tuple-element.84), channel_id=1, source_target_pairs={{0,16},{16,32},{32,48},{48,64},{64,80},{80,96},{96,112},{1,17},{17... | collective-permute-start | bytes 49160 | tf_op jit(solution)/shard_map/ppermute | solution.py:368
  69.9 10.8 %collective-permute-start.9 = (bf16[32,256]{1,0:T(8,128)(2,1)}, bf16[32,256]{1,0:T(8,128)(2,1)S(1)}, u32[]{:S(2)}, u32[]{:S(2)}) collective-permute-start(bf16[32,256]{1,0:T(8,128)(2,1)} %get-tuple-element.85), channel_id=1, source_target_pairs={{16,0},{32,16},{48,32},{64,48},{80,64},{96,80},{112,96},{17,1},{33... | collective-permute-start | bytes 49160 | tf_op jit(solution)/shard_map/ppermute | solution.py:369
  71.8 8.8 %collective-permute-start.10 = (bf16[32,256]{1,0:T(8,128)(2,1)}, bf16[32,256]{1,0:T(8,128)(2,1)S(1)}, u32[]{:S(2)}, u32[]{:S(2)}) collective-permute-start(bf16[32,256]{1,0:T(8,128)(2,1)} %get-tuple-element.86), channel_id=1, source_target_pairs={{0,1},{1,2},{2,3},{3,4},{4,5},{5,6},{6,7},{7,8},{8,9},{9,10},{10,1... | collective-permute-start | bytes 49160 | tf_op jit(solution)/shard_map/ppermute | solution.py:370
  71.9 8.8 %collective-permute-start.11 = (bf16[32,256]{1,0:T(8,128)(2,1)}, bf16[32,256]{1,0:T(8,128)(2,1)S(1)}, u32[]{:S(2)}, u32[]{:S(2)}) collective-permute-start(bf16[32,256]{1,0:T(8,128)(2,1)} %get-tuple-element.87), channel_id=1, source_target_pairs={{1,0},{2,1},{3,2},{4,3},{5,4},{6,5},{7,6},{8,7},{9,8},{10,9},{11,1... | collective-permute-start | bytes 49160 | tf_op jit(solution)/shard_map/ppermute | solution.py:371
  80.6 25.2 %collective-permute-start.16 = (bf16[640,512]{1,0:T(8,128)(2,1)}, bf16[640,512]{1,0:T(8,128)(2,1)S(1)}, u32[]{:S(2)}, u32[]{:S(2)}) collective-permute-start(bf16[640,512]{1,0:T(8,128)(2,1)} %get-tuple-element.95), channel_id=1, source_target_pairs={{0,16},{16,0},{1,17},{17,1},{2,18},{18,2},{3,19},{19,3},{4,20},{20... | collective-permute-start | bytes 1966088 | tf_op jit(solution)/shard_map/ppermute | solution.py:376
  80.6 0.6 copy-start.16
  80.6 0.6 copy-start.17
  80.7 0.6 copy-start.18
  80.7 0.6 copy-start.19
  81.3 24.5 %copy-start.2 = (bf16[640,512]{1,0:T(8,128)(2,1)S(1)}, bf16[640,512]{1,0:T(8,128)(2,1)}, u32[]{:S(2)}) copy-start(bf16[640,512]{1,0:T(8,128)(2,1)} %get-tuple-element.94) | copy-start | bytes 1966084
  105.2 2.9 %copy-start.1 = (bf16[896,512]{1,0:T(8,128)(2,1)S(1)}, bf16[896,512]{1,0:T(8,128)(2,1)}, u32[]{:S(2)}) copy-start(bf16[896,512]{1,0:T(8,128)(2,1)} %get-tuple-element.96) | copy-start | bytes 2752516
  105.2 2.9 %collective-permute-start.17 = (bf16[896,512]{1,0:T(8,128)(2,1)}, bf16[896,512]{1,0:T(8,128)(2,1)S(1)}, u32[]{:S(2)}, u32[]{:S(2)}) collective-permute-start(bf16[896,512]{1,0:T(8,128)(2,1)} %get-tuple-element.97), channel_id=1, source_target_pairs={{0,16},{16,0},{1,17},{17,1},{2,18},{18,2},{3,19},{19,3},{4,20},{20... | collective-permute-start | bytes 2752520 | tf_op jit(solution)/shard_map/ppermute | solution.py:376
  141.4 31.4 %copy-start.8 = (bf16[227,128]{1,0:T(8,128)(2,1)S(1)}, bf16[227,128]{1,0:T(8,128)(2,1)}, u32[]{:S(2)}) copy-start(bf16[227,128]{1,0:T(8,128)(2,1)} %get-tuple-element.91) | copy-start | bytes 174340
  141.4 31.7 %copy-start.6 = (bf16[227,128]{1,0:T(8,128)(2,1)S(1)}, bf16[227,128]{1,0:T(8,128)(2,1)}, u32[]{:S(2)}) copy-start(bf16[227,128]{1,0:T(8,128)(2,1)} %get-tuple-element.92) | copy-start | bytes 174340
  141.5 36.2 %copy-start.5 = (bf16[227,128]{1,0:T(8,128)(2,1)S(1)}, bf16[227,128]{1,0:T(8,128)(2,1)}, u32[]{:S(2)}) copy-start(bf16[227,128]{1,0:T(8,128)(2,1)} %get-tuple-element.89.own1) | copy-start | bytes 174340
  141.5 38.7 %copy-start.4 = (bf16[227,128]{1,0:T(8,128)(2,1)S(1)}, bf16[227,128]{1,0:T(8,128)(2,1)}, u32[]{:S(2)}) copy-start(bf16[227,128]{1,0:T(8,128)(2,1)} %get-tuple-element.90.own0) | copy-start | bytes 174340
  170.3 21.1 %copy-start = (bf16[64,24,512]{2,1,0:T(8,128)(2,1)}, bf16[64,24,512]{2,1,0:T(8,128)(2,1)S(1)}, u32[]{:S(2)}) copy-start(bf16[64,24,512]{2,1,0:T(8,128)(2,1)S(1)} %all_to_all.11) | copy-start | bytes 4718596
  170.3 21.1 %collective-permute-start.18 = (bf16[1536,512]{1,0:T(8,128)(2,1)S(1)}, bf16[1536,512]{1,0:T(8,128)(2,1)S(1)}, u32[]{:S(2)}, u32[]{:S(2)}) collective-permute-start(bf16[1536,512]{1,0:T(8,128)(2,1)S(1)} %bitcast.8), channel_id=1, source_target_pairs={{0,16},{16,0},{1,17},{17,1},{2,18},{18,2},{3,19},{19,3},{4,20},{20... | collective-permute-start | bytes 4718600 | tf_op jit(solution)/shard_map/ppermute | solution.py:376
  172.9 9.2 %collective-permute-start.14 = (bf16[227,128]{1,0:T(8,128)(2,1)S(1)}, bf16[227,128]{1,0:T(8,128)(2,1)S(1)}, u32[]{:S(2)}, u32[]{:S(2)}) collective-permute-start(bf16[227,128]{1,0:T(8,128)(2,1)S(1)} %copy-done.8), channel_id=1, source_target_pairs={{0,1},{1,2},{2,3},{3,4},{4,5},{5,6},{6,7},{7,8},{8,9},{9,10},{10,1... | collective-permute-start | bytes 174344 | tf_op jit(solution)/shard_map/ppermute | solution.py:370
  173.2 8.9 %collective-permute-start.15 = (bf16[227,128]{1,0:T(8,128)(2,1)S(1)}, bf16[227,128]{1,0:T(8,128)(2,1)S(1)}, u32[]{:S(2)}, u32[]{:S(2)}) collective-permute-start(bf16[227,128]{1,0:T(8,128)(2,1)S(1)} %copy-done.6), channel_id=1, source_target_pairs={{1,0},{2,1},{3,2},{4,3},{5,4},{6,5},{7,6},{8,7},{9,8},{10,9},{11,1... | collective-permute-start | bytes 174344 | tf_op jit(solution)/shard_map/ppermute | solution.py:371
  177.7 4.5 %collective-permute-start.12 = (bf16[227,128]{1,0:T(8,128)(2,1)S(1)}, bf16[227,128]{1,0:T(8,128)(2,1)S(1)}, u32[]{:S(2)}, u32[]{:S(2)}) collective-permute-start(bf16[227,128]{1,0:T(8,128)(2,1)S(1)} %copy-done.5), channel_id=1, source_target_pairs={{0,16},{16,32},{32,48},{48,64},{64,80},{80,96},{96,112},{1,17},{17... | collective-permute-start | bytes 174344 | tf_op jit(solution)/shard_map/ppermute | solution.py:368
  180.1 5.5 %collective-permute-start.13 = (bf16[227,128]{1,0:T(8,128)(2,1)S(1)}, bf16[227,128]{1,0:T(8,128)(2,1)S(1)}, u32[]{:S(2)}, u32[]{:S(2)}) collective-permute-start(bf16[227,128]{1,0:T(8,128)(2,1)S(1)} %copy-done.4), channel_id=1, source_target_pairs={{16,0},{32,16},{48,32},{64,48},{80,64},{96,80},{112,96},{17,1},{33... | collective-permute-start | bytes 174344 | tf_op jit(solution)/shard_map/ppermute | solution.py:369
  182.1 3.6 %copy-start.12 = (bf16[227,128]{1,0:T(8,128)(2,1)}, bf16[227,128]{1,0:T(8,128)(2,1)S(1)}, u32[]{:S(2)}) copy-start(bf16[227,128]{1,0:T(8,128)(2,1)S(1)} %collective-permute-done.14.in2) | copy-start | bytes 174340
  182.1 3.6 %copy-start.13 = (bf16[227,128]{1,0:T(8,128)(2,1)}, bf16[227,128]{1,0:T(8,128)(2,1)S(1)}, u32[]{:S(2)}) copy-start(bf16[227,128]{1,0:T(8,128)(2,1)S(1)} %collective-permute-done.15.in3) | copy-start | bytes 174340
  182.1 3.5 %copy-start.14 = (bf16[227,128]{1,0:T(8,128)(2,1)}, bf16[227,128]{1,0:T(8,128)(2,1)S(1)}, u32[]{:S(2)}) copy-start(bf16[227,128]{1,0:T(8,128)(2,1)S(1)} %collective-permute-done.12.in0) | copy-start | bytes 174340
  185.7 0.6 copy-start.15
  191.5 1.2 copy-start.3

commit v4 on v3

--- a/solution.py
+++ b/solution.py
@@ -16,7 +16,6 @@
 VMEM_LIMIT = 56 * 1024 * 1024
 BAND = ("z", "core")
 PATCH = ("y", "x")
-CHIPS = ("z", "y", "x")
 
 
 def mm(left, right):
@@ -50,6 +49,12 @@
     return parts[0] if len(parts) == 1 else jnp.concatenate(parts, axis=0)
 
 
+def table_by_wide(column, count):
+    wide = jnp.concatenate([column.astype(F32)] * (count // LANES), axis=1)
+    columns = lax.broadcasted_iota(jnp.int32, wide.shape, 1).astype(F32)
+    return jnp.where(wide == columns, 1.0, 0.0).astype(BF16)
+
+
 def silu_both(value):
     sigma = 0.5 * jnp.tanh(0.5 * value) + 0.5
     act = value * sigma
@@ -79,8 +84,29 @@
         out_refs[k][...] = picked[:, k * rim : (k + 1) * rim]
 
 
-def keep_kernel(order_ref, grid_ref, mesh_ref, embed_ref, send_ref, recv_ref, rows_ref, sender_ref, node_ref):
+def keep_kernel(
+    order_ref, src_ref, dst_ref, grid_ref, mesh_ref, embed_ref, send_ref, recv_ref,
+    rows_ref, sender_ref, node_ref, column_ref, row_ref, dst_s,
+):
     keep = rows_ref.shape[1]
+    rows = order_ref.shape[1]
+    for start in range(0, rows, LANES):
+        piece = jnp.broadcast_to(dst_ref[:, start : start + LANES], (LANES, LANES))
+        dst_s[start : start + LANES, :] = jnp.transpose(piece).astype(F32).astype(BF16)
+    first = src_ref[:, 0:rows]
+
+    def sort(i, carry):
+        start = pl.multiple_of(i * ROW_TILE, ROW_TILE)
+        ids = lax.broadcasted_iota(jnp.int32, (ROW_TILE, rows), 0) + start
+        table = jnp.where(ids == first, 1.0, 0.0).astype(BF16)
+        column = mm(table, dst_s[...])
+        column_ref[pl.ds(start, ROW_TILE), :] = column.astype(BF16)
+        for k in range(0, ROW_TILE, LANES):
+            turned = jnp.transpose(column[k : k + LANES, :])
+            row_ref[:, pl.ds(pl.multiple_of(start + k, LANES), LANES)] = turned[0:1, :].astype(jnp.int32)
+        return carry
+
+    lax.fori_loop(0, rows // ROW_TILE, sort, 0)
     node_ref[...] = mm(mesh_ref[...], recv_ref[...]).astype(BF16)
 
     def step(i, carry):
@@ -96,7 +122,7 @@
 
 
 def encode_kernel(
-    flag_ref, src_ref, dst_ref, halo_ref, sender_ref, node_ref, mesh_ref, embed_ref, send_ref, out_w_ref,
+    flag_ref, src_ref, dst_ref, column_ref, row_ref, halo_ref, sender_ref, node_ref, mesh_ref, embed_ref, send_ref, out_w_ref,
     in0, in1, in2, in3, own0, own1,
     rim_ref, slope_ref, gathered_ref, latent_ref, h00, h01, h10, h11,
     table, total,
@@ -119,10 +145,24 @@
         table[keep:rows, :] = mm(embedded, send_ref[...]).astype(BF16)
         total[...] = jnp.zeros_like(total)
 
-    both = jnp.concatenate([table_by_column(src_ref[...], rows), table_by_column(dst_ref[...], nodes)], axis=1)
-    act, slope = silu_both(mm(both, table[...]))
-    slope_ref[...] = slope.astype(BF16)
-    total[...] += mm(table_by_row(dst_ref[...], nodes), act.astype(BF16))
+    def finish(value, by_row):
+        act, slope = silu_both(value)
+        slope_ref[...] = slope.astype(BF16)
+        total[...] += mm(by_row, act.astype(BF16))
+
+    tile = slope_ref.shape[0]
+    early = rows // tile
+
+    @pl.when(step < early)
+    def _():
+        start = pl.multiple_of(step * tile, tile)
+        node = mm(table_by_wide(column_ref[...], nodes), node_ref[...])
+        finish(table[pl.ds(start, tile), :].astype(F32) + node, table_by_row(row_ref[...], nodes))
+
+    @pl.when(step >= early)
+    def _():
+        both = jnp.concatenate([table_by_column(src_ref[...], rows), table_by_column(dst_ref[...], nodes)], axis=1)
+        finish(mm(both, table[...]), table_by_row(dst_ref[...], nodes))
 
     @pl.when(step == pl.num_programs(0) - 1)
     def _():
@@ -246,7 +286,7 @@
 
 
 def encoder_back_kernel(
-    core_ref, src_ref, dst_ref, halo_ref, slope_ref, keep_rows_ref, rim_rows_ref, gathered_ref, mesh_ref,
+    core_ref, src_ref, dst_ref, column_ref, row_ref, halo_ref, slope_ref, keep_rows_ref, rim_rows_ref, gathered_ref, mesh_ref,
     coupled_grad_ref, lower_grad_ref, r0, r1, r2, r3, embed_ref, send_ref, recv_ref, out_w_ref,
     keep_grad_ref, g0, g1, g2, g3, mesh_grad_ref, mine_ref, other_ref,
     grad_embed_ref, grad_send_ref, edge_s, latent_s, nodes_s,
@@ -266,31 +306,46 @@
     gathered_grad = mm_right(latent_grad, out_w_ref[...]).astype(BF16)
     nodes_s[...] = jnp.zeros_like(nodes_s)
 
-    def edges(i, carry):
+    rows = column_ref.shape[0]
+
+    def edge(start, by_column, by_row):
+        grad = mm(by_column, gathered_grad) * slope_ref[pl.ds(start, EDGE_TILE), :].astype(F32)
+        grad = grad.astype(BF16)
+        edge_s[pl.ds(start, EDGE_TILE), :] = grad
+        nodes_s[...] += mm(by_row, grad)
+
+    def first(i, carry):
+        start = pl.multiple_of(i * EDGE_TILE, EDGE_TILE)
+        column = column_ref[pl.ds(start, EDGE_TILE), :]
+        edge(start, table_by_wide(column, nodes), table_by_row(row_ref[:, pl.ds(start, EDGE_TILE)], nodes))
+        return carry
+
+    def later(i, carry):
         start = pl.multiple_of(i * EDGE_TILE, EDGE_TILE)
         dst = dst_ref[:, pl.ds(start, EDGE_TILE)]
-        grad = mm(table_by_column(dst, nodes), gathered_grad) * slope_ref[pl.ds(start, EDGE_TILE), :].astype(F32)
-        grad = grad.astype(BF16)
-        edge_s[pl.ds(start, EDGE_TILE), :] = grad
-        nodes_s[...] += mm(table_by_row(dst, nodes), grad)
-        return carry
-
-    lax.fori_loop(0, src_ref.shape[1] // EDGE_TILE, edges, 0)
+        edge(start, table_by_column(dst, nodes), table_by_row(dst, nodes))
+        return carry
+
+    lax.fori_loop(0, rows // EDGE_TILE, first, 0)
+    lax.fori_loop(rows // EDGE_TILE, src_ref.shape[1] // EDGE_TILE, later, 0)
     node_grad = nodes_s[...].astype(BF16)
     store_halves(core_ref, mine_ref, other_ref, dim, mm_left(mesh_ref[...], node_grad))
     mesh_grad_ref[...] = latent_grad.astype(F32) + mm_right(node_grad, recv_ref[...])
     grad_embed_ref[...] = jnp.zeros_like(grad_embed_ref)
     grad_send_ref[...] = jnp.zeros_like(grad_send_ref)
 
-    def back(rows, start, count):
-        ids = lax.broadcasted_iota(jnp.int32, (count, src_ref.shape[1]), 0) + start
-        table = jnp.where(ids == src_ref[...], 1.0, 0.0).astype(BF16)
-        sender_grad = mm(table, edge_s[...]).astype(BF16)
-        act, slope = silu_both(mm_left(rows, embed_ref[...]))
+    extra = src_ref[:, rows:]
+
+    def back(cols, start, count):
+        ids = lax.broadcasted_iota(jnp.int32, (count, extra.shape[1]), 0) + start
+        table = jnp.where(ids == extra, 1.0, 0.0).astype(BF16)
+        own = edge_s[pl.ds(start, count), :].astype(F32)
+        sender_grad = (own + mm(table, edge_s[rows:, :])).astype(BF16)
+        act, slope = silu_both(mm_left(cols, embed_ref[...]))
         grad_send_ref[...] += mm_left(act.astype(BF16), sender_grad)
         embedded_grad = mm_right(sender_grad, send_ref[...]).astype(BF16)
         embed_grad = (embedded_grad.astype(F32) * slope).astype(BF16)
-        grad_embed_ref[0 : rows.shape[0], :] += mm(rows, embed_grad)
+        grad_embed_ref[0 : cols.shape[0], :] += mm(cols, embed_grad)
         return mm_right(embed_ref[...], embed_grad).astype(BF16)
 
     rim_grad = back(rim_rows_ref[...], keep, 4 * rim)
@@ -398,17 +453,24 @@
     grid_cols = grid_feats.T
     own = call(pick_rim_kernel, [shape((chans, rim), BF16)] * 4, 3)(send_rows, grid_cols)
     arrived = trade(*own)
-    keep_rows, keep_sender, node_part = call(
+    keep_rows, keep_sender, node_part, column, row = call(
         keep_kernel,
-        [shape((chans, keep), BF16), shape((keep, dim), BF16), shape((nodes, dim), BF16)],
-        7,
-    )(send_rows, grid_cols, mesh_feats, w_embed, w_send, w_recv)
+        [
+            shape((chans, keep), BF16), shape((keep, dim), BF16), shape((nodes, dim), BF16),
+            shape((grid_rows, LANES), BF16), shape((1, grid_rows), jnp.int32),
+        ],
+        9,
+        scratch_shapes=[pltpu.VMEM((grid_rows, LANES), BF16)],
+    )(send_rows, enc_src, enc_dst, grid_cols, mesh_feats, w_embed, w_send, w_recv)
 
     def whole(array):
         dims = array.shape
         return pl.BlockSpec(dims, lambda i: (0,) * len(dims))
 
-    tile = pl.BlockSpec((1, EDGE_TILE), lambda i: (0, i))
+    early = grid_rows // EDGE_TILE
+    tile = pl.BlockSpec((1, EDGE_TILE), lambda i: (0, jnp.maximum(i, early)))
+    column_tile = pl.BlockSpec((EDGE_TILE, LANES), lambda i: (jnp.minimum(i, early - 1), 0))
+    row_tile = pl.BlockSpec((1, EDGE_TILE), lambda i: (0, jnp.minimum(i, early - 1)))
     outs = [
         shape((chans, 4 * rim), BF16), shape((edges, dim), BF16), shape((nodes, dim), BF16), shape((nodes, dim), BF16),
     ] + [shape((width, half), BF16)] * 4
@@ -418,12 +480,12 @@
         outs,
         20,
         grid=(edges // EDGE_TILE,),
-        in_specs=[smem, tile, tile] + [whole(x) for x in ins],
+        in_specs=[smem, tile, tile, column_tile, row_tile] + [whole(x) for x in ins],
         out_specs=[
             whole(outs[0]), pl.BlockSpec((EDGE_TILE, dim), lambda i: (i, 0)),
         ] + [whole(x) for x in outs[2:]],
         scratch_shapes=[pltpu.VMEM((grid_rows + nodes, dim), BF16), pltpu.VMEM((nodes, dim), F32)],
-    )(flags, enc_src, enc_dst, *ins)
+    )(flags, enc_src, enc_dst, column, row, *ins)
 
     halos = trade(h00, h01, h10, h11)
     outs = [shape((width, half), BF16)] * 4 + [
@@ -454,13 +516,13 @@
         [shape((chans, keep), BF16)] + [shape((chans, rim), BF16)] * 4 + [shape((nodes, dim), F32)]
         + [shape((b_rows // 2, dim), BF16)] * 2,
         25,
-        in_specs=[smem] + [vmem] * 18,
+        in_specs=[smem] + [vmem] * 20,
         scratch_shapes=[
             pltpu.VMEM((half, dim), F32), pltpu.VMEM((dim, dim), F32),
             pltpu.VMEM((edges, dim), BF16), pltpu.VMEM((nodes, dim), BF16), pltpu.VMEM((nodes, dim), F32),
         ],
     )(
-        core, enc_src, enc_dst, halo_send, slope, keep_rows, rim_rows, gathered, mesh_feats, coupled_grad, lower_grad,
+        core, enc_src, enc_dst, column, row, halo_send, slope, keep_rows, rim_rows, gathered, mesh_feats, coupled_grad, lower_grad,
         *returned, w_embed, w_send, w_recv, w_out,
     )
     b_in = swap_cores(b_other)
@@ -472,14 +534,16 @@
         in_specs=[smem] + [vmem] * 8,
         scratch_shapes=[pltpu.VMEM((chans, grid_rows), BF16)],
     )(flags, send_rows, keep_grad, *back, q0, q1)
-    chips = lax.axis_size(CHIPS)
+    patches = lax.axis_size(PATCH)
     packed = (a_rows + b_rows) // 2
     pair = jnp.concatenate([a_mine.astype(F32) + a_in.astype(F32), b_mine.astype(F32) + b_in.astype(F32)], axis=0)
-    pair = pair.astype(BF16).reshape(chips, packed // chips, dim)
-    parts = lax.all_to_all(pair, CHIPS, 0, 0)
-    total = jnp.sum(parts.astype(F32), axis=0).astype(BF16)
-    parts = jnp.broadcast_to(total[None], parts.shape)
-    mine = lax.all_to_all(parts, CHIPS, 0, 0).reshape(packed, dim)
+    pair = pair.astype(BF16).reshape(patches, packed // patches, dim)
+    parts = lax.all_to_all(pair, PATCH, 0, 0)
+    part = jnp.sum(parts.astype(F32), axis=0).astype(BF16)
+    away = [part] + [lax.ppermute(part, "z", [(i, (i + k) % 4) for i in range(4)]) for k in (1, 2, 3)]
+    away = [piece.astype(F32) for piece in away]
+    total = ((away[0] + away[2]) + (away[1] + away[3])).astype(BF16)
+    mine = lax.all_to_all(jnp.broadcast_to(total[None], parts.shape), PATCH, 0, 0).reshape(packed, dim)
     other = swap_cores(mine)
     totals = call(
         functools.partial(unpack_kernel, a_rows),

time: 198 us -> 190 us (0.960)
  blocking collectives: 61.5 us -> 49.1 us
  starting transfers between devices: 47 us -> 54.5 us
  Pallas kernels: 75.6 us -> 70.9 us
    all_to_all x2, blocking collectives: 61.5 us -> 49.1 us  [the longest x1 24.8 us: body(): parts = lax.all_to_all(pair, PATCH, 0, 0)]
    ppermute x0 -> x3, starting transfers between devices: none -> 6.7 us  [body(): lax.ppermute(part, 'z', [(i, (i + k) % 4) for i in range(4)])]
    pallas_call x1, Pallas kernels: 18.5 us -> 14.4 us  [body(): call(encode_kernel, outs, 20, grid=(edges // EDGE_TILE,), in_specs=[smem,...]
    pallas_call x1, Pallas kernels: 23.9 us -> 20 us  [body(): call(encoder_back_kernel, [shape((chans, keep), BF16)] + [shape((chans, r...]
    ppermute x4, waiting for transfers between devices: 3.53 us -> 0.01 us  [trade(): lax.ppermute(below, BAND, down)]
    pallas_call x1, Pallas kernels: 7.16 us -> 10.5 us  [body(): call(keep_kernel, [shape((chans, keep), BF16), shape((keep, dim), BF16),...]
    ppermute x0 -> x3, waiting for transfers between devices: none -> 2.6 us  [body(): lax.ppermute(part, 'z', [(i, (i + k) % 4) for i in range(4)])]
    ppermute x4, waiting for transfers between devices: 1.32 us -> 3.49 us  [trade(): lax.ppermute(east, PATCH, right)]
  transfers between devices with their start and end apart: 19 -> 22, of which waited for: 3 -> 4; matrix products, arithmetic and copies ran while one was open for 0% -> 0% of each run, Pallas kernels for 20% -> 21%
where the time goes in v4:
time: 190 us; the launch traced here: 189 us
  Pallas kernels  70.9 us (37%)
  starting transfers between devices  54.5 us (29%)
  blocking collectives  49.1 us (26%)
  waiting for transfers between devices  8.25 us (4%)
  local copies, waits for them, and re-layouts  3.77 us (2%)
    all_to_all x1, blocking collectives, body(): parts = lax.all_to_all(pair, PATCH, 0, 0)  24.8 us
    all_to_all x1, blocking collectives, body(): lax.all_to_all(jnp.broadcast_to(total[None], parts.shape), PATCH, 0, 0)  24.3 us
    pallas_call x1, Pallas kernels, body(): call(encoder_back_kernel, [shape((chans, keep), BF16)] + [shape((chans, r...  20 us
    ppermute x4, starting transfers between devices, trade(): lax.ppermute(west, PATCH, left)  18 us
    ppermute x4, starting transfers between devices, trade(): lax.ppermute(above, BAND, up)  16.2 us
    pallas_call x1, Pallas kernels, body(): call(encode_kernel, outs, 20, grid=(edges // EDGE_TILE,), in_specs=[smem,...  14.4 us
    pallas_call x1, Pallas kernels, body(): call(keep_kernel, [shape((chans, keep), BF16), shape((keep, dim), BF16),...  10.5 us
    pallas_call x1, Pallas kernels, body(): call(mesh_kernel, outs, 12, scratch_shapes=[pltpu.VMEM((table_rows + node...  10.3 us
  transfers between devices with their start and end apart: 22, of which 4 were waited for; matrix products, arithmetic and copies ran while one was open for 0% of the time, Pallas kernels for 21%

profile of v4, /device:TPU:1, one launch (start us, length us, event | category | flops | bytes accessed | tf_op | source)
XLA Modules:
  0.0 189.0 jit_solution(7397694642409308341)
XLA Ops:
  0.6 2.6 %shard_map.258 = (bf16[227,128]{1,0:T(8,128)(2,1)}, bf16[227,128]{1,0:T(8,128)(2,1)}, bf16[227,128]{1,0:T(8,128)(2,1)}, bf16[227,128]{1,0:T(8,128)(2,1)}) custom-call(s32[1,2048]{1,0:T(1,128)} %order_ref.5, bf16[227,2048]{1,0:T(8,128)(2,1)} %bitcast.10), custom_call_target="tpu_custom_call" | custom-call | flops 3000000000 | bytes 3000000 | tf_op jit(solution)/shard_map/pallas_call | solution.py:454
  3.2 4.9 %collective-permute-start = (bf16[227,128]{1,0:T(8,128)(2,1)}, bf16[227,128]{1,0:T(8,128)(2,1)S(1)}, u32[]{:S(2)}, u32[]{:S(2)}) collective-permute-start(bf16[227,128]{1,0:T(8,128)(2,1)} %get-tuple-element.65.own1), channel_id=1, source_target_pairs={{0,16},{16,32},{32,48},{48,64},{64,80},{80,96},{96,112},{1,17},{17... | collective-permute-start | bytes 174344 | tf_op jit(solution)/shard_map/ppermute | solution.py:423
  8.2 1.9 %collective-permute-start.1 = (bf16[227,128]{1,0:T(8,128)(2,1)}, bf16[227,128]{1,0:T(8,128)(2,1)S(1)}, u32[]{:S(2)}, u32[]{:S(2)}) collective-permute-start(bf16[227,128]{1,0:T(8,128)(2,1)} %get-tuple-element.66.own0), channel_id=1, source_target_pairs={{16,0},{32,16},{48,32},{64,48},{80,64},{96,80},{112,96},{17,1},{33... | collective-permute-start | bytes 174344 | tf_op jit(solution)/shard_map/ppermute | solution.py:424
  10.1 1.3 collective-permute-start.2
  11.4 3.8 %collective-permute-start.3 = (bf16[227,128]{1,0:T(8,128)(2,1)}, bf16[227,128]{1,0:T(8,128)(2,1)S(1)}, u32[]{:S(2)}, u32[]{:S(2)}) collective-permute-start(bf16[227,128]{1,0:T(8,128)(2,1)} %get-tuple-element.68), channel_id=1, source_target_pairs={{1,0},{2,1},{3,2},{4,3},{5,4},{6,5},{7,6},{8,7},{9,8},{10,9},{11,1... | collective-permute-start | bytes 174344 | tf_op jit(solution)/shard_map/ppermute | solution.py:426
  15.2 10.5 %shard_map.257 = (bf16[227,1536]{1,0:T(8,128)(2,1)}, bf16[1536,512]{1,0:T(8,128)(2,1)}, bf16[256,512]{1,0:T(8,128)(2,1)}, bf16[2048,128]{1,0:T(8,128)(2,1)}, s32[1,2048]{1,0:T(1,128)}) custom-call(s32[1,2048]{1,0:T(1,128)} %order_ref.5, s32[1,4096]{1,0:T(1,128)} %src_ref.7, s32[1,4096]{1,0:T(1,128)} %dst_ref.7, bf16[227,2048]{1,0:T(8,128)(2,1)} %bitcast.11, ...), custom_call_target="tpu_custom_call" | custom-call | flops 8999999488 | bytes 9000000 | tf_op jit(solution)/shard_map/pallas_call | solution.py:456
  25.7 0.6 pad_add_fusion.flag_ref
  26.3 0.6 copy-done.8
  27.0 14.4 %shard_map.259 = (bf16[227,512]{1,0:T(8,128)(2,1)}, bf16[4096,512]{1,0:T(8,128)(2,1)}, bf16[256,512]{1,0:T(8,128)(2,1)}, bf16[256,512]{1,0:T(8,128)(2,1)}, bf16[...) custom-call(s32[2]{0:T(128)} %pad_add_fusion.flag_ref, ...), custom_call_target="tpu_custom_call" | custom-call | flops 20000000000 | bytes 20000000 | tf_op jit(solution)/shard_map/pallas_call | solution.py:478
  41.4 4.0 %collective-permute-start.4 = (bf16[32,256]{1,0:T(8,128)(2,1)}, bf16[32,256]{1,0:T(8,128)(2,1)S(1)}, u32[]{:S(2)}, u32[]{:S(2)}) collective-permute-start(bf16[32,256]{1,0:T(8,128)(2,1)} %get-tuple-element.74), channel_id=1, source_target_pairs={{0,16},{16,32},{32,48},{48,64},{64,80},{80,96},{96,112},{1,17},{17... | collective-permute-start | bytes 49160 | tf_op jit(solution)/shard_map/ppermute | solution.py:423
  45.3 1.9 %collective-permute-start.5 = (bf16[32,256]{1,0:T(8,128)(2,1)}, bf16[32,256]{1,0:T(8,128)(2,1)S(1)}, u32[]{:S(2)}, u32[]{:S(2)}) collective-permute-start(bf16[32,256]{1,0:T(8,128)(2,1)} %get-tuple-element.75), channel_id=1, source_target_pairs={{16,0},{32,16},{48,32},{64,48},{80,64},{96,80},{112,96},{17,1},{33... | collective-permute-start | bytes 49160 | tf_op jit(solution)/shard_map/ppermute | solution.py:424
  47.3 0.1 collective-permute-start.6
  47.4 4.8 %collective-permute-start.7 = (bf16[32,256]{1,0:T(8,128)(2,1)}, bf16[32,256]{1,0:T(8,128)(2,1)S(1)}, u32[]{:S(2)}, u32[]{:S(2)}) collective-permute-start(bf16[32,256]{1,0:T(8,128)(2,1)} %get-tuple-element.77), channel_id=1, source_target_pairs={{1,0},{2,1},{3,2},{4,3},{5,4},{6,5},{7,6},{8,7},{9,8},{10,9},{11,1... | collective-permute-start | bytes 49160 | tf_op jit(solution)/shard_map/ppermute | solution.py:426
  52.1 1.3 collective-permute-done.6.b2
  53.5 0.6 copy-done.22
  54.1 10.3 %shard_map.260 = (bf16[32,256]{1,0:T(8,128)(2,1)}, bf16[32,256]{1,0:T(8,128)(2,1)}, bf16[32,256]{1,0:T(8,128)(2,1)}, bf16[32,256]{1,0:T(8,128)(2,1)}, bf16[256,2...) custom-call(s32[1,2048]{1,0:T(1,128)} %src_ref.6, ...), custom_call_target="tpu_custom_call" | custom-call | flops 12000000000 | bytes 12000000 | tf_op jit(solution)/shard_map/pallas_call | solution.py:496
  64.3 0.1 collective-permute-start.10
  64.4 4.8 %collective-permute-start.11 = (bf16[32,256]{1,0:T(8,128)(2,1)}, bf16[32,256]{1,0:T(8,128)(2,1)S(1)}, u32[]{:S(2)}, u32[]{:S(2)}) collective-permute-start(bf16[32,256]{1,0:T(8,128)(2,1)} %get-tuple-element.91), channel_id=1, source_target_pairs={{1,0},{2,1},{3,2},{4,3},{5,4},{6,5},{7,6},{8,7},{9,8},{10,9},{11,1... | collective-permute-start | bytes 49160 | tf_op jit(solution)/shard_map/ppermute | solution.py:426
  69.3 5.3 %collective-permute-start.8 = (bf16[32,256]{1,0:T(8,128)(2,1)}, bf16[32,256]{1,0:T(8,128)(2,1)S(1)}, u32[]{:S(2)}, u32[]{:S(2)}) collective-permute-start(bf16[32,256]{1,0:T(8,128)(2,1)} %get-tuple-element.88), channel_id=1, source_target_pairs={{0,16},{16,32},{32,48},{48,64},{64,80},{80,96},{96,112},{1,17},{17... | collective-permute-start | bytes 49160 | tf_op jit(solution)/shard_map/ppermute | solution.py:423
  74.6 1.9 %collective-permute-start.9 = (bf16[32,256]{1,0:T(8,128)(2,1)}, bf16[32,256]{1,0:T(8,128)(2,1)S(1)}, u32[]{:S(2)}, u32[]{:S(2)}) collective-permute-start(bf16[32,256]{1,0:T(8,128)(2,1)} %get-tuple-element.89), channel_id=1, source_target_pairs={{16,0},{32,16},{48,32},{64,48},{80,64},{96,80},{112,96},{17,1},{33... | collective-permute-start | bytes 49160 | tf_op jit(solution)/shard_map/ppermute | solution.py:424
  76.5 3.4 %shard_map.261 = (bf16[640,512]{1,0:T(8,128)(2,1)}, bf16[640,512]{1,0:T(8,128)(2,1)}) custom-call(s32[1]{0:T(128)} %bitcast.2.core_ref, bf16[384,256]{1,0:T(8,128)(2,1)} %get-tuple-element.80.halo_table_ref, bf16[640,512]{1,0:T(8,128)(2,1)} %get-tuple-element.81.ends_ref, bf16[256,512]{1,0:T(8,128)(2,1)} %get-tuple-element.82.summed_ref, ...), custom_call_target="tpu_custom_call" | custom-call | flops 4000000000 | bytes 4000000 | tf_op jit(solution)/shard_map/pallas_call | solution.py:507
  80.0 0.5 copy-done.16
  80.6 0.0 copy-done.18
  80.6 20.0 %shard_map.262 = (bf16[227,1536]{1,0:T(8,128)(2,1)}, bf16[227,128]{1,0:T(8,128)(2,1)}, bf16[227,128]{1,0:T(8,128)(2,1)}, bf16[227,128]{1,0:T(8,128)(2,1)}, bf16[...) custom-call(s32[1]{0:T(128)} %bitcast.2.core_ref, ...), custom_call_target="tpu_custom_call" | custom-call | flops 24999999488 | bytes 25000000 | tf_op jit(solution)/shard_map/pallas_call | solution.py:514
  100.6 0.6 collective-permute-start.17
  101.2 0.2 add_convert_fusion.1
  101.4 2.1 %collective-permute-done.17 = bf16[896,512]{1,0:T(8,128)(2,1)S(1)} collective-permute-done((bf16[896,512]{1,0:T(8,128)(2,1)}, bf16[896,512]{1,0:T(8,128)(2,1)S(1)}, u32[]{:S(2)}, u32[]{:S(2)}) %collective-permute-start.17) | collective-permute-done | bytes 917536 | tf_op jit(solution)/shard_map/ppermute | solution.py:431
  103.5 0.3 add_convert_fusion
  103.8 0.1 pad_maximum_fusion
  103.9 24.8 %all_to_all.10 = bf16[16,96,512]{2,1,0:T(8,128)(2,1)S(1)} all-to-all(bf16[16,96,512]{2,1,0:T(8,128)(2,1)S(1)} %bitcast.7), channel_id=1, replica_groups=mesh['z'=4,'core'=2,'y'=4,'x'=4] {'y','x'}, dimensions={0} | all-to-all | bytes 3145728 | tf_op jit(solution)/shard_map/all_to_all | solution.py:541
  128.7 0.2 reduce_sum.12
  128.9 4.0 %collective-permute-start.18 = (bf16[96,512]{1,0:T(8,128)(2,1)S(1)}, bf16[96,512]{1,0:T(8,128)(2,1)S(1)}, u32[]{:S(2)}, u32[]{:S(2)}) collective-permute-start(bf16[96,512]{1,0:T(8,128)(2,1)S(1)} %reduce_sum.12), channel_id=1, source_target_pairs={{0,64},{32,96},{64,0},{96,32},{1,65},{33,97},{65,1},{97,33},{2,66}... | collective-permute-start | bytes 294920 | tf_op jit(solution)/shard_map/ppermute | solution.py:543
  132.9 0.8 collective-permute-start.19
  133.7 1.9 %collective-permute-start.20 = (bf16[96,512]{1,0:T(8,128)(2,1)S(1)}, bf16[96,512]{1,0:T(8,128)(2,1)S(1)}, u32[]{:S(2)}, u32[]{:S(2)}) collective-permute-start(bf16[96,512]{1,0:T(8,128)(2,1)S(1)} %reduce_sum.12), channel_id=1, source_target_pairs={{0,96},{32,0},{64,32},{96,64},{1,97},{33,1},{65,33},{97,65},{2,98}... | collective-permute-start | bytes 294920 | tf_op jit(solution)/shard_map/ppermute | solution.py:543
  135.6 2.6 %collective-permute-done.19 = bf16[96,512]{1,0:T(8,128)(2,1)S(1)} collective-permute-done((bf16[96,512]{1,0:T(8,128)(2,1)S(1)}, bf16[96,512]{1,0:T(8,128)(2,1)S(1)}, u32[]{:S(2)}, u32[]{:S(2)}) %collective-permute-start.19) | collective-permute-done | bytes 98336 | tf_op jit(solution)/shard_map/ppermute | solution.py:543
  138.2 0.1 add_convert_fusion.2
  138.3 0.1 broadcast_in_dim.2
  138.5 24.3 %all_to_all.11 = bf16[16,96,512]{2,1,0:T(8,128)(2,1)S(1)} all-to-all(bf16[16,96,512]{2,1,0:T(8,128)(2,1)S(1)} %broadcast_in_dim.2), channel_id=1, replica_groups=mesh['z'=4,'core'=2,'y'=4,'x'=4] {'y','x'}, dimensions={0} | all-to-all | bytes 3145728 | tf_op jit(solution)/shard_map/all_to_all | solution.py:546
  162.8 3.2 %collective-permute-start.21 = (bf16[1536,512]{1,0:T(8,128)(2,1)S(1)}, bf16[1536,512]{1,0:T(8,128)(2,1)S(1)}, u32[]{:S(2)}, u32[]{:S(2)}) collective-permute-start(bf16[1536,512]{1,0:T(8,128)(2,1)S(1)} %bitcast.8), channel_id=1, source_target_pairs={{0,16},{16,0},{1,17},{17,1},{2,18},{18,2},{3,19},{19,3},{4,20},{20... | collective-permute-start | bytes 4718600 | tf_op jit(solution)/shard_map/ppermute | solution.py:431
  166.0 1.9 %collective-permute-start.12 = (bf16[227,128]{1,0:T(8,128)(2,1)S(1)}, bf16[227,128]{1,0:T(8,128)(2,1)S(1)}, u32[]{:S(2)}, u32[]{:S(2)}) collective-permute-start(bf16[227,128]{1,0:T(8,128)(2,1)S(1)} %copy-done.5), channel_id=1, source_target_pairs={{0,16},{16,32},{32,48},{48,64},{64,80},{80,96},{96,112},{1,17},{17... | collective-permute-start | bytes 174344 | tf_op jit(solution)/shard_map/ppermute | solution.py:423
  167.9 2.4 %collective-permute-start.13 = (bf16[227,128]{1,0:T(8,128)(2,1)S(1)}, bf16[227,128]{1,0:T(8,128)(2,1)S(1)}, u32[]{:S(2)}, u32[]{:S(2)}) collective-permute-start(bf16[227,128]{1,0:T(8,128)(2,1)S(1)} %copy-done.4), channel_id=1, source_target_pairs={{16,0},{32,16},{48,32},{64,48},{80,64},{96,80},{112,96},{17,1},{33... | collective-permute-start | bytes 174344 | tf_op jit(solution)/shard_map/ppermute | solution.py:424
  170.4 0.3 collective-permute-start.14
  170.7 4.5 %collective-permute-start.15 = (bf16[227,128]{1,0:T(8,128)(2,1)S(1)}, bf16[227,128]{1,0:T(8,128)(2,1)S(1)}, u32[]{:S(2)}, u32[]{:S(2)}) collective-permute-start(bf16[227,128]{1,0:T(8,128)(2,1)S(1)} %copy-done.6), channel_id=1, source_target_pairs={{1,0},{2,1},{3,2},{4,3},{5,4},{6,5},{7,6},{8,7},{9,8},{10,9},{11,1... | collective-permute-start | bytes 174344 | tf_op jit(solution)/shard_map/ppermute | solution.py:426
  175.2 2.2 %collective-permute-done.14.in2 = bf16[227,128]{1,0:T(8,128)(2,1)S(1)} collective-permute-done((bf16[227,128]{1,0:T(8,128)(2,1)S(1)}, bf16[227,128]{1,0:T(8,128)(2,1)S(1)}, u32[]{:S(2)}, u32[]{:S(2)}) %collective-permute-start.14) | collective-permute-done | bytes 58144 | tf_op jit(solution)/shard_map/ppermute | solution.py:425
  177.4 0.6 copy-done.14
  178.1 5.2 %shard_map.263 = bf16[227,2048]{1,0:T(8,128)(2,1)} custom-call(s32[2]{0:T(128)} %pad_add_fusion.flag_ref, s32[1,2048]{1,0:T(1,128)} %order_ref.5, bf16[227,1536]{1,0:T(8,128)(2,1)} %get-tuple-element.92.keep_ref, bf16[227,128]{1,0:T(8,128)(2,1)} %copy-done.12, bf16[227,128]{1,0:T(8,128)(2,1)} %copy-done.13, bf16[227,128]{1,0:T(8,128)(2,1)} %copy-done.14, ...), custom_call_target="tpu_custom_call" | custom-call | flops 5000000000 | bytes 5000000 | tf_op jit(solution)/shard_map/pallas_call | solution.py:530
  183.3 1.1 copy-done.3
  184.4 4.6 %shard_map.264 = (f32[227,512]{1,0:T(8,128)}, f32[512,512]{1,0:T(8,128)}, f32[512,512]{1,0:T(8,128)}, f32[512,512]{1,0:T(8,128)}, f32[256,512]{1,0:T(8,128)}, /*...) custom-call(s32[1]{0:T(128)} %bitcast.2.core_ref, bf16[1536,512]{1,0:T(8,128)(2,1)} %bitcast.9, ...), custom_call_target="tpu_custom_call" | custom-call | flops 5000000000 | bytes 5000000 | tf_op jit(solution)/shard_map/pallas_call | solution.py:548
  (61 shorter events, 0.3 us)
Async XLA Ops:
  3.2 23.0 %collective-permute-start = (bf16[227,128]{1,0:T(8,128)(2,1)}, bf16[227,128]{1,0:T(8,128)(2,1)S(1)}, u32[]{:S(2)}, u32[]{:S(2)}) collective-permute-start(bf16[227,128]{1,0:T(8,128)(2,1)} %get-tuple-element.65.own1), channel_id=1, source_target_pairs={{0,16},{16,32},{32,48},{48,64},{64,80},{80,96},{96,112},{1,17},{17... | collective-permute-start | bytes 174344 | tf_op jit(solution)/shard_map/ppermute | solution.py:423
  8.2 18.1 %collective-permute-start.1 = (bf16[227,128]{1,0:T(8,128)(2,1)}, bf16[227,128]{1,0:T(8,128)(2,1)S(1)}, u32[]{:S(2)}, u32[]{:S(2)}) collective-permute-start(bf16[227,128]{1,0:T(8,128)(2,1)} %get-tuple-element.66.own0), channel_id=1, source_target_pairs={{16,0},{32,16},{48,32},{64,48},{80,64},{96,80},{112,96},{17,1},{33... | collective-permute-start | bytes 174344 | tf_op jit(solution)/shard_map/ppermute | solution.py:424
  10.1 16.2 %collective-permute-start.2 = (bf16[227,128]{1,0:T(8,128)(2,1)}, bf16[227,128]{1,0:T(8,128)(2,1)S(1)}, u32[]{:S(2)}, u32[]{:S(2)}) collective-permute-start(bf16[227,128]{1,0:T(8,128)(2,1)} %get-tuple-element.67), channel_id=1, source_target_pairs={{0,1},{1,2},{2,3},{3,4},{4,5},{5,6},{6,7},{7,8},{8,9},{9,10},{10,1... | collective-permute-start | bytes 174344 | tf_op jit(solution)/shard_map/ppermute | solution.py:425
  11.4 14.9 %collective-permute-start.3 = (bf16[227,128]{1,0:T(8,128)(2,1)}, bf16[227,128]{1,0:T(8,128)(2,1)S(1)}, u32[]{:S(2)}, u32[]{:S(2)}) collective-permute-start(bf16[227,128]{1,0:T(8,128)(2,1)} %get-tuple-element.68), channel_id=1, source_target_pairs={{1,0},{2,1},{3,2},{4,3},{5,4},{6,5},{7,6},{8,7},{9,8},{10,9},{11,1... | collective-permute-start | bytes 174344 | tf_op jit(solution)/shard_map/ppermute | solution.py:426
  26.3 0.6 copy-start.8
  26.3 0.6 copy-start.9
  26.3 0.6 copy-start.10
  26.3 0.6 copy-start.11
  41.4 10.8 %collective-permute-start.4 = (bf16[32,256]{1,0:T(8,128)(2,1)}, bf16[32,256]{1,0:T(8,128)(2,1)S(1)}, u32[]{:S(2)}, u32[]{:S(2)}) collective-permute-start(bf16[32,256]{1,0:T(8,128)(2,1)} %get-tuple-element.74), channel_id=1, source_target_pairs={{0,16},{16,32},{32,48},{48,64},{64,80},{80,96},{96,112},{1,17},{17... | collective-permute-start | bytes 49160 | tf_op jit(solution)/shard_map/ppermute | solution.py:423
  45.3 6.8 %collective-permute-start.5 = (bf16[32,256]{1,0:T(8,128)(2,1)}, bf16[32,256]{1,0:T(8,128)(2,1)S(1)}, u32[]{:S(2)}, u32[]{:S(2)}) collective-permute-start(bf16[32,256]{1,0:T(8,128)(2,1)} %get-tuple-element.75), channel_id=1, source_target_pairs={{16,0},{32,16},{48,32},{64,48},{80,64},{96,80},{112,96},{17,1},{33... | collective-permute-start | bytes 49160 | tf_op jit(solution)/shard_map/ppermute | solution.py:424
  47.3 6.2 %collective-permute-start.6 = (bf16[32,256]{1,0:T(8,128)(2,1)}, bf16[32,256]{1,0:T(8,128)(2,1)S(1)}, u32[]{:S(2)}, u32[]{:S(2)}) collective-permute-start(bf16[32,256]{1,0:T(8,128)(2,1)} %get-tuple-element.76), channel_id=1, source_target_pairs={{0,1},{1,2},{2,3},{3,4},{4,5},{5,6},{6,7},{7,8},{8,9},{9,10},{10,1... | collective-permute-start | bytes 49160 | tf_op jit(solution)/shard_map/ppermute | solution.py:425
  47.4 6.1 %collective-permute-start.7 = (bf16[32,256]{1,0:T(8,128)(2,1)}, bf16[32,256]{1,0:T(8,128)(2,1)S(1)}, u32[]{:S(2)}, u32[]{:S(2)}) collective-permute-start(bf16[32,256]{1,0:T(8,128)(2,1)} %get-tuple-element.77), channel_id=1, source_target_pairs={{1,0},{2,1},{3,2},{4,3},{5,4},{6,5},{7,6},{8,7},{9,8},{10,9},{11,1... | collective-permute-start | bytes 49160 | tf_op jit(solution)/shard_map/ppermute | solution.py:426
  52.1 1.3 copy-start.20
  52.1 1.3 copy-start.21
  53.5 0.6 copy-start.22
  53.5 0.6 copy-start.23
  64.3 15.6 %collective-permute-start.10 = (bf16[32,256]{1,0:T(8,128)(2,1)}, bf16[32,256]{1,0:T(8,128)(2,1)S(1)}, u32[]{:S(2)}, u32[]{:S(2)}) collective-permute-start(bf16[32,256]{1,0:T(8,128)(2,1)} %get-tuple-element.90), channel_id=1, source_target_pairs={{0,1},{1,2},{2,3},{3,4},{4,5},{5,6},{6,7},{7,8},{8,9},{9,10},{10,1... | collective-permute-start | bytes 49160 | tf_op jit(solution)/shard_map/ppermute | solution.py:425
  64.4 15.6 %collective-permute-start.11 = (bf16[32,256]{1,0:T(8,128)(2,1)}, bf16[32,256]{1,0:T(8,128)(2,1)S(1)}, u32[]{:S(2)}, u32[]{:S(2)}) collective-permute-start(bf16[32,256]{1,0:T(8,128)(2,1)} %get-tuple-element.91), channel_id=1, source_target_pairs={{1,0},{2,1},{3,2},{4,3},{5,4},{6,5},{7,6},{8,7},{9,8},{10,9},{11,1... | collective-permute-start | bytes 49160 | tf_op jit(solution)/shard_map/ppermute | solution.py:426
  69.3 10.7 %collective-permute-start.8 = (bf16[32,256]{1,0:T(8,128)(2,1)}, bf16[32,256]{1,0:T(8,128)(2,1)S(1)}, u32[]{:S(2)}, u32[]{:S(2)}) collective-permute-start(bf16[32,256]{1,0:T(8,128)(2,1)} %get-tuple-element.88), channel_id=1, source_target_pairs={{0,16},{16,32},{32,48},{48,64},{64,80},{80,96},{96,112},{1,17},{17... | collective-permute-start | bytes 49160 | tf_op jit(solution)/shard_map/ppermute | solution.py:423
  74.6 5.4 %collective-permute-start.9 = (bf16[32,256]{1,0:T(8,128)(2,1)}, bf16[32,256]{1,0:T(8,128)(2,1)S(1)}, u32[]{:S(2)}, u32[]{:S(2)}) collective-permute-start(bf16[32,256]{1,0:T(8,128)(2,1)} %get-tuple-element.89), channel_id=1, source_target_pairs={{16,0},{32,16},{48,32},{64,48},{80,64},{96,80},{112,96},{17,1},{33... | collective-permute-start | bytes 49160 | tf_op jit(solution)/shard_map/ppermute | solution.py:424
  79.9 21.2 %collective-permute-start.16 = (bf16[640,512]{1,0:T(8,128)(2,1)}, bf16[640,512]{1,0:T(8,128)(2,1)S(1)}, u32[]{:S(2)}, u32[]{:S(2)}) collective-permute-start(bf16[640,512]{1,0:T(8,128)(2,1)} %get-tuple-element.99), channel_id=1, source_target_pairs={{0,16},{16,0},{1,17},{17,1},{2,18},{18,2},{3,19},{19,3},{4,20},{20... | collective-permute-start | bytes 1966088 | tf_op jit(solution)/shard_map/ppermute | solution.py:431
  80.0 0.6 copy-start.16
  80.0 0.6 copy-start.17
  80.0 0.6 copy-start.18
  80.0 0.6 copy-start.19
  80.6 20.6 %copy-start.2 = (bf16[640,512]{1,0:T(8,128)(2,1)S(1)}, bf16[640,512]{1,0:T(8,128)(2,1)}, u32[]{:S(2)}) copy-start(bf16[640,512]{1,0:T(8,128)(2,1)} %get-tuple-element.98) | copy-start | bytes 1966084
  100.6 2.9 %copy-start.1 = (bf16[896,512]{1,0:T(8,128)(2,1)S(1)}, bf16[896,512]{1,0:T(8,128)(2,1)}, u32[]{:S(2)}) copy-start(bf16[896,512]{1,0:T(8,128)(2,1)} %get-tuple-element.100) | copy-start | bytes 2752516
  100.6 2.9 %collective-permute-start.17 = (bf16[896,512]{1,0:T(8,128)(2,1)}, bf16[896,512]{1,0:T(8,128)(2,1)S(1)}, u32[]{:S(2)}, u32[]{:S(2)}) collective-permute-start(bf16[896,512]{1,0:T(8,128)(2,1)} %get-tuple-element.101), channel_id=1, source_target_pairs={{0,16},{16,0},{1,17},{17,1},{2,18},{18,2},{3,19},{19,3},{4,20},{20... | collective-permute-start | bytes 2752520 | tf_op jit(solution)/shard_map/ppermute | solution.py:431
  128.9 6.7 %collective-permute-start.18 = (bf16[96,512]{1,0:T(8,128)(2,1)S(1)}, bf16[96,512]{1,0:T(8,128)(2,1)S(1)}, u32[]{:S(2)}, u32[]{:S(2)}) collective-permute-start(bf16[96,512]{1,0:T(8,128)(2,1)S(1)} %reduce_sum.12), channel_id=1, source_target_pairs={{0,64},{32,96},{64,0},{96,32},{1,65},{33,97},{65,1},{97,33},{2,66}... | collective-permute-start | bytes 294920 | tf_op jit(solution)/shard_map/ppermute | solution.py:543
  132.9 5.3 %collective-permute-start.19 = (bf16[96,512]{1,0:T(8,128)(2,1)S(1)}, bf16[96,512]{1,0:T(8,128)(2,1)S(1)}, u32[]{:S(2)}, u32[]{:S(2)}) collective-permute-start(bf16[96,512]{1,0:T(8,128)(2,1)S(1)} %reduce_sum.12), channel_id=1, source_target_pairs={{0,32},{32,64},{64,96},{96,0},{1,33},{33,65},{65,97},{97,1},{2,34}... | collective-permute-start | bytes 294920 | tf_op jit(solution)/shard_map/ppermute | solution.py:543
  133.7 4.5 %collective-permute-start.20 = (bf16[96,512]{1,0:T(8,128)(2,1)S(1)}, bf16[96,512]{1,0:T(8,128)(2,1)S(1)}, u32[]{:S(2)}, u32[]{:S(2)}) collective-permute-start(bf16[96,512]{1,0:T(8,128)(2,1)S(1)} %reduce_sum.12), channel_id=1, source_target_pairs={{0,96},{32,0},{64,32},{96,64},{1,97},{33,1},{65,33},{97,65},{2,98}... | collective-permute-start | bytes 294920 | tf_op jit(solution)/shard_map/ppermute | solution.py:543
  138.4 27.6 %copy-start.5 = (bf16[227,128]{1,0:T(8,128)(2,1)S(1)}, bf16[227,128]{1,0:T(8,128)(2,1)}, u32[]{:S(2)}) copy-start(bf16[227,128]{1,0:T(8,128)(2,1)} %get-tuple-element.93.own1) | copy-start | bytes 174340
  138.4 29.5 %copy-start.4 = (bf16[227,128]{1,0:T(8,128)(2,1)S(1)}, bf16[227,128]{1,0:T(8,128)(2,1)}, u32[]{:S(2)}) copy-start(bf16[227,128]{1,0:T(8,128)(2,1)} %get-tuple-element.94.own0) | copy-start | bytes 174340
  138.4 31.9 %copy-start.7 = (bf16[227,128]{1,0:T(8,128)(2,1)S(1)}, bf16[227,128]{1,0:T(8,128)(2,1)}, u32[]{:S(2)}) copy-start(bf16[227,128]{1,0:T(8,128)(2,1)} %get-tuple-element.95) | copy-start | bytes 174340
  138.4 32.2 %copy-start.6 = (bf16[227,128]{1,0:T(8,128)(2,1)S(1)}, bf16[227,128]{1,0:T(8,128)(2,1)}, u32[]{:S(2)}) copy-start(bf16[227,128]{1,0:T(8,128)(2,1)} %get-tuple-element.96) | copy-start | bytes 174340
  162.8 20.5 %copy-start = (bf16[16,96,512]{2,1,0:T(8,128)(2,1)}, bf16[16,96,512]{2,1,0:T(8,128)(2,1)S(1)}, u32[]{:S(2)}) copy-start(bf16[16,96,512]{2,1,0:T(8,128)(2,1)S(1)} %all_to_all.11) | copy-start | bytes 4718596
  162.8 20.5 %collective-permute-start.21 = (bf16[1536,512]{1,0:T(8,128)(2,1)S(1)}, bf16[1536,512]{1,0:T(8,128)(2,1)S(1)}, u32[]{:S(2)}, u32[]{:S(2)}) collective-permute-start(bf16[1536,512]{1,0:T(8,128)(2,1)S(1)} %bitcast.8), channel_id=1, source_target_pairs={{0,16},{16,0},{1,17},{17,1},{2,18},{18,2},{3,19},{19,3},{4,20},{20... | collective-permute-start | bytes 4718600 | tf_op jit(solution)/shard_map/ppermute | solution.py:431
  166.0 9.2 %collective-permute-start.12 = (bf16[227,128]{1,0:T(8,128)(2,1)S(1)}, bf16[227,128]{1,0:T(8,128)(2,1)S(1)}, u32[]{:S(2)}, u32[]{:S(2)}) collective-permute-start(bf16[227,128]{1,0:T(8,128)(2,1)S(1)} %copy-done.5), channel_id=1, source_target_pairs={{0,16},{16,32},{32,48},{48,64},{64,80},{80,96},{96,112},{1,17},{17... | collective-permute-start | bytes 174344 | tf_op jit(solution)/shard_map/ppermute | solution.py:423
  167.9 7.3 %collective-permute-start.13 = (bf16[227,128]{1,0:T(8,128)(2,1)S(1)}, bf16[227,128]{1,0:T(8,128)(2,1)S(1)}, u32[]{:S(2)}, u32[]{:S(2)}) collective-permute-start(bf16[227,128]{1,0:T(8,128)(2,1)S(1)} %copy-done.4), channel_id=1, source_target_pairs={{16,0},{32,16},{48,32},{64,48},{80,64},{96,80},{112,96},{17,1},{33... | collective-permute-start | bytes 174344 | tf_op jit(solution)/shard_map/ppermute | solution.py:424
  170.4 7.1 %collective-permute-start.14 = (bf16[227,128]{1,0:T(8,128)(2,1)S(1)}, bf16[227,128]{1,0:T(8,128)(2,1)S(1)}, u32[]{:S(2)}, u32[]{:S(2)}) collective-permute-start(bf16[227,128]{1,0:T(8,128)(2,1)S(1)} %copy-done.7), channel_id=1, source_target_pairs={{0,1},{1,2},{2,3},{3,4},{4,5},{5,6},{6,7},{7,8},{8,9},{9,10},{10,1... | collective-permute-start | bytes 174344 | tf_op jit(solution)/shard_map/ppermute | solution.py:425
  170.7 6.7 %collective-permute-start.15 = (bf16[227,128]{1,0:T(8,128)(2,1)S(1)}, bf16[227,128]{1,0:T(8,128)(2,1)S(1)}, u32[]{:S(2)}, u32[]{:S(2)}) collective-permute-start(bf16[227,128]{1,0:T(8,128)(2,1)S(1)} %copy-done.6), channel_id=1, source_target_pairs={{1,0},{2,1},{3,2},{4,3},{5,4},{6,5},{7,6},{8,7},{9,8},{10,9},{11,1... | collective-permute-start | bytes 174344 | tf_op jit(solution)/shard_map/ppermute | solution.py:426
  175.2 2.2 %copy-start.12 = (bf16[227,128]{1,0:T(8,128)(2,1)}, bf16[227,128]{1,0:T(8,128)(2,1)S(1)}, u32[]{:S(2)}) copy-start(bf16[227,128]{1,0:T(8,128)(2,1)S(1)} %collective-permute-done.12.in0) | copy-start | bytes 174340
  175.2 2.2 %copy-start.13 = (bf16[227,128]{1,0:T(8,128)(2,1)}, bf16[227,128]{1,0:T(8,128)(2,1)S(1)}, u32[]{:S(2)}) copy-start(bf16[227,128]{1,0:T(8,128)(2,1)S(1)} %collective-permute-done.13.in1) | copy-start | bytes 174340
  177.4 0.6 copy-start.14
  177.4 0.6 copy-start.15
  183.2 1.1 copy-start.3
